TPU v7x, 32 devices: a whole 2x2x4 slice. The times are simulated.
32 devices in a mesh: groups: 2 (over x), seq: 8 (over z, y), wide: 2 (over core).
Axes of the slice: x: 2, y: 2, z: 4, core: 2. Of those that a mesh axis runs over, the one named last changes fastest.
Arguments:
- fine_input: bfloat16 [2, 1536, 768], P('groups', 'seq', 'wide'), parts along dimension 0, may hold values from -6 to 6
- conv_weight: bfloat16 [5, 768, 1536], P(None, 'wide'), may hold values from -0.09375 to 0.09375
- conv_bias: float32 [1536], replicated, may hold values from -3 to 3
- norm_gain: float32 [1536], replicated, may hold values from 0.25 to 1.75
- query_weight: bfloat16 [1536, 768], P(None, 'wide'), may hold values from -0.15625 to 0.15625
- key_weight: bfloat16 [1536, 768], P(None, 'wide'), may hold values from -0.15625 to 0.15625
- value_weight: bfloat16 [1536, 768], P(None, 'wide'), may hold values from -0.15625 to 0.15625
- out_weight: bfloat16 [768, 1536], P('wide'), may hold values from -0.21875 to 0.21875
- cotangent: bfloat16 [2, 768, 1536], P('groups', 'seq'), parts along dimension 0, may hold values from -6 to 6
Outputs:
- section_out: bfloat16 [2, 768, 1536], P('groups', 'seq'), parts along dimension 0
- input_grad: bfloat16 [2, 1536, 768], P('groups', 'seq', 'wide'), parts along dimension 0
- value_grad: float32 [1536, 1536], P(('groups', 'wide'), 'seq'), parts along dimension 0
There are 2 independent parts, one for each index of `groups`. A program takes and returns all parts, laid end to end along the dimension named above; an argument that names none is the same for every part. Nothing has to cross between parts.
All inputs are finite; a program needn't handle non-finite values.
Results may differ from a plain program's by a relative error of at most 0.02.
Values may be sent and summed in bfloat16 or wider, within the bound.
No kernel may reach another device: no remote copies, remote signals or barrier semaphores. Data moves between devices by JAX's collectives and lax.ppermute only.
A program may use at most 128 MiB of HBM per device.

v0:
```python
import math

import jax
import jax.numpy as jnp
from jax import lax
from jax.sharding import PartitionSpec as P

DH = 192


EPSILON = 1e-06
SCORE_GAIN = 3.0
GELU_ROOT = 0.7978845608028654
GELU_CUBIC = 0.044715


def extended(value, sides, width):
    for axis, dim in sides:
        devices, length = (lax.axis_size(axis), value.shape[dim])
        up = [(i, (i + 1) % devices) for i in range(devices - 1)]
        down = [(j, i) for i, j in up]
        last = lax.slice_in_dim(value, length - width, length, axis=dim)
        leading = lax.slice_in_dim(value, 0, width, axis=dim)
        before = lax.ppermute(last, axis, up)
        after = lax.ppermute(leading, axis, down)
        value = jnp.concatenate([before, value, after], axis=dim)
    return value


def gelu_parts(preact):
    tangent = jnp.tanh(GELU_ROOT * (preact + GELU_CUBIC * preact * preact * preact))
    gelu_value = 0.5 * preact * (1.0 + tangent)
    gelu_slope = 0.5 * (1.0 + tangent) + 0.5 * preact * (1.0 - tangent * tangent) * GELU_ROOT * (
        1.0 + 3.0 * GELU_CUBIC * preact * preact
    )
    return (gelu_value, gelu_slope)


def matmul(left_op, right_op):
    return lax.dot_general(
        left_op,
        right_op,
        (((left_op.ndim - 1,), (0,)), ((), ())),
        preferred_element_type=jnp.float32,
    )


def matmul_t(left_op, right_op):
    return lax.dot_general(
        left_op,
        right_op,
        (((left_op.ndim - 1,), (1,)), ((), ())),
        preferred_element_type=jnp.float32,
    )


def outer_sum(left_op, right_op):
    return lax.dot_general(
        left_op, right_op, (((0, 1), (0, 1)), ((), ())), preferred_element_type=jnp.float32
    )


def head_norm(projected):
    head_split = projected.reshape(projected.shape[:-1] + (projected.shape[-1] // DH, DH))
    inverse = lax.rsqrt(jnp.mean(head_split * head_split, -1, keepdims=True) + EPSILON)
    return (head_split * inverse, inverse)


def head_norm_back(grad_hat, normal, inverse):
    upstream = grad_hat.astype(jnp.float32)
    result = inverse * (upstream - normal * jnp.mean(upstream * normal, -1, keepdims=True))
    return result.reshape(result.shape[:-2] + (-1,))


def seq_rim(rows_block):
    return extended(rows_block, (("seq", 1),), 1)


def wide_total(partial_value):
    return lax.psum(partial_value, "wide")


def on_device(
    fine_input,
    conv_weight,
    conv_bias,
    norm_gain,
    query_weight,
    key_weight,
    value_weight,
    out_weight,
    cotangent,
):
    samples, fine_rows, channels = fine_input.shape
    tok_rows = fine_rows // 2
    features = conv_weight.shape[2]
    heads_here = query_weight.shape[1] // DH
    score_scale = SCORE_GAIN / math.sqrt(DH)
    grad_scale = 1.0 / math.sqrt(samples * tok_rows * lax.axis_size("seq"))
    paired = fine_input.reshape(samples, tok_rows, 2 * channels)
    framed = seq_rim(paired)
    low_taps = conv_weight[0:2].reshape(2 * channels, features)
    mid_taps = conv_weight[2:4].reshape(2 * channels, features)
    top_taps = conv_weight[4]
    partial_value = (
        matmul(framed[:, :-2], low_taps)
        + matmul(framed[:, 1:-1], mid_taps)
        + matmul(framed[:, 2:, :channels], top_taps)
    )
    preact = wide_total(partial_value) + conv_bias
    active, gelu_slope = gelu_parts(preact)
    hidden = active.astype(jnp.bfloat16)
    hidden_f = hidden.astype(jnp.float32)
    row_inv = lax.rsqrt(jnp.mean(hidden_f * hidden_f, -1, keepdims=True) + EPSILON)
    normed = (hidden_f * row_inv * norm_gain).astype(jnp.bfloat16)
    query_n, query_inv = head_norm(matmul(normed, query_weight))
    key_n, key_inv = head_norm(matmul(normed, key_weight))
    values = matmul(normed, value_weight).astype(jnp.bfloat16)
    query_hat = query_n.astype(jnp.bfloat16)
    key_hat = key_n.astype(jnp.bfloat16).reshape(samples, tok_rows, -1)
    all_keys, all_values = (
        lax.all_gather(key_hat, "seq", axis=1, tiled=True),
        lax.all_gather(values, "seq", axis=1, tiled=True),
    )
    key_heads = all_keys.reshape(samples, -1, heads_here, DH)
    value_heads = all_values.reshape(samples, -1, heads_here, DH)
    scores = (
        jnp.einsum("bqhd,bkhd->bhqk", query_hat, key_heads, preferred_element_type=jnp.float32)
        * score_scale
    )
    exp_scores = jnp.exp(scores)
    totals = jnp.sum(exp_scores, -1)
    numerator = jnp.einsum(
        "bhqk,bkhd->bqhd",
        exp_scores.astype(jnp.bfloat16),
        value_heads,
        preferred_element_type=jnp.float32,
    )
    attended = (numerator / totals.transpose(0, 2, 1)[..., None]).astype(jnp.bfloat16)
    att_flat = attended.reshape(samples, tok_rows, -1)
    section_out = (hidden_f + wide_total(matmul(att_flat, out_weight))).astype(jnp.bfloat16)
    att_grad = matmul_t(cotangent, out_weight).astype(jnp.bfloat16)
    grad_heads = att_grad.reshape(samples, tok_rows, heads_here, DH)
    delta_rows = jnp.sum(grad_heads.astype(jnp.float32) * attended.astype(jnp.float32), -1)
    prob_rows = exp_scores / totals[..., None]
    prob_grad = jnp.einsum(
        "bqhd,bkhd->bhqk", grad_heads, value_heads, preferred_element_type=jnp.float32
    )
    score_back = (
        prob_rows * (prob_grad - delta_rows.transpose(0, 2, 1)[..., None]) * score_scale
    ).astype(jnp.bfloat16)
    query_upstream = jnp.einsum(
        "bhqk,bkhd->bqhd", score_back, key_heads, preferred_element_type=jnp.float32
    ).astype(jnp.bfloat16)
    query_sums, query_deltas = (
        lax.all_gather(totals.transpose(0, 2, 1), "seq", axis=1, tiled=True),
        lax.all_gather(delta_rows, "seq", axis=1, tiled=True),
    )
    own_keys = key_hat.reshape(samples, tok_rows, heads_here, DH)
    own_values = values.reshape(samples, tok_rows, heads_here, DH)
    query_piece = lax.all_gather(
        query_hat.reshape(samples, tok_rows, -1), "seq", axis=1, tiled=True
    )
    grad_piece = lax.all_gather(att_grad, "seq", axis=1, tiled=True)
    row_count = query_piece.shape[1]
    query_four = query_piece.reshape(samples, row_count, heads_here, DH)
    grad_four = grad_piece.reshape(samples, row_count, heads_here, DH)
    total_piece = query_sums.transpose(0, 2, 1)
    delta_piece = query_deltas.transpose(0, 2, 1)
    score_piece = (
        jnp.einsum("bqhd,bkhd->bhqk", query_four, own_keys, preferred_element_type=jnp.float32)
        * score_scale
    )
    prob_piece = jnp.exp(score_piece) / total_piece[..., None]
    grad_prob = jnp.einsum(
        "bqhd,bkhd->bhqk", grad_four, own_values, preferred_element_type=jnp.float32
    )
    back_piece = (prob_piece * (grad_prob - delta_piece[..., None]) * score_scale).astype(
        jnp.bfloat16
    )
    key_acc = jnp.einsum(
        "bhqk,bqhd->bkhd", back_piece, query_four, preferred_element_type=jnp.float32
    )
    value_acc = jnp.einsum(
        "bhqk,bqhd->bkhd",
        prob_piece.astype(jnp.bfloat16),
        grad_four,
        preferred_element_type=jnp.float32,
    )
    key_acc, value_acc = (key_acc, value_acc)
    key_upstream = key_acc.astype(jnp.bfloat16)
    value_back = value_acc.astype(jnp.bfloat16)
    query_back = head_norm_back(query_upstream, query_n, query_inv).astype(jnp.bfloat16)
    key_back = head_norm_back(key_upstream, key_n, key_inv).astype(jnp.bfloat16)
    value_flat = value_back.reshape(samples, tok_rows, -1)
    value_grad = (
        lax.psum_scatter(outer_sum(value_flat, normed), "seq", scatter_dimension=1, tiled=True)
        * grad_scale
    )
    head_terms = (
        matmul_t(query_back, query_weight)
        + matmul_t(key_back, key_weight)
        + matmul_t(value_flat, value_weight)
    )
    norm_back = wide_total(head_terms)
    gain_back = norm_back * norm_gain
    hidden_back = cotangent.astype(jnp.float32) + row_inv * (
        gain_back - hidden_f * row_inv * row_inv * jnp.mean(gain_back * hidden_f, -1, keepdims=True)
    )
    pre_back = (hidden_back * gelu_slope).astype(jnp.bfloat16)
    back_framed = seq_rim(pre_back)
    pair_grad = matmul_t(back_framed[:, 2:], low_taps) + matmul_t(back_framed[:, 1:-1], mid_taps)
    top_grad = matmul_t(back_framed[:, :-2], top_taps)
    pair_grad = pair_grad + jnp.concatenate([top_grad, jnp.zeros_like(top_grad)], -1)
    input_grad = pair_grad.astype(jnp.bfloat16).reshape(samples, fine_rows, channels)
    return (section_out, input_grad, value_grad)


def solution(mesh):
    in_specs = (
        P("groups", "seq", "wide"),
        P(None, "wide", None),
        P(),
        P(),
        P(None, "wide"),
        P(None, "wide"),
        P(None, "wide"),
        P("wide", None),
        P("groups", "seq", None),
    )
    out_specs = (P("groups", "seq", None), P("groups", "seq", "wide"), P(("groups", "wide"), "seq"))
    return jax.shard_map(
        on_device, mesh=mesh, in_specs=in_specs, out_specs=out_specs, check_vma=False
    )
```

profile of v0, /device:TPU:4, one launch (start us, length us, event | category | flops | bytes accessed | tf_op | source)
XLA Modules:
  0.0 390.9 jit_solution(13803582261640900830)
XLA Ops:
  8.3 1.9 collective-permute-start.1
  10.2 4.8 %collective-permute-start = (bf16[1,1,768]{2,1,0:T(2,128)(2,1)S(1)}, bf16[1,1,768]{2,1,0:T(2,128)(2,1)S(1)}, u32[]{:S(2)}, u32[]{:S(2)}) collective-permute-start(bf16[1,1,768]{2,1,0:T(2,128)(2,1)S(1)} %get-tuple-element.13), channel_id=1, source_target_pairs={{0,2},{2,4},{4,6},{6,8},{8,10},{10,12},{12,14},{1,3},{3,5},{5,7},{... | collective-permute-start | bytes 4616 | tf_op jit(solution)/shard_map/ppermute | solution.py:24
  15.1 1.6 reshape.380
  16.7 2.8 fusion.100
  21.0 1.6 fusion.14
  22.6 1.3 fusion.1
  24.0 2.1 convolution_convert_fusion.1
  26.2 1.7 copy.88
  27.8 1.6 reshape.391
  29.5 31.7 %all-gather.3 = bf16[768,384]{1,0:T(8,128)(2,1)} all-gather(bf16[96,384]{1,0:T(8,128)(2,1)} %convolution_convert_fusion.1), channel_id=5, replica_groups=mesh['groups'=2,'seq'=8,'wide'=2] {'seq'}, dimensions={0}, use_global_device_ids=true | all-gather | bytes 663552 | tf_op jit(solution)/shard_map/all_gather | solution.py:164
  61.1 2.1 copy.95
  63.3 1.4 fusion.50
  65.4 2.3 fusion.97
  67.8 1.8 reshape.385
  69.6 1.8 reshape.386
  71.3 1.7 multiply_reduce_fusion.4
  73.1 1.7 copy.89
  74.8 2.4 fusion.95
  77.2 1.8 reshape.387
  79.0 1.7 multiply_reduce_fusion.3
  80.7 1.7 copy.98
  82.5 1.8 reshape.393
  84.2 1.8 convolution_convert_fusion.2
  86.6 33.5 %all-gather = bf16[768,384]{1,0:T(8,128)(2,1)} all-gather(bf16[96,384]{1,0:T(8,128)(2,1)S(1)} %convolution_convert_fusion.2), channel_id=2, replica_groups=mesh['groups'=2,'seq'=8,'wide'=2] {'seq'}, dimensions={0}, use_global_device_ids=true | all-gather | bytes 663552 | tf_op jit(solution)/shard_map/all_gather | solution.py:123
  120.1 1.6 reshape.395
  121.7 1.5 copy.84
  123.2 1.3 add_rsqrt_fusion
  124.4 1.4 copy.99
  125.8 1.7 mul.286.clone
  127.5 1.8 mul.287
  130.3 33.5 %all-gather.1 = bf16[768,384]{1,0:T(8,128)(2,1)} all-gather(bf16[96,384]{1,0:T(8,128)(2,1)S(1)} %multiply_convert_fusion.4), channel_id=3, replica_groups=mesh['groups'=2,'seq'=8,'wide'=2] {'seq'}, dimensions={0}, use_global_device_ids=true | all-gather | bytes 663552 | tf_op jit(solution)/shard_map/all_gather | solution.py:122
  163.8 2.1 copy.86
  165.9 1.4 copy.82
  167.3 1.3 add_rsqrt_fusion.1
  168.6 2.1 copy.81
  170.7 1.4 copy.100
  172.1 1.6 fusion.103
  174.6 1.2 convolution_bitcast_fusion
  175.9 3.2 multiply_reduce_fusion.1
  180.8 2.6 fusion.109
  184.2 1.8 mul.300
  187.0 33.4 %all-gather.2 = bf16[768,384]{1,0:T(8,128)(2,1)} all-gather(bf16[96,384]{1,0:T(8,128)(2,1)S(1)} %multiply_convert_fusion.3), channel_id=4, replica_groups=mesh['groups'=2,'seq'=8,'wide'=2] {'seq'}, dimensions={0}, use_global_device_ids=true | all-gather | bytes 663552 | tf_op jit(solution)/shard_map/all_gather | solution.py:161
  220.4 2.1 copy.91
  222.5 1.4 copy.93
  223.9 33.2 %all_gather.21 = f32[1,768,2]{2,0,1:T(1,128)} all-gather(f32[1,96,2]{2,0,1:T(1,128)} %copy.93), channel_id=1, replica_groups=mesh['groups'=2,'seq'=8,'wide'=2] {'seq'}, dimensions={1}, use_global_device_ids=true | all-gather | bytes 6912 | tf_op jit(solution)/shard_map/all_gather | solution.py:156
  257.1 1.7 copy.94
  258.8 18.6 %all-gather.5 = f32[8,96,2]{1,2,0:T(2,128)S(1)} all-gather(f32[1,96,2]{1,2,0:T(2,128)} %bitcast.153), channel_id=6, replica_groups=mesh['groups'=2,'seq'=8,'wide'=2] {'seq'}, dimensions={0}, use_global_device_ids=true | all-gather | bytes 6912 | tf_op jit(solution)/shard_map/all_gather | solution.py:157
  278.0 1.4 reshape.408
  279.4 1.5 fusion.6
  281.9 3.3 multiply_reduce_fusion
  286.9 2.0 convolution_add_fusion.1
  289.0 1.3 fusion.2
  290.4 3.0 fusion.93
  293.4 16.5 %all-reduce.7.cloned.1.call-done = (f32[1,96,1536]{2,1,0:T(8,128)}, f32[1,96,1536]{2,1,0:T(8,128)}) async-done(((f32[1,96,1536]{2,1,0:T(8,128)}, f32[1,96,1536]{2,1,0:T(8,128)}), (f32[1,96,1536]{2,1,0:T(8,128)}, f32[1,96,1536]{2,1,0:T(8,128)})) %all-reduce.7.cloned.1.call-update) | async-done | bytes 1179664 | tf_op jit(solution)/shard_map/psum | solution.py:80
  309.8 1.4 fusion.52
  311.3 2.9 fusion.44
  314.2 3.4 collective-permute-start.3
  318.4 2.5 collective-permute-start.2
  320.9 1.9 fusion.23
  322.8 2.7 collective-permute-done.2
  325.5 1.5 fusion.20
  327.1 1.6 reshape.400
  328.7 53.9 %reduce-scatter.2.cloned.1.call-done = f32[384,192]{0,1:T(8,128)} async-done(((f32[384,1536]{0,1:T(8,128)}), f32[384,192]{0,1:T(8,128)}) %reduce-scatter.2.cloned.1.call-update) | async-done | bytes 294928 | tf_op jit(solution)/shard_map/reduce_scatter | solution.py:197
  382.6 1.7 broadcast_multiply_fusion
  (69 shorter events, 13.6 us)
Async XLA Ops:
  7.2 16.9 %copy-start = (bf16[384,1536]{1,0:T(8,128)(2,1)S(1)}, bf16[384,1536]{1,0:T(8,128)(2,1)}, u32[]{:S(2)}) copy-start(bf16[384,1536]{1,0:T(8,128)(2,1)} %param.16) | copy-start | bytes 3538948
  7.2 56.1 %all-reduce.5.cloned.1.call-start = ((), (), s32[]{:S(2)}) async-start(), calls=%async_computation.1 | async-start | bytes 1179648 | tf_op jit(solution)/shard_map/psum | solution.py:80
  8.3 6.8 %copy-start.8 = (bf16[1,96,768]{2,1,0:T(8,128)(2,1)}, bf16[1,96,768]{2,1,0:T(8,128)(2,1)S(1)}, u32[]{:S(2)}) copy-start(bf16[1,96,768]{2,1,0:T(8,128)(2,1)S(1)} %reshape.377) | copy-start | bytes 442372
  8.3 12.7 %collective-permute-start.1 = (bf16[1,1,768]{2,1,0:T(2,128)(2,1)S(1)}, bf16[1,1,768]{2,1,0:T(2,128)(2,1)S(1)}, u32[]{:S(2)}, u32[]{:S(2)}) collective-permute-start(bf16[1,1,768]{2,1,0:T(2,128)(2,1)S(1)} %get-tuple-element.14), channel_id=1, source_target_pairs={{2,0},{4,2},{6,4},{8,6},{10,8},{12,10},{14,12},{3,1},{5,3},{7,5},{... | collective-permute-start | bytes 4616 | tf_op jit(solution)/shard_map/ppermute | solution.py:25
  10.2 12.4 %collective-permute-start = (bf16[1,1,768]{2,1,0:T(2,128)(2,1)S(1)}, bf16[1,1,768]{2,1,0:T(2,128)(2,1)S(1)}, u32[]{:S(2)}, u32[]{:S(2)}) collective-permute-start(bf16[1,1,768]{2,1,0:T(2,128)(2,1)S(1)} %get-tuple-element.13), channel_id=1, source_target_pairs={{0,2},{2,4},{4,6},{6,8},{8,10},{10,12},{12,14},{1,3},{3,5},{5,7},{... | collective-permute-start | bytes 4616 | tf_op jit(solution)/shard_map/ppermute | solution.py:24
  16.7 2.9 copy-start.12
  19.6 1.4 copy-start.1
  19.6 1.4 copy-start.9
  24.0 285.9 %all-reduce.7.cloned.1.call-start = ((), (), s32[]{:S(2)}) async-start(), calls=%async_computation.3 | async-start | bytes 2359296 | tf_op jit(solution)/shard_map/psum | solution.py:80
  26.1 37.2 %copy-start.18 = (f32[1536]{0:T(1024)S(1)}, f32[1536]{0:T(1024)}, u32[]{:S(2)}) copy-start(f32[1536]{0:T(1024)} %param.11) | copy-start | bytes 18436
  61.1 4.3 %copy-start.15 = (f32[1536]{0:T(1024)S(1)}, f32[1536]{0:T(1024)}, u32[]{:S(2)}) copy-start(f32[1536]{0:T(1024)} %param.12) | copy-start | bytes 18436
  64.7 0.7 copy-start.3
  64.7 0.7 copy-start.19
  86.0 0.6 copy-start.11
  172.1 1.6 copy-start.13
  172.1 1.6 copy-start.16
  173.7 2.2 copy-start.14
  173.7 2.2 copy-start.20
  179.7 3.7 copy-start.17
  279.4 1.5 copy-start.4
  280.9 1.0 copy-start.6
  286.9 2.0 copy-start.5
  286.9 2.0 copy-start.10
  290.3 92.3 %reduce-scatter.2.cloned.1.call-start = ((), (), s32[]{:S(2)}) async-start(), calls=%async_computation.2 | async-start | bytes 2654208 | tf_op jit(solution)/shard_map/reduce_scatter | solution.py:197
  309.8 1.4 copy-start.7
  311.2 6.3 %copy-start.2 = (bf16[2,384,1536]{2,1,0:T(8,128)(2,1)S(1)}, bf16[2,384,1536]{2,1,0:T(8,128)(2,1)}, u32[]{:S(2)}) copy-start(bf16[2,384,1536]{2,1,0:T(8,128)(2,1)} %copy-done.1) | copy-start | bytes 7077892
  314.2 6.7 %collective-permute-start.3 = (bf16[1,1,1536]{2,1,0:T(2,128)(2,1)S(1)}, bf16[1,1,1536]{2,1,0:T(2,128)(2,1)S(1)}, u32[]{:S(2)}, u32[]{:S(2)}) collective-permute-start(bf16[1,1,1536]{2,1,0:T(2,128)(2,1)S(1)} %get-tuple-element.9), channel_id=1, source_target_pairs={{0,2},{2,4},{4,6},{6,8},{8,10},{10,12},{12,14},{1,3},{3,5},{5,7},{... | collective-permute-start | bytes 9224 | tf_op jit(solution)/shard_map/ppermute | solution.py:24
  318.4 7.1 %collective-permute-start.2 = (bf16[1,1,1536]{2,1,0:T(2,128)(2,1)S(1)}, bf16[1,1,1536]{2,1,0:T(2,128)(2,1)S(1)}, u32[]{:S(2)}, u32[]{:S(2)}) collective-permute-start(bf16[1,1,1536]{2,1,0:T(2,128)(2,1)S(1)} %get-tuple-element.10), channel_id=1, source_target_pairs={{2,0},{4,2},{6,4},{8,6},{10,8},{12,10},{14,12},{3,1},{5,3},{7,5},{... | collective-permute-start | bytes 9224 | tf_op jit(solution)/shard_map/ppermute | solution.py:25
Sparse Core Ops, SparseCore 0:
  24.1 19.2 all-reduce.4
  290.4 19.3 all-reduce.6
  313.3 69.2 reduce-scatter.1
where the time goes:
time: 395 us; the launch traced here: 391 us
  blocking collectives  184 us (47%)
  waiting for transfers between devices  73.2 us (19%)
  local copies, waits for them, and re-layouts  50.2 us (13%)
  matrix products  38 us (10%)
  other arithmetic  18.8 us (5%)
  between operations  14.1 us (4%)
  starting transfers between devices  12.7 us (3%)
    reduce_scatter x1, waiting for transfers between devices, on_device(): lax.psum_scatter(outer_sum(value_flat, normed), 'seq', scatter_dimension=...  53.9 us
    all_gather x1, blocking collectives, on_device(): lax.all_gather(key_hat, 'seq', axis=1, tiled=True)  33.5 us
    all_gather x1, blocking collectives, on_device(): lax.all_gather(values, 'seq', axis=1, tiled=True)  33.5 us
    all_gather x1, blocking collectives, on_device(): lax.all_gather(query_hat.reshape(samples, tok_rows, -1), 'seq', axis=1, t...  33.4 us
    all_gather x1, blocking collectives, on_device(): lax.all_gather(totals.transpose(0, 2, 1), 'seq', axis=1, tiled=True)  33.2 us
    all_gather x1, blocking collectives, on_device(): grad_piece = lax.all_gather(att_grad, 'seq', axis=1, tiled=True)  31.7 us
    all_gather x1, blocking collectives, on_device(): lax.all_gather(delta_rows, 'seq', axis=1, tiled=True)  18.6 us
    psum x2, waiting for transfers between devices, wide_total(): return lax.psum(partial_value, 'wide')  16.5 us
  transfers between devices with their start and end apart: 7, of which 3 were waited for; matrix products, arithmetic and copies ran while one was open for 7% of the time, Pallas kernels for 0%

commit v1 on v0

v1 whole, which is shorter than its diff:
```python
import functools
import math

import jax
import jax.numpy as jnp
from jax import lax
from jax.experimental import pallas as pl
from jax.experimental.pallas import tpu as pltpu
from jax.sharding import PartitionSpec as P

DH = 192
EPSILON = 1e-06
SCORE_GAIN = 3.0
GELU_ROOT = 0.7978845608028654
GELU_CUBIC = 0.044715
F32 = jnp.float32
BF16 = jnp.bfloat16
HALO_ROWS = 16
CHUNK = 16
VMEM_BYTES = 50 * 1024 * 1024


def spec(*_):
    return pl.BlockSpec(memory_space=pltpu.VMEM)


def anywhere():
    return pl.BlockSpec(memory_space=pl.ANY)


def params(limit=VMEM_BYTES):
    return pltpu.CompilerParams(vmem_limit_bytes=limit)


def cost(flops, nbytes):
    return pl.CostEstimate(flops=int(flops), bytes_accessed=int(nbytes), transcendentals=0)


def dot(left, right):
    return jnp.dot(left, right, preferred_element_type=F32)


def dot_rt(left, right):
    return lax.dot_general(left, right, (((1,), (1,)), ((), ())), preferred_element_type=F32)


def dot_lt(left, right):
    return lax.dot_general(left, right, (((0,), (0,)), ((), ())), preferred_element_type=F32)


def pick(shape, test):
    row = lax.broadcasted_iota(jnp.int32, shape, 0)
    col = lax.broadcasted_iota(jnp.int32, shape, 1)
    return jnp.where(test(row, col), 1.0, 0.0).astype(BF16)


def conv_kernel(pieces, tok, taps, *refs):
    fine_refs, side_refs = refs[:pieces], refs[pieces : 2 * pieces]
    weight_ref, out_ref, lhs = refs[2 * pieces :]
    channels = fine_refs[0].shape[1]
    fine_rows = 2 * tok

    @pl.when(pl.program_id(0) == 0)
    def _():
        for i in range(pieces):
            block = jnp.concatenate([fine_refs[i][...], side_refs[i][tok : tok + HALO_ROWS, :]], 0)
            for k in range(taps):

                def test(row, col, k=k):
                    want = 2 * row + k - 2
                    inside = (want >= 0) & (want < fine_rows)
                    spare = jnp.where(want < 0, fine_rows + 2 + want, want + 2)
                    return col == jnp.where(inside, want, spare)

                rows = dot(pick((tok, fine_rows + HALO_ROWS), test), block)
                lhs[i * tok : (i + 1) * tok, k * channels : (k + 1) * channels] = rows.astype(BF16)

    out_ref[...] = dot(lhs[...], weight_ref[...]).astype(BF16)


def conv_partial(fines, sides, weight, tok, taps):
    pieces = len(fines)
    depth, features = weight.shape
    tile = features // 3
    rows = pieces * tok
    whole = lambda a: pl.BlockSpec(a.shape, lambda i: (0, 0))
    return pl.pallas_call(
        functools.partial(conv_kernel, pieces, tok, taps),
        grid=(3,),
        out_shape=jax.ShapeDtypeStruct((rows, features), BF16),
        in_specs=[whole(a) for a in fines]
        + [whole(a) for a in sides]
        + [pl.BlockSpec((depth, tile), lambda i: (0, i))],
        out_specs=pl.BlockSpec((rows, tile), lambda i: (0, i)),
        scratch_shapes=[pltpu.VMEM((rows, depth), BF16)],
        compiler_params=params(),
        cost_estimate=cost(2 * rows * depth * features, 2 * depth * features),
        name="conv_partial",
    )(*fines, *sides, weight)


def gelu_value(preact):
    tangent = jnp.tanh(GELU_ROOT * (preact + GELU_CUBIC * preact * preact * preact))
    return 0.5 * preact * (1.0 + tangent), tangent


def head_scale(value):
    lane = lax.broadcasted_iota(jnp.int32, value.shape, 1)
    square = value * value
    parts = value.shape[1] // DH
    scale = jnp.zeros_like(value)
    for h in range(parts):
        here = (lane >= h * DH) & (lane < (h + 1) * DH)
        mean = jnp.sum(jnp.where(here, square, 0.0), -1, keepdims=True) * (1.0 / DH)
        scale = jnp.where(here, lax.rsqrt(mean + EPSILON), scale)
    return scale


def head_mean(value):
    lane = lax.broadcasted_iota(jnp.int32, value.shape, 1)
    parts = value.shape[1] // DH
    out = jnp.zeros_like(value)
    for h in range(parts):
        here = (lane >= h * DH) & (lane < (h + 1) * DH)
        mean = jnp.sum(jnp.where(here, value, 0.0), -1, keepdims=True) * (1.0 / DH)
        out = jnp.where(here, mean, out)
    return out


def post_kernel(own, place_ref, mine_ref, theirs_ref, bias_ref, gain_ref, wq_any, wk_any, wv_any, *refs):
    if own:
        qkv_ref, slice_ref, proj_ref, normed, wq, wk, wv, sems = refs
    else:
        qkv_ref, slice_ref, normed, wq, wk, wv, sems = refs
    copies = [
        pltpu.make_async_copy(a, b, sems.at[i])
        for i, (a, b) in enumerate(((wq_any, wq), (wk_any, wk), (wv_any, wv)))
    ]
    for c in copies:
        c.start()
    rows = mine_ref.shape[0]

    @pl.loop(0, rows // CHUNK)
    def _(i):
        at = pl.ds(pl.multiple_of(i * CHUNK, CHUNK), CHUNK)
        preact = mine_ref[at, :].astype(F32) + theirs_ref[at, :].astype(F32) + bias_ref[...]
        hidden = gelu_value(preact)[0].astype(BF16).astype(F32)
        inv = lax.rsqrt(jnp.mean(hidden * hidden, -1, keepdims=True) + EPSILON)
        normed[at, :] = (hidden * inv * gain_ref[...]).astype(BF16)

    features, width = wq.shape
    count = slice_ref.shape[1]
    start = place_ref[0] * count
    value = normed[...]
    slice_ref[...] = dot(value, pick((features, count), lambda r, c: r == c + start)).astype(BF16)
    for i, w in enumerate((wq, wk, wv)):
        copies[i].wait()
        proj = dot(value, w[...])
        if own and i < 2:
            proj_ref[:, i * width : (i + 1) * width] = proj
        if i < 2:
            proj = proj * head_scale(proj)
        qkv_ref[:, i * width : (i + 1) * width] = proj.astype(BF16)


def post(own, place, mine, theirs, bias, gain, wq, wk, wv, count):
    rows, features = mine.shape
    width = wq.shape[1]
    outs = [
        jax.ShapeDtypeStruct((rows, 3 * width), BF16),
        jax.ShapeDtypeStruct((rows, count), BF16),
    ]
    if own:
        outs.append(jax.ShapeDtypeStruct((rows, 2 * width), F32))
    return pl.pallas_call(
        functools.partial(post_kernel, own),
        out_shape=outs,
        in_specs=[pl.BlockSpec(memory_space=pltpu.SMEM)] + [spec()] * 4 + [anywhere()] * 3,
        out_specs=[spec()] * len(outs),
        scratch_shapes=[pltpu.VMEM((rows, features), BF16)]
        + [pltpu.VMEM((features, width), BF16)] * 3
        + [pltpu.SemaphoreType.DMA((3,))],
        compiler_params=params(),
        cost_estimate=cost(6 * rows * features * width, 6 * features * width),
        name="post",
    )(place, mine, theirs, bias, gain, wq, wk, wv)


def attention_kernel(tok, tile, heads, qkv_rows, grad_rows, *refs):
    groups, parts = len(qkv_rows), len(grad_rows)
    qkv_in, grad_in = refs[:groups], refs[groups : groups + parts]
    proj_ref, wq_any, wk_any, wv_any, wo_any, both_ref, dv_ref = refs[groups + parts : groups + parts + 7]
    qkv, grad, dv_acc, dk_acc, dq_acc, att, wq, wk, wv, wo, sems = refs[groups + parts + 7 :]
    width = heads * DH
    total = qkv.shape[0]
    step, steps = pl.program_id(0), pl.num_programs(0)
    loads, weights = [], []
    at = 0
    for i, rows in enumerate(qkv_rows):
        loads.append(pltpu.make_async_copy(qkv_in[i], qkv.at[pl.ds(at, rows)], sems.at[len(loads)]))
        at += rows
    at = 0
    for i, rows in enumerate(grad_rows):
        source = grad_in[i].at[pl.ds(0, rows)]
        loads.append(pltpu.make_async_copy(source, grad.at[pl.ds(at, rows)], sems.at[len(loads)]))
        at += rows
    for a, b in ((wo_any, wo), (wq_any, wq), (wk_any, wk), (wv_any, wv)):
        weights.append(pltpu.make_async_copy(a, b, sems.at[len(loads) + len(weights)]))

    @pl.when(step == 0)
    def _():
        for c in loads:
            c.start()
        for c in weights:
            c.start()
        for c in loads:
            c.wait()
        dv_acc[...] = jnp.zeros_like(dv_acc)
        dk_acc[...] = jnp.zeros_like(dk_acc)

    scale = SCORE_GAIN / math.sqrt(DH)
    here = pl.ds(pl.multiple_of(step * tile, tile), tile)
    lanes = min(128, tile)
    for h in range(heads):
        cols = slice(h * DH, (h + 1) * DH)
        key = qkv[:, width + h * DH : width + (h + 1) * DH]
        val = qkv[:, 2 * width + h * DH : 2 * width + (h + 1) * DH]
        query = qkv[here, :][:, cols]
        up = grad[here, :][:, cols]
        expo = jnp.exp(dot_rt(key, query) * scale)
        back = dot_rt(val, up)
        inv = 1.0 / jnp.sum(expo, 0, keepdims=True)
        delta = jnp.sum(expo * back, 0, keepdims=True) * inv
        prob = expo * inv
        prob_b = prob.astype(BF16)
        dv_acc[:, cols] += dot(prob_b, up)
        score_own = (prob[:tok] * (back[:tok] - delta) * scale).astype(BF16)
        dk_acc[:, cols] += dot(score_own, query)

        @pl.when(step == 0)
        def _():
            att[:, cols] = dot_lt(prob_b[:, :lanes], val)[:tok].astype(BF16)
            score = (prob[:, :lanes] * (back[:, :lanes] - delta[:, :lanes]) * scale).astype(BF16)
            dq_acc[:, cols] = dot_lt(score, key)[:tok]

    @pl.when(step == steps - 1)
    def _():
        dv = dv_acc[...].astype(BF16)
        dv_ref[...] = dv
        for c in weights:
            c.wait()
        both_ref[:tok, :] = dot(att[...], wo[...]).astype(BF16)
        backs = []
        for acc, lo in ((dq_acc, 0), (dk_acc, width)):
            proj = proj_ref[:, lo : lo + width]
            inv = head_scale(proj)
            normal = proj * inv
            up = acc[...].astype(BF16).astype(F32)
            backs.append((inv * (up - normal * head_mean(up * normal))).astype(BF16))
        norm_back = dot_rt(backs[0], wq[...]) + dot_rt(backs[1], wk[...]) + dot_rt(dv[:tok], wv[...])
        both_ref[tok:, :] = norm_back.astype(BF16)


def attention(qkvs, grads, grad_rows, proj, wq, wk, wv, wo, tok):
    qkv_rows = tuple(a.shape[0] for a in qkvs)
    total = sum(qkv_rows)
    features, width = wq.shape
    heads = width // DH
    tile = 256 if total <= 2048 else 128
    copies = len(qkvs) + len(grads) + 4
    return pl.pallas_call(
        functools.partial(attention_kernel, tok, tile, heads, qkv_rows, tuple(grad_rows)),
        grid=(total // tile,),
        out_shape=[
            jax.ShapeDtypeStruct((2 * tok, features), BF16),
            jax.ShapeDtypeStruct((total, width), BF16),
        ],
        in_specs=[anywhere()] * (len(qkvs) + len(grads))
        + [pl.BlockSpec(proj.shape, lambda i: (0, 0))]
        + [anywhere()] * 4,
        out_specs=[
            pl.BlockSpec((2 * tok, features), lambda i: (0, 0)),
            pl.BlockSpec((total, width), lambda i: (0, 0)),
        ],
        scratch_shapes=[
            pltpu.VMEM((total, 3 * width), BF16),
            pltpu.VMEM((total, width), BF16),
            pltpu.VMEM((total, width), F32),
            pltpu.VMEM((tok, width), F32),
            pltpu.VMEM((tok, width), F32),
            pltpu.VMEM((tok, width), BF16),
            pltpu.VMEM((features, width), BF16),
            pltpu.VMEM((features, width), BF16),
            pltpu.VMEM((features, width), BF16),
            pltpu.VMEM((width, features), BF16),
            pltpu.SemaphoreType.DMA((copies,)),
        ],
        compiler_params=params(VMEM_BYTES if total <= 2048 else VMEM_BYTES + VMEM_BYTES // 5),
        cost_estimate=cost(6 * total * total * width, 8 * total * width),
        name="attention",
    )(*qkvs, *grads, proj, wq, wk, wv, wo)


def finish_kernel(mine_ref, theirs_ref, bias_ref, gain_ref, cot_ref, here_ref, there_ref, out_ref, pre_ref, head_ref, tail_ref):
    tok = out_ref.shape[0]

    @pl.loop(0, tok // CHUNK)
    def _(i):
        at = pl.ds(pl.multiple_of(i * CHUNK, CHUNK), CHUNK)
        low = pl.ds(pl.multiple_of(tok + i * CHUNK, CHUNK), CHUNK)
        preact = mine_ref[at, :].astype(F32) + theirs_ref[at, :].astype(F32) + bias_ref[...]
        active, tangent = gelu_value(preact)
        slope = 0.5 * (1.0 + tangent) + 0.5 * preact * (1.0 - tangent * tangent) * GELU_ROOT * (
            1.0 + 3.0 * GELU_CUBIC * preact * preact
        )
        hidden = active.astype(BF16).astype(F32)
        inv = lax.rsqrt(jnp.mean(hidden * hidden, -1, keepdims=True) + EPSILON)
        attended = here_ref[at, :].astype(F32) + there_ref[at, :].astype(F32)
        out_ref[at, :] = (hidden + attended).astype(BF16)
        gain_back = (here_ref[low, :].astype(F32) + there_ref[low, :].astype(F32)) * gain_ref[...]
        mean = jnp.mean(gain_back * hidden, -1, keepdims=True)
        back = cot_ref[at, :].astype(F32) + inv * (gain_back - hidden * (inv * inv * mean))
        pre_ref[at, :] = (back * slope).astype(BF16)

    head_ref[...] = pre_ref[0:1, :]
    tail_ref[...] = pre_ref[tok - 1 : tok, :]


def finish(mine, theirs, bias, gain, cot, here, there):
    tok, features = cot.shape
    row = jax.ShapeDtypeStruct((1, features), BF16)
    full = jax.ShapeDtypeStruct((tok, features), BF16)
    return pl.pallas_call(
        finish_kernel,
        out_shape=[full, full, row, row],
        in_specs=[spec()] * 7,
        out_specs=[spec()] * 4,
        compiler_params=params(),
        cost_estimate=cost(40 * tok * features, 12 * tok * features),
        name="finish",
    )(mine, theirs, bias, gain, cot, here, there)


def conv_back_kernel(order, pre_ref, before_ref, after_ref, weight_ref, out_ref, acc):
    step = pl.program_id(0)
    tok = pre_ref.shape[0]
    channels = weight_ref.shape[1]
    pre = pre_ref[...]
    for i, k in enumerate(order):

        @pl.when(step == i)
        def _(k=k):
            if k < 2:
                left = jnp.concatenate([pre[1:], after_ref[...]], 0)
            elif k < 4:
                left = pre
            else:
                left = jnp.concatenate([before_ref[...], pre[:-1]], 0)
            value = dot_rt(left, weight_ref[0])
            cols = slice((k % 2) * channels, (k % 2 + 1) * channels)
            if k in (2, 3):
                acc[:, cols] = value
            else:
                acc[:, cols] += value

    @pl.when(step == len(order) - 1)
    def _():
        even = pick((2 * tok, tok), lambda r, c: r == 2 * c)
        odd = pick((2 * tok, tok), lambda r, c: r == 2 * c + 1)
        rows = dot(even, acc[:, :channels].astype(BF16)) + dot(odd, acc[:, channels:].astype(BF16))
        out_ref[...] = rows.astype(BF16)


def conv_back(pre, before, after, weight):
    tok, features = pre.shape
    taps, channels = weight.shape[:2]
    order = (2, 3, 0, 1, 4)
    whole = lambda a: pl.BlockSpec(a.shape, lambda i: (0, 0))
    return pl.pallas_call(
        functools.partial(conv_back_kernel, order),
        grid=(taps,),
        out_shape=jax.ShapeDtypeStruct((2 * tok, channels), BF16),
        in_specs=[whole(pre), whole(before), whole(after)]
        + [
            pl.BlockSpec(
                (1, channels, features),
                lambda i: (jnp.where(i < 2, i + 2, jnp.where(i < 4, i - 2, 4)), 0, 0),
            )
        ],
        out_specs=pl.BlockSpec((2 * tok, channels), lambda i: (0, 0)),
        scratch_shapes=[pltpu.VMEM((tok, 2 * channels), F32)],
        compiler_params=params(),
        cost_estimate=cost(2 * tok * taps * channels * features, 2 * taps * channels * features),
        name="conv_back",
    )(pre, before, after, weight)


def value_kernel(rows_of, scale, dv_ref, *refs):
    slices, out_ref = refs[:-1], refs[-1]
    total, at = None, 0
    for ref, rows in zip(slices, rows_of):
        term = dot_lt(dv_ref[at : at + rows, :], ref[...])
        total = term if total is None else total + term
        at += rows
    out_ref[...] = total * scale


def value_gradient(dv, slices, scale):
    rows_of = tuple(a.shape[0] for a in slices)
    return pl.pallas_call(
        functools.partial(value_kernel, rows_of, scale),
        out_shape=jax.ShapeDtypeStruct((dv.shape[1], slices[0].shape[1]), F32),
        in_specs=[spec()] * (1 + len(slices)),
        out_specs=spec(),
        compiler_params=params(),
        cost_estimate=cost(2 * dv.shape[0] * dv.shape[1] * 192, 2 * dv.size),
        name="value_gradient",
    )(dv, *slices)


def on_device(
    fine_input,
    conv_weight,
    conv_bias,
    norm_gain,
    query_weight,
    key_weight,
    value_weight,
    out_weight,
    cotangent,
):
    samples, fine_rows, channels = fine_input.shape
    tok = fine_rows // 2
    taps, _, features = conv_weight.shape
    n = lax.axis_size("seq")
    grad_scale = 1.0 / math.sqrt(samples * tok * n)
    up = [(i, i + 1) for i in range(n - 1)]
    down = [(j, i) for i, j in up]
    cycle = list(range(0, n, 2)) + list(range(n - 1, 0, -2))
    ahead = [(cycle[i], cycle[(i + 1) % n]) for i in range(n)]
    behind = [(j, i) for i, j in ahead]
    swap = [(0, 1), (1, 0)]
    place = lax.axis_index("seq").astype(jnp.int32).reshape(1)
    bias, gain = conv_bias.reshape(1, features), norm_gain.reshape(1, features)
    flat_weight = conv_weight.reshape(taps * channels, features)
    fine, cot = fine_input[0], cotangent[0]

    before = lax.ppermute(fine[-2:], "seq", up)
    after = lax.ppermute(fine[:1], "seq", down)
    att_grad = dot_rt(cot, out_weight).astype(BF16)
    pad = jnp.zeros((HALO_ROWS - 3, channels), BF16)
    side = jnp.concatenate([att_grad, before, after, pad], 0)

    fine_groups, side_groups = [[fine]], [[side]]
    f_cw = f_ccw = fine
    s_cw = s_ccw = side
    half = n // 2
    side_cut = (side.shape[0] // 2 + 15) // 16 * 16
    for k in range(1, half + 1):
        if k < half:
            f_cw, f_ccw = lax.ppermute(f_cw, "seq", ahead), lax.ppermute(f_ccw, "seq", behind)
            s_cw, s_ccw = lax.ppermute(s_cw, "seq", ahead), lax.ppermute(s_ccw, "seq", behind)
            fine_groups.append([f_cw, f_ccw])
            side_groups.append([s_cw, s_ccw])
        else:
            f_a, f_b = lax.ppermute(f_cw[:tok], "seq", ahead), lax.ppermute(f_ccw[tok:], "seq", behind)
            s_a = lax.ppermute(s_cw[:side_cut], "seq", ahead)
            s_b = lax.ppermute(s_ccw[side_cut:], "seq", behind)
            fine_groups.append([jnp.concatenate([f_a, f_b], 0)])
            side_groups.append([jnp.concatenate([s_a, s_b], 0)])

    qkvs, slices = [], []
    for g, (fines, sides) in enumerate(zip(fine_groups, side_groups)):
        mine = conv_partial(fines, sides, flat_weight, tok, taps)
        theirs = lax.ppermute(mine, "wide", swap)
        outs = post(g == 0, place, mine, theirs, bias, gain, query_weight, key_weight, value_weight, features // n)
        qkvs.append(outs[0])
        slices.append(outs[1])
        if g == 0:
            proj, own_mine, own_theirs = outs[2], mine, theirs

    grads = [a for sides in side_groups for a in sides]
    both, dv = attention(
        qkvs, grads, [tok] * len(grads), proj, query_weight, key_weight, value_weight, out_weight, tok
    )
    there = lax.ppermute(both, "wide", swap)
    value_grad = value_gradient(dv, slices, grad_scale)
    section_out, pre_back, head, tail = finish(own_mine, own_theirs, bias, gain, cot, both, there)
    pre_before = lax.ppermute(tail, "seq", up)
    pre_after = lax.ppermute(head, "seq", down)
    input_grad = conv_back(pre_back, pre_before, pre_after, conv_weight)
    return (section_out[None], input_grad[None], value_grad)


def solution(mesh):
    in_specs = (
        P("groups", "seq", "wide"),
        P(None, "wide", None),
        P(),
        P(),
        P(None, "wide"),
        P(None, "wide"),
        P(None, "wide"),
        P("wide", None),
        P("groups", "seq", None),
    )
    out_specs = (P("groups", "seq", None), P("groups", "seq", "wide"), P(("groups", "wide"), "seq"))
    return jax.shard_map(
        on_device, mesh=mesh, in_specs=in_specs, out_specs=out_specs, check_vma=False
    )
```

time: 395 us -> 116 us (0.29)
  the two profiles are of different devices: /device:TPU:4 before, /device:TPU:0 now
where the time goes in v1:
time: 116 us; the launch traced here: 115 us
  Pallas kernels  69.9 us (60%)
  starting transfers between devices  29.9 us (26%)
  waiting for transfers between devices  10 us (9%)
  local copies, waits for them, and re-layouts  2.57 us (2%)
  matrix products  1.88 us (2%)
  between operations  1.16 us (1%)
    pallas_call x5, Pallas kernels, post(): pl.pallas_call(functools.partial(post_kernel, own), out_shape=outs, in_sp...  25.4 us
    pallas_call x5, Pallas kernels, conv_partial(): pl.pallas_call(functools.partial(conv_kernel, pieces, tok, taps), grid=(3...  24.9 us
    pallas_call x1, Pallas kernels, attention(): pl.pallas_call(functools.partial(attention_kernel, tok, tile, heads, qkv_...  9.8 us
    pallas_call x1, Pallas kernels, conv_back(): pl.pallas_call(functools.partial(conv_back_kernel, order), grid=(taps,),...  6.4 us
    ppermute x3, starting transfers between devices, on_device(): lax.ppermute(f_cw, 'seq', ahead)  4.33 us
    ppermute x1, starting transfers between devices, on_device(): before = lax.ppermute(fine[-2:], 'seq', up)  3.83 us
    ppermute x1, starting transfers between devices, on_device(): pre_before = lax.ppermute(tail, 'seq', up)  3.8 us
    ppermute x3, starting transfers between devices, on_device(): lax.ppermute(s_ccw, 'seq', behind)  3.69 us
  transfers between devices with their start and end apart: 26, of which 5 were waited for; matrix products, arithmetic and copies ran while one was open for 4% of the time, Pallas kernels for 39%

profile of v1, /device:TPU:0, one launch (start us, length us, event | category | flops | bytes accessed | tf_op | source)
XLA Modules:
  0.0 115.5 jit_solution(8897961629513205435)
XLA Ops:
  0.6 0.0 copy-start.19
  0.6 3.1 %collective-permute-start.3 = (bf16[192,384]{1,0:T(8,128)(2,1)}, bf16[192,384]{1,0:T(8,128)(2,1)S(1)}, u32[]{:S(2)}, u32[]{:S(2)}) collective-permute-start(bf16[192,384]{1,0:T(8,128)(2,1)} %bitcast.14), channel_id=1, source_target_pairs={{0,4},{4,8},{8,12},{12,14},{14,10},{10,6},{6,2},{2,0},{1,5},{5,9},... | collective-permute-start | bytes 442376 | tf_op jit(solution)/shard_map/ppermute | solution.py:461
  3.7 0.0 collective-permute-start.4
  3.7 0.8 slice_bitcast_fusion.1
  4.5 3.8 %collective-permute-start = (bf16[2,384]{1,0:T(2,128)(2,1)S(1)}, bf16[2,384]{1,0:T(2,128)(2,1)S(1)}, u32[]{:S(2)}, u32[]{:S(2)}) collective-permute-start(bf16[2,384]{1,0:T(2,128)(2,1)S(1)} %slice_bitcast_fusion.1), channel_id=1, source_target_pairs={{0,2},{2,4},{4,6},{6,8},{8,10},{10,12},{12,14},{1,3},{3,5},{5,7},{... | collective-permute-start | bytes 4616 | tf_op jit(solution)/shard_map/ppermute | solution.py:448
  8.3 0.7 slice_bitcast_fusion
  9.0 1.3 %collective-permute-start.1 = (bf16[1,384]{1,0:T(2,128)(2,1)S(1)}, bf16[1,384]{1,0:T(2,128)(2,1)S(1)}, u32[]{:S(2)}, u32[]{:S(2)}) collective-permute-start(bf16[1,384]{1,0:T(2,128)(2,1)S(1)} %slice_bitcast_fusion), channel_id=1, source_target_pairs={{2,0},{4,2},{6,4},{8,6},{10,8},{12,10},{14,12},{3,1},{5,3},{7,5},{... | collective-permute-start | bytes 2312 | tf_op jit(solution)/shard_map/ppermute | solution.py:449
  10.3 1.9 %convolution_convert_fusion = bf16[96,384]{1,0:T(8,128)(2,1)S(1)} fusion(bf16[384,1536]{1,0:T(8,128)(2,1)} %refs_17_.1, bf16[1,96,1536]{2,1,0:T(8,128)(2,1)} %param.17), kind=kOutput, calls=%fused_computation | convolution fusion | flops 113283072 | bytes 1548288 | tf_op jit(solution)/shard_map/dot_general | solution.py:44
  12.2 0.1 pad.5.clone
  12.3 2.2 %collective-permute-done.1 = bf16[1,384]{1,0:T(2,128)(2,1)S(1)} collective-permute-done((bf16[1,384]{1,0:T(2,128)(2,1)S(1)}, bf16[1,384]{1,0:T(2,128)(2,1)S(1)}, u32[]{:S(2)}, u32[]{:S(2)}) %collective-permute-start.1) | collective-permute-done | bytes 800 | tf_op jit(solution)/shard_map/ppermute | solution.py:449
  14.5 0.1 maximum_maximum_fusion.refs_1_.refs_5_
  14.6 0.0 copy-start.3
  14.6 1.6 %collective-permute-start.5 = (bf16[112,384]{1,0:T(8,128)(2,1)S(1)}, bf16[112,384]{1,0:T(8,128)(2,1)S(1)}, u32[]{:S(2)}, u32[]{:S(2)}) collective-permute-start(bf16[112,384]{1,0:T(8,128)(2,1)S(1)} %maximum_maximum_fusion.refs_1_.refs_5_), channel_id=1, source_target_pairs={{0,4},{4,8},{8,12},{12,14},{14,10},{10,6},{6,2},{2,0},{1,5},{5,9},... | collective-permute-start | bytes 258056 | tf_op jit(solution)/shard_map/ppermute | solution.py:462
  16.2 0.9 collective-permute-start.6
  17.1 2.9 %collective-permute-done.5.refs_2_.refs_6_ = bf16[112,384]{1,0:T(8,128)(2,1)S(1)} collective-permute-done((bf16[112,384]{1,0:T(8,128)(2,1)S(1)}, bf16[112,384]{1,0:T(8,128)(2,1)S(1)}, u32[]{:S(2)}, u32[]{:S(2)}) %collective-permute-start.5) | collective-permute-done | bytes 86048 | tf_op jit(solution)/shard_map/ppermute | solution.py:462
  20.0 0.7 collective-permute-start.10
  20.7 0.3 collective-permute-done.6.refs_3_.refs_7_
  21.0 1.3 %collective-permute-start.11 = (bf16[112,384]{1,0:T(8,128)(2,1)S(1)}, bf16[112,384]{1,0:T(8,128)(2,1)S(1)}, u32[]{:S(2)}, u32[]{:S(2)}) collective-permute-start(bf16[112,384]{1,0:T(8,128)(2,1)S(1)} %collective-permute-done.6.refs_3_.refs_7_), channel_id=1, source_target_pairs={{4,0},{8,4},{12,8},{14,12},{10,14},{6,10},{2,6},{0,2},{5,1},{9,5},... | collective-permute-start | bytes 258056 | tf_op jit(solution)/shard_map/ppermute | solution.py:462
  22.3 0.7 collective-permute-start.8
  23.1 0.0 collective-permute-done.4.refs_1_
  23.1 1.5 %collective-permute-start.9 = (bf16[192,384]{1,0:T(8,128)(2,1)S(1)}, bf16[192,384]{1,0:T(8,128)(2,1)S(1)}, u32[]{:S(2)}, u32[]{:S(2)}) collective-permute-start(bf16[192,384]{1,0:T(8,128)(2,1)S(1)} %collective-permute-done.4.refs_1_), channel_id=1, source_target_pairs={{4,0},{8,4},{12,8},{14,12},{10,14},{6,10},{2,6},{0,2},{5,1},{9,5},... | collective-permute-start | bytes 442376 | tf_op jit(solution)/shard_map/ppermute | solution.py:461
  24.6 4.4 %conv_partial.5.mine_ref = bf16[96,1536]{1,0:T(8,128)(2,1)S(1)} custom-call(bf16[192,384]{1,0:T(8,128)(2,1)S(1)} %bitcast.16, bf16[112,384]{1,0:T(8,128)(2,1)S(1)} %maximum_maximum_fusion.refs_1_.refs_5_, bf16[1920,1536]{1,0:T(8,128)(2,1)} %bitcast.17), custom_call_target="tpu_custom_call" | custom-call | flops 566231040 | bytes 5898240 | tf_op jit(solution)/shard_map/conv_partial/pallas_call | solution.py:87
  29.0 0.6 collective-permute-start.15
  29.6 1.5 %collective-permute-start.16 = (bf16[112,384]{1,0:T(8,128)(2,1)S(1)}, bf16[112,384]{1,0:T(8,128)(2,1)S(1)}, u32[]{:S(2)}, u32[]{:S(2)}) collective-permute-start(bf16[112,384]{1,0:T(8,128)(2,1)S(1)} %collective-permute-done.11.refs_3_.refs_9_), channel_id=1, source_target_pairs={{4,0},{8,4},{12,8},{14,12},{10,14},{6,10},{2,6},{0,2},{5,1},{9,5},... | collective-permute-start | bytes 258056 | tf_op jit(solution)/shard_map/ppermute | solution.py:462
  31.1 4.8 %conv_partial.6.mine_ref = bf16[192,1536]{1,0:T(8,128)(2,1)S(1)} custom-call(bf16[192,384]{1,0:T(8,128)(2,1)S(1)} %collective-permute-done.3.refs_0_, bf16[192,384]{1,0:T(8,128)(2,1)S(1)} %collective-permute-done.4.refs_1_, bf16[112,384]{1,0:T(8,128)(2,1)S(1)} %collective-permute-done.5.refs_2_.refs_6_, ...), custom_call_target="tpu_custom_call" | custom-call | flops 1132462080 | bytes 5898240 | tf_op jit(solution)/shard_map/conv_partial/pallas_call | solution.py:87
  35.9 0.1 collective-permute-start.7
  36.0 0.0 collective-permute-done.15.refs_2_.refs_10_
  36.0 0.6 collective-permute-start.20
  36.6 1.6 %collective-permute-start.21 = (bf16[48,384]{1,0:T(8,128)(2,1)S(1)}, bf16[48,384]{1,0:T(8,128)(2,1)S(1)}, u32[]{:S(2)}, u32[]{:S(2)}) collective-permute-start(bf16[48,384]{1,0:T(8,128)(2,1)S(1)} %slice.35), channel_id=1, source_target_pairs={{4,0},{8,4},{12,8},{14,12},{10,14},{6,10},{2,6},{0,2},{5,1},{9,5},... | collective-permute-start | bytes 110600 | tf_op jit(solution)/shard_map/ppermute | solution.py:468
  38.1 0.0 collective-permute-done.8.refs_0_
  38.1 0.5 collective-permute-start.13
  38.6 0.0 collective-permute-done.9.refs_1_
  38.6 1.5 %collective-permute-start.14 = (bf16[192,384]{1,0:T(8,128)(2,1)S(1)}, bf16[192,384]{1,0:T(8,128)(2,1)S(1)}, u32[]{:S(2)}, u32[]{:S(2)}) collective-permute-start(bf16[192,384]{1,0:T(8,128)(2,1)S(1)} %collective-permute-done.9.refs_1_), channel_id=1, source_target_pairs={{4,0},{8,4},{12,8},{14,12},{10,14},{6,10},{2,6},{0,2},{5,1},{9,5},... | collective-permute-start | bytes 442376 | tf_op jit(solution)/shard_map/ppermute | solution.py:461
  40.2 5.6 %conv_partial.7.mine_ref = bf16[192,1536]{1,0:T(8,128)(2,1)} custom-call(bf16[192,384]{1,0:T(8,128)(2,1)S(1)} %collective-permute-done.8.refs_0_, bf16[192,384]{1,0:T(8,128)(2,1)S(1)} %collective-permute-done.9.refs_1_, bf16[112,384]{1,0:T(8,128)(2,1)S(1)} %collective-permute-done.10.refs_2_.refs_8_, ...), custom_call_target="tpu_custom_call" | custom-call | flops 1132462080 | bytes 5898240 | tf_op jit(solution)/shard_map/conv_partial/pallas_call | solution.py:87
  45.8 0.5 collective-permute-start.18
  46.4 1.8 %collective-permute-start.19 = (bf16[96,384]{1,0:T(8,128)(2,1)S(1)}, bf16[96,384]{1,0:T(8,128)(2,1)S(1)}, u32[]{:S(2)}, u32[]{:S(2)}) collective-permute-start(bf16[96,384]{1,0:T(8,128)(2,1)S(1)} %slice.33), channel_id=1, source_target_pairs={{4,0},{8,4},{12,8},{14,12},{10,14},{6,10},{2,6},{0,2},{5,1},{9,5},... | collective-permute-start | bytes 221192 | tf_op jit(solution)/shard_map/ppermute | solution.py:466
  48.2 5.6 %conv_partial.8.mine_ref = bf16[192,1536]{1,0:T(8,128)(2,1)} custom-call(bf16[192,384]{1,0:T(8,128)(2,1)S(1)} %collective-permute-done.13.refs_0_, bf16[192,384]{1,0:T(8,128)(2,1)S(1)} %collective-permute-done.14.refs_1_, bf16[112,384]{1,0:T(8,128)(2,1)S(1)} %collective-permute-done.15.refs_2_.refs_10_, ...), custom_call_target="tpu_custom_call" | custom-call | flops 1132462080 | bytes 5898240 | tf_op jit(solution)/shard_map/conv_partial/pallas_call | solution.py:87
  53.8 0.2 collective-permute-start.17
  54.0 0.4 collective-permute-start.2
  54.4 0.0 copy-start.20
  54.4 0.0 copy-start.21
  54.5 0.0 copy-start
  54.5 0.0 copy-start.1
  54.5 4.5 %conv_partial.9.mine_ref = bf16[96,1536]{1,0:T(8,128)(2,1)S(1)} custom-call(bf16[192,384]{1,0:T(8,128)(2,1)S(1)} %pad_maximum_fusion.refs_0_, bf16[112,384]{1,0:T(8,128)(2,1)S(1)} %constant_dynamic-update-slice_fusion.refs_1_.refs_12_, bf16[1920,1536]{1,0:T(8,128)(2,1)} %bitcast.21), custom_call_target="tpu_custom_call" | custom-call | flops 566231040 | bytes 5898240 | tf_op jit(solution)/shard_map/conv_partial/pallas_call | solution.py:87
  59.0 0.2 collective-permute-start.22
  59.3 4.1 %post.5 = (bf16[96,1152]{1,0:T(8,128)(2,1)S(1)}, bf16[96,192]{1,0:T(8,128)(2,1)S(1)}, f32[96,768]{1,0:T(8,128)S(1)}) custom-call(s32[1]{0:T(128)} %bitcast.5.place_ref, bf16[96,1536]{1,0:T(8,128)(2,1)S(1)} %conv_partial.5.mine_ref, bf16[96,1536]{1,0:T(8,128)(2,1)} %collective-permute-done.2.theirs_ref, f32[1,1536]{1,0:T(1,128)S(1)} %reshape.21.bias_ref, ...), custom_call_target="tpu_custom_call" | custom-call | flops 339738624 | bytes 3538944 | tf_op jit(solution)/shard_map/post/pallas_call | solution.py:175
  63.4 5.6 %post.6 = (bf16[192,1152]{1,0:T(8,128)(2,1)S(1)}, bf16[192,192]{1,0:T(8,128)(2,1)S(1)}) custom-call(s32[1]{0:T(128)} %bitcast.5.place_ref, bf16[192,1536]{1,0:T(8,128)(2,1)S(1)} %conv_partial.6.mine_ref, bf16[192,1536]{1,0:T(8,128)(2,1)} %collective-permute-done.7.theirs_ref, f32[1,1536]{1,0:T(1,128)S(1)} %reshape.21.bias_ref, ...), custom_call_target="tpu_custom_call" | custom-call | flops 679477248 | bytes 3538944 | tf_op jit(solution)/shard_map/post/pallas_call | solution.py:175
  69.0 4.1 %post.9 = (bf16[96,1152]{1,0:T(8,128)(2,1)S(1)}, bf16[96,192]{1,0:T(8,128)(2,1)S(1)}) custom-call(s32[1]{0:T(128)} %bitcast.5.place_ref, bf16[96,1536]{1,0:T(8,128)(2,1)S(1)} %conv_partial.9.mine_ref, bf16[96,1536]{1,0:T(8,128)(2,1)} %collective-permute-done.22.theirs_ref, f32[1,1536]{1,0:T(1,128)S(1)} %reshape.21.bias_ref, f32[1,1536]{1,0:T(1,128)S(1)} %reshape.22.gain_ref, ...), custom_call_target="tpu_custom_call" | custom-call | flops 339738624 | bytes 3538944 | tf_op jit(solution)/shard_map/post/pallas_call | solution.py:175
  73.1 5.8 %post.7 = (bf16[192,1152]{1,0:T(8,128)(2,1)S(1)}, bf16[192,192]{1,0:T(8,128)(2,1)S(1)}) custom-call(s32[1]{0:T(128)} %bitcast.5.place_ref, bf16[192,1536]{1,0:T(8,128)(2,1)} %conv_partial.7.mine_ref, bf16[192,1536]{1,0:T(8,128)(2,1)} %collective-permute-done.12.theirs_ref, f32[1,1536]{1,0:T(1,128)S(1)} %reshape.21.bias_ref, f32[1,1536]{1,0:T(1,128)S(1)} %reshape.22.gain_ref, ...), custom_call_target="tpu_custom_call" | custom-call | flops 679477248 | bytes 3538944 | tf_op jit(solution)/shard_map/post/pallas_call | solution.py:175
  78.9 0.0 copy-start.4
  78.9 0.0 copy-start.12
  78.9 0.0 copy-start.14
  79.0 5.9 %post.8 = (bf16[192,1152]{1,0:T(8,128)(2,1)S(1)}, bf16[192,192]{1,0:T(8,128)(2,1)S(1)}) custom-call(s32[1]{0:T(128)} %bitcast.5.place_ref, bf16[192,1536]{1,0:T(8,128)(2,1)} %conv_partial.8.mine_ref, bf16[192,1536]{1,0:T(8,128)(2,1)} %collective-permute-done.17.theirs_ref, f32[1,1536]{1,0:T(1,128)S(1)} %reshape.21.bias_ref, f32[1,1536]{1,0:T(1,128)S(1)} %reshape.22.gain_ref, ...), custom_call_target="tpu_custom_call" | custom-call | flops 679477248 | bytes 3538944 | tf_op jit(solution)/shard_map/post/pallas_call | solution.py:175
  85.0 0.0 copy-start.2
  85.0 9.8 %attention.1 = (bf16[192,1536]{1,0:T(8,128)(2,1)S(1)}, bf16[768,384]{1,0:T(8,128)(2,1)S(1)}) custom-call(bf16[96,1152]{1,0:T(8,128)(2,1)S(1)} %get-tuple-element.20.refs_0_, bf16[192,1152]{1,0:T(8,128)(2,1)S(1)} %get-tuple-element.21.refs_1_, bf16[192,1152]{1,0:T(8,128)(2,1)S(1)} %get-tuple-element.22.refs_2_, ...), custom_call_target="tpu_custom_call" | custom-call | flops 1358954496 | bytes 2359296 | tf_op jit(solution)/shard_map/attention/pallas_call | solution.py:271
  94.8 0.4 collective-permute-start.23
  95.2 1.7 %collective-permute-done.23.there_ref = bf16[192,1536]{1,0:T(8,128)(2,1)S(1)} collective-permute-done((bf16[192,1536]{1,0:T(8,128)(2,1)S(1)}, bf16[192,1536]{1,0:T(8,128)(2,1)S(1)}, u32[]{:S(2)}, u32[]{:S(2)}) %collective-permute-start.23) | collective-permute-done | bytes 589856 | tf_op jit(solution)/shard_map/ppermute | solution.py:486
  96.9 2.9 %finish.1 = (bf16[96,1536]{1,0:T(8,128)(2,1)}, bf16[96,1536]{1,0:T(8,128)(2,1)S(1)}, bf16[1,1536]{1,0:T(2,128)(2,1)S(1)}, bf16[1,1536]{1,0:T(2,128)(2,1)S(1)}) custom-call(bf16[96,1536]{1,0:T(8,128)(2,1)S(1)} %conv_partial.5.mine_ref, bf16[96,1536]{1,0:T(8,128)(2,1)} %collective-permute-done.2.theirs_ref, f32[1,1536]{1,0:T(1,128)S(1)} %reshape.21.bias_ref, ...), custom_call_target="tpu_custom_call" | custom-call | flops 5898240 | bytes 1769472 | tf_op jit(solution)/shard_map/finish/pallas_call | solution.py:333
  99.8 3.8 %collective-permute-start.24 = (bf16[1,1536]{1,0:T(2,128)(2,1)S(1)}, bf16[1,1536]{1,0:T(2,128)(2,1)S(1)}, u32[]{:S(2)}, u32[]{:S(2)}) collective-permute-start(bf16[1,1536]{1,0:T(2,128)(2,1)S(1)} %get-tuple-element.29), channel_id=1, source_target_pairs={{0,2},{2,4},{4,6},{6,8},{8,10},{10,12},{12,14},{1,3},{3,5},{5,7},{... | collective-permute-start | bytes 9224 | tf_op jit(solution)/shard_map/ppermute | solution.py:489
  103.6 1.3 %collective-permute-start.25 = (bf16[1,1536]{1,0:T(2,128)(2,1)S(1)}, bf16[1,1536]{1,0:T(2,128)(2,1)S(1)}, u32[]{:S(2)}, u32[]{:S(2)}) collective-permute-start(bf16[1,1536]{1,0:T(2,128)(2,1)S(1)} %get-tuple-element.30), channel_id=1, source_target_pairs={{2,0},{4,2},{6,4},{8,6},{10,8},{12,10},{14,12},{3,1},{5,3},{7,5},{... | collective-permute-start | bytes 9224 | tf_op jit(solution)/shard_map/ppermute | solution.py:490
  104.9 0.5 value_gradient.1
  105.3 0.9 copy.12
  106.2 2.9 %collective-permute-done.25.after_ref = bf16[1,1536]{1,0:T(2,128)(2,1)S(1)} collective-permute-done((bf16[1,1536]{1,0:T(2,128)(2,1)S(1)}, bf16[1,1536]{1,0:T(2,128)(2,1)S(1)}, u32[]{:S(2)}, u32[]{:S(2)}) %collective-permute-start.25) | collective-permute-done | bytes 3104 | tf_op jit(solution)/shard_map/ppermute | solution.py:490
  109.1 6.4 %conv_back.1 = bf16[192,384]{1,0:T(8,128)(2,1)} custom-call(bf16[96,1536]{1,0:T(8,128)(2,1)S(1)} %get-tuple-element.28.pre_ref, bf16[1,1536]{1,0:T(2,128)(2,1)S(1)} %collective-permute-done.24.before_ref, bf16[1,1536]{1,0:T(2,128)(2,1)S(1)} %collective-permute-done.25.after_ref, bf16[5,384,1536]{2,1,0:T(8,128)(2,1)} %weight_ref.1), custom_call_target="tpu_custom_call" | custom-call | flops 566231040 | bytes 5898240 | tf_op jit(solution)/shard_map/conv_back/pallas_call | solution.py:379
  (62 shorter events, 0.2 us)
Async XLA Ops:
  0.6 23.9 %copy-start.19 = (bf16[1,192,384]{2,1,0:T(8,128)(2,1)S(1)}, bf16[1,192,384]{2,1,0:T(8,128)(2,1)}, u32[]{:S(2)}) copy-start(bf16[1,192,384]{2,1,0:T(8,128)(2,1)} %param.9) | copy-start | bytes 442372
  0.6 21.7 %collective-permute-start.3 = (bf16[192,384]{1,0:T(8,128)(2,1)}, bf16[192,384]{1,0:T(8,128)(2,1)S(1)}, u32[]{:S(2)}, u32[]{:S(2)}) collective-permute-start(bf16[192,384]{1,0:T(8,128)(2,1)} %bitcast.14), channel_id=1, source_target_pairs={{0,4},{4,8},{8,12},{12,14},{14,10},{10,6},{6,2},{2,0},{1,5},{5,9},... | collective-permute-start | bytes 442376 | tf_op jit(solution)/shard_map/ppermute | solution.py:461
  3.7 19.4 %collective-permute-start.4 = (bf16[192,384]{1,0:T(8,128)(2,1)}, bf16[192,384]{1,0:T(8,128)(2,1)S(1)}, u32[]{:S(2)}, u32[]{:S(2)}) collective-permute-start(bf16[192,384]{1,0:T(8,128)(2,1)} %bitcast.15), channel_id=1, source_target_pairs={{4,0},{8,4},{12,8},{14,12},{10,14},{6,10},{2,6},{0,2},{5,1},{9,5},... | collective-permute-start | bytes 442376 | tf_op jit(solution)/shard_map/ppermute | solution.py:461
  4.5 10.0 %collective-permute-start = (bf16[2,384]{1,0:T(2,128)(2,1)S(1)}, bf16[2,384]{1,0:T(2,128)(2,1)S(1)}, u32[]{:S(2)}, u32[]{:S(2)}) collective-permute-start(bf16[2,384]{1,0:T(2,128)(2,1)S(1)} %slice_bitcast_fusion.1), channel_id=1, source_target_pairs={{0,2},{2,4},{4,6},{6,8},{8,10},{10,12},{12,14},{1,3},{3,5},{5,7},{... | collective-permute-start | bytes 4616 | tf_op jit(solution)/shard_map/ppermute | solution.py:448
  9.0 5.5 %collective-permute-start.1 = (bf16[1,384]{1,0:T(2,128)(2,1)S(1)}, bf16[1,384]{1,0:T(2,128)(2,1)S(1)}, u32[]{:S(2)}, u32[]{:S(2)}) collective-permute-start(bf16[1,384]{1,0:T(2,128)(2,1)S(1)} %slice_bitcast_fusion), channel_id=1, source_target_pairs={{2,0},{4,2},{6,4},{8,6},{10,8},{12,10},{14,12},{3,1},{5,3},{7,5},{... | collective-permute-start | bytes 2312 | tf_op jit(solution)/shard_map/ppermute | solution.py:449
  14.6 14.4 %copy-start.3 = (bf16[112,384]{1,0:T(8,128)(2,1)}, bf16[112,384]{1,0:T(8,128)(2,1)S(1)}, u32[]{:S(2)}) copy-start(bf16[112,384]{1,0:T(8,128)(2,1)S(1)} %maximum_maximum_fusion.refs_1_.refs_5_) | copy-start | bytes 258052
  14.6 5.4 %collective-permute-start.5 = (bf16[112,384]{1,0:T(8,128)(2,1)S(1)}, bf16[112,384]{1,0:T(8,128)(2,1)S(1)}, u32[]{:S(2)}, u32[]{:S(2)}) collective-permute-start(bf16[112,384]{1,0:T(8,128)(2,1)S(1)} %maximum_maximum_fusion.refs_1_.refs_5_), channel_id=1, source_target_pairs={{0,4},{4,8},{8,12},{12,14},{14,10},{10,6},{6,2},{2,0},{1,5},{5,9},... | collective-permute-start | bytes 258056 | tf_op jit(solution)/shard_map/ppermute | solution.py:462
  16.2 4.8 %collective-permute-start.6 = (bf16[112,384]{1,0:T(8,128)(2,1)S(1)}, bf16[112,384]{1,0:T(8,128)(2,1)S(1)}, u32[]{:S(2)}, u32[]{:S(2)}) collective-permute-start(bf16[112,384]{1,0:T(8,128)(2,1)S(1)} %maximum_maximum_fusion.refs_1_.refs_5_), channel_id=1, source_target_pairs={{4,0},{8,4},{12,8},{14,12},{10,14},{6,10},{2,6},{0,2},{5,1},{9,5},... | collective-permute-start | bytes 258056 | tf_op jit(solution)/shard_map/ppermute | solution.py:462
  20.0 11.0 %copy-start.11 = (bf16[112,384]{1,0:T(8,128)(2,1)}, bf16[112,384]{1,0:T(8,128)(2,1)S(1)}, u32[]{:S(2)}) copy-start(bf16[112,384]{1,0:T(8,128)(2,1)S(1)} %collective-permute-done.5.refs_2_.refs_6_) | copy-start | bytes 258052
  20.0 8.9 %collective-permute-start.10 = (bf16[112,384]{1,0:T(8,128)(2,1)S(1)}, bf16[112,384]{1,0:T(8,128)(2,1)S(1)}, u32[]{:S(2)}, u32[]{:S(2)}) collective-permute-start(bf16[112,384]{1,0:T(8,128)(2,1)S(1)} %collective-permute-done.5.refs_2_.refs_6_), channel_id=1, source_target_pairs={{0,4},{4,8},{8,12},{12,14},{14,10},{10,6},{6,2},{2,0},{1,5},{5,9},... | collective-permute-start | bytes 258056 | tf_op jit(solution)/shard_map/ppermute | solution.py:462
  21.0 10.0 %copy-start.13 = (bf16[112,384]{1,0:T(8,128)(2,1)}, bf16[112,384]{1,0:T(8,128)(2,1)S(1)}, u32[]{:S(2)}) copy-start(bf16[112,384]{1,0:T(8,128)(2,1)S(1)} %collective-permute-done.6.refs_3_.refs_7_) | copy-start | bytes 258052
  21.0 8.5 %collective-permute-start.11 = (bf16[112,384]{1,0:T(8,128)(2,1)S(1)}, bf16[112,384]{1,0:T(8,128)(2,1)S(1)}, u32[]{:S(2)}, u32[]{:S(2)}) collective-permute-start(bf16[112,384]{1,0:T(8,128)(2,1)S(1)} %collective-permute-done.6.refs_3_.refs_7_), channel_id=1, source_target_pairs={{4,0},{8,4},{12,8},{14,12},{10,14},{6,10},{2,6},{0,2},{5,1},{9,5},... | collective-permute-start | bytes 258056 | tf_op jit(solution)/shard_map/ppermute | solution.py:462
  22.3 15.8 %collective-permute-start.8 = (bf16[192,384]{1,0:T(8,128)(2,1)S(1)}, bf16[192,384]{1,0:T(8,128)(2,1)S(1)}, u32[]{:S(2)}, u32[]{:S(2)}) collective-permute-start(bf16[192,384]{1,0:T(8,128)(2,1)S(1)} %collective-permute-done.3.refs_0_), channel_id=1, source_target_pairs={{0,4},{4,8},{8,12},{12,14},{14,10},{10,6},{6,2},{2,0},{1,5},{5,9},... | collective-permute-start | bytes 442376 | tf_op jit(solution)/shard_map/ppermute | solution.py:461
  23.1 15.6 %collective-permute-start.9 = (bf16[192,384]{1,0:T(8,128)(2,1)S(1)}, bf16[192,384]{1,0:T(8,128)(2,1)S(1)}, u32[]{:S(2)}, u32[]{:S(2)}) collective-permute-start(bf16[192,384]{1,0:T(8,128)(2,1)S(1)} %collective-permute-done.4.refs_1_), channel_id=1, source_target_pairs={{4,0},{8,4},{12,8},{14,12},{10,14},{6,10},{2,6},{0,2},{5,1},{9,5},... | collective-permute-start | bytes 442376 | tf_op jit(solution)/shard_map/ppermute | solution.py:461
  29.0 11.2 %copy-start.15 = (bf16[112,384]{1,0:T(8,128)(2,1)}, bf16[112,384]{1,0:T(8,128)(2,1)S(1)}, u32[]{:S(2)}) copy-start(bf16[112,384]{1,0:T(8,128)(2,1)S(1)} %collective-permute-done.10.refs_2_.refs_8_) | copy-start | bytes 258052
  29.0 7.0 %collective-permute-start.15 = (bf16[112,384]{1,0:T(8,128)(2,1)S(1)}, bf16[112,384]{1,0:T(8,128)(2,1)S(1)}, u32[]{:S(2)}, u32[]{:S(2)}) collective-permute-start(bf16[112,384]{1,0:T(8,128)(2,1)S(1)} %collective-permute-done.10.refs_2_.refs_8_), channel_id=1, source_target_pairs={{0,4},{4,8},{8,12},{12,14},{14,10},{10,6},{6,2},{2,0},{1,5},{5,9},... | collective-permute-start | bytes 258056 | tf_op jit(solution)/shard_map/ppermute | solution.py:462
  29.6 10.6 %copy-start.17 = (bf16[112,384]{1,0:T(8,128)(2,1)}, bf16[112,384]{1,0:T(8,128)(2,1)S(1)}, u32[]{:S(2)}) copy-start(bf16[112,384]{1,0:T(8,128)(2,1)S(1)} %collective-permute-done.11.refs_3_.refs_9_) | copy-start | bytes 258052
  29.6 7.0 %collective-permute-start.16 = (bf16[112,384]{1,0:T(8,128)(2,1)S(1)}, bf16[112,384]{1,0:T(8,128)(2,1)S(1)}, u32[]{:S(2)}, u32[]{:S(2)}) collective-permute-start(bf16[112,384]{1,0:T(8,128)(2,1)S(1)} %collective-permute-done.11.refs_3_.refs_9_), channel_id=1, source_target_pairs={{4,0},{8,4},{12,8},{14,12},{10,14},{6,10},{2,6},{0,2},{5,1},{9,5},... | collective-permute-start | bytes 258056 | tf_op jit(solution)/shard_map/ppermute | solution.py:462
  35.9 27.5 %collective-permute-start.7 = (bf16[192,1536]{1,0:T(8,128)(2,1)S(1)}, bf16[192,1536]{1,0:T(8,128)(2,1)}, u32[]{:S(2)}, u32[]{:S(2)}) collective-permute-start(bf16[192,1536]{1,0:T(8,128)(2,1)S(1)} %conv_partial.6.mine_ref), channel_id=1, source_target_pairs={{0,1},{1,0},{2,3},{3,2},{4,5},{5,4},{6,7},{7,6},{8,9},{9,8},{10,11... | collective-permute-start | bytes 1769480 | tf_op jit(solution)/shard_map/ppermute | solution.py:475
  36.0 12.2 %copy-start.5 = (bf16[112,384]{1,0:T(8,128)(2,1)}, bf16[112,384]{1,0:T(8,128)(2,1)S(1)}, u32[]{:S(2)}) copy-start(bf16[112,384]{1,0:T(8,128)(2,1)S(1)} %collective-permute-done.15.refs_2_.refs_10_) | copy-start | bytes 258052
  36.0 9.8 %collective-permute-start.20 = (bf16[64,384]{1,0:T(8,128)(2,1)S(1)}, bf16[64,384]{1,0:T(8,128)(2,1)S(1)}, u32[]{:S(2)}, u32[]{:S(2)}) collective-permute-start(bf16[64,384]{1,0:T(8,128)(2,1)S(1)} %slice.34), channel_id=1, source_target_pairs={{0,4},{4,8},{8,12},{12,14},{14,10},{10,6},{6,2},{2,0},{1,5},{5,9},... | collective-permute-start | bytes 147464 | tf_op jit(solution)/shard_map/ppermute | solution.py:467
  36.6 11.6 %copy-start.9 = (bf16[112,384]{1,0:T(8,128)(2,1)}, bf16[112,384]{1,0:T(8,128)(2,1)S(1)}, u32[]{:S(2)}) copy-start(bf16[112,384]{1,0:T(8,128)(2,1)S(1)} %collective-permute-done.16.refs_3_.refs_11_) | copy-start | bytes 258052
  36.6 17.2 %collective-permute-start.21 = (bf16[48,384]{1,0:T(8,128)(2,1)S(1)}, bf16[48,384]{1,0:T(8,128)(2,1)S(1)}, u32[]{:S(2)}, u32[]{:S(2)}) collective-permute-start(bf16[48,384]{1,0:T(8,128)(2,1)S(1)} %slice.35), channel_id=1, source_target_pairs={{4,0},{8,4},{12,8},{14,12},{10,14},{6,10},{2,6},{0,2},{5,1},{9,5},... | collective-permute-start | bytes 110600 | tf_op jit(solution)/shard_map/ppermute | solution.py:468
  38.1 7.7 %collective-permute-start.13 = (bf16[192,384]{1,0:T(8,128)(2,1)S(1)}, bf16[192,384]{1,0:T(8,128)(2,1)S(1)}, u32[]{:S(2)}, u32[]{:S(2)}) collective-permute-start(bf16[192,384]{1,0:T(8,128)(2,1)S(1)} %collective-permute-done.8.refs_0_), channel_id=1, source_target_pairs={{0,4},{4,8},{8,12},{12,14},{14,10},{10,6},{6,2},{2,0},{1,5},{5,9},... | collective-permute-start | bytes 442376 | tf_op jit(solution)/shard_map/ppermute | solution.py:461
  38.6 7.7 %collective-permute-start.14 = (bf16[192,384]{1,0:T(8,128)(2,1)S(1)}, bf16[192,384]{1,0:T(8,128)(2,1)S(1)}, u32[]{:S(2)}, u32[]{:S(2)}) collective-permute-start(bf16[192,384]{1,0:T(8,128)(2,1)S(1)} %collective-permute-done.9.refs_1_), channel_id=1, source_target_pairs={{4,0},{8,4},{12,8},{14,12},{10,14},{6,10},{2,6},{0,2},{5,1},{9,5},... | collective-permute-start | bytes 442376 | tf_op jit(solution)/shard_map/ppermute | solution.py:461
  45.8 27.3 %collective-permute-start.12 = (bf16[192,1536]{1,0:T(8,128)(2,1)}, bf16[192,1536]{1,0:T(8,128)(2,1)}, u32[]{:S(2)}, u32[]{:S(2)}) collective-permute-start(bf16[192,1536]{1,0:T(8,128)(2,1)} %conv_partial.7.mine_ref), channel_id=1, source_target_pairs={{0,1},{1,0},{2,3},{3,2},{4,5},{5,4},{6,7},{7,6},{8,9},{9,8},{10,11... | collective-permute-start | bytes 1769480 | tf_op jit(solution)/shard_map/ppermute | solution.py:475
  45.8 8.1 %collective-permute-start.18 = (bf16[96,384]{1,0:T(8,128)(2,1)S(1)}, bf16[96,384]{1,0:T(8,128)(2,1)S(1)}, u32[]{:S(2)}, u32[]{:S(2)}) collective-permute-start(bf16[96,384]{1,0:T(8,128)(2,1)S(1)} %slice.32), channel_id=1, source_target_pairs={{0,4},{4,8},{8,12},{12,14},{14,10},{10,6},{6,2},{2,0},{1,5},{5,9},... | collective-permute-start | bytes 221192 | tf_op jit(solution)/shard_map/ppermute | solution.py:466
  46.4 8.0 %collective-permute-start.19 = (bf16[96,384]{1,0:T(8,128)(2,1)S(1)}, bf16[96,384]{1,0:T(8,128)(2,1)S(1)}, u32[]{:S(2)}, u32[]{:S(2)}) collective-permute-start(bf16[96,384]{1,0:T(8,128)(2,1)S(1)} %slice.33), channel_id=1, source_target_pairs={{4,0},{8,4},{12,8},{14,12},{10,14},{6,10},{2,6},{0,2},{5,1},{9,5},... | collective-permute-start | bytes 221192 | tf_op jit(solution)/shard_map/ppermute | solution.py:466
  53.8 25.2 %collective-permute-start.17 = (bf16[192,1536]{1,0:T(8,128)(2,1)}, bf16[192,1536]{1,0:T(8,128)(2,1)}, u32[]{:S(2)}, u32[]{:S(2)}) collective-permute-start(bf16[192,1536]{1,0:T(8,128)(2,1)} %conv_partial.8.mine_ref), channel_id=1, source_target_pairs={{0,1},{1,0},{2,3},{3,2},{4,5},{5,4},{6,7},{7,6},{8,9},{9,8},{10,11... | collective-permute-start | bytes 1769480 | tf_op jit(solution)/shard_map/ppermute | solution.py:475
  54.0 5.0 %copy-start.7 = (bf16[112,384]{1,0:T(8,128)(2,1)}, bf16[112,384]{1,0:T(8,128)(2,1)S(1)}, u32[]{:S(2)}) copy-start(bf16[112,384]{1,0:T(8,128)(2,1)S(1)} %constant_dynamic-update-slice_fusion.refs_1_.refs_12_) | copy-start | bytes 258052
  54.0 5.3 %collective-permute-start.2 = (bf16[96,1536]{1,0:T(8,128)(2,1)S(1)}, bf16[96,1536]{1,0:T(8,128)(2,1)}, u32[]{:S(2)}, u32[]{:S(2)}) collective-permute-start(bf16[96,1536]{1,0:T(8,128)(2,1)S(1)} %conv_partial.5.mine_ref), channel_id=1, source_target_pairs={{0,1},{1,0},{2,3},{3,2},{4,5},{5,4},{6,7},{7,6},{8,9},{9,8},{10,11... | collective-permute-start | bytes 884744 | tf_op jit(solution)/shard_map/ppermute | solution.py:475
  54.4 4.8 %copy-start.20 = (f32[1536]{0:T(1024)S(1)}, f32[1536]{0:T(1024)}, u32[]{:S(2)}) copy-start(f32[1536]{0:T(1024)} %param.11) | copy-start | bytes 18436
  54.4 4.8 %copy-start.21 = (f32[1536]{0:T(1024)S(1)}, f32[1536]{0:T(1024)}, u32[]{:S(2)}) copy-start(f32[1536]{0:T(1024)} %param.12) | copy-start | bytes 18436
  54.5 4.9 %copy-start = (bf16[1536,384]{1,0:T(8,128)(2,1)S(1)}, bf16[1536,384]{1,0:T(8,128)(2,1)}, u32[]{:S(2)}) copy-start(bf16[1536,384]{1,0:T(8,128)(2,1)} %refs_14_.1) | copy-start | bytes 3538948
  54.5 4.9 %copy-start.1 = (bf16[1536,384]{1,0:T(8,128)(2,1)S(1)}, bf16[1536,384]{1,0:T(8,128)(2,1)}, u32[]{:S(2)}) copy-start(bf16[1536,384]{1,0:T(8,128)(2,1)} %refs_15_.1) | copy-start | bytes 3538948
  59.0 10.0 %collective-permute-start.22 = (bf16[96,1536]{1,0:T(8,128)(2,1)S(1)}, bf16[96,1536]{1,0:T(8,128)(2,1)}, u32[]{:S(2)}, u32[]{:S(2)}) collective-permute-start(bf16[96,1536]{1,0:T(8,128)(2,1)S(1)} %conv_partial.9.mine_ref), channel_id=1, source_target_pairs={{0,1},{1,0},{2,3},{3,2},{4,5},{5,4},{6,7},{7,6},{8,9},{9,8},{10,11... | collective-permute-start | bytes 884744 | tf_op jit(solution)/shard_map/ppermute | solution.py:475
  78.9 6.0 %copy-start.4 = (bf16[112,384]{1,0:T(8,128)(2,1)S(1)}, bf16[112,384]{1,0:T(8,128)(2,1)}, u32[]{:S(2)}) copy-start(bf16[112,384]{1,0:T(8,128)(2,1)} %copy-done.3) | copy-start | bytes 258052
  78.9 6.0 %copy-start.6 = (bf16[112,384]{1,0:T(8,128)(2,1)S(1)}, bf16[112,384]{1,0:T(8,128)(2,1)}, u32[]{:S(2)}) copy-start(bf16[112,384]{1,0:T(8,128)(2,1)} %copy-done.5) | copy-start | bytes 258052
  78.9 6.0 %copy-start.8 = (bf16[112,384]{1,0:T(8,128)(2,1)S(1)}, bf16[112,384]{1,0:T(8,128)(2,1)}, u32[]{:S(2)}) copy-start(bf16[112,384]{1,0:T(8,128)(2,1)} %copy-done.7) | copy-start | bytes 258052
  78.9 6.0 %copy-start.10 = (bf16[112,384]{1,0:T(8,128)(2,1)S(1)}, bf16[112,384]{1,0:T(8,128)(2,1)}, u32[]{:S(2)}) copy-start(bf16[112,384]{1,0:T(8,128)(2,1)} %copy-done.9) | copy-start | bytes 258052
  78.9 6.0 %copy-start.12 = (bf16[112,384]{1,0:T(8,128)(2,1)S(1)}, bf16[112,384]{1,0:T(8,128)(2,1)}, u32[]{:S(2)}) copy-start(bf16[112,384]{1,0:T(8,128)(2,1)} %copy-done.11) | copy-start | bytes 258052
  78.9 6.0 %copy-start.14 = (bf16[112,384]{1,0:T(8,128)(2,1)S(1)}, bf16[112,384]{1,0:T(8,128)(2,1)}, u32[]{:S(2)}) copy-start(bf16[112,384]{1,0:T(8,128)(2,1)} %copy-done.13) | copy-start | bytes 258052
  78.9 6.0 %copy-start.16 = (bf16[112,384]{1,0:T(8,128)(2,1)S(1)}, bf16[112,384]{1,0:T(8,128)(2,1)}, u32[]{:S(2)}) copy-start(bf16[112,384]{1,0:T(8,128)(2,1)} %copy-done.15) | copy-start | bytes 258052
  79.0 6.0 %copy-start.18 = (bf16[112,384]{1,0:T(8,128)(2,1)S(1)}, bf16[112,384]{1,0:T(8,128)(2,1)}, u32[]{:S(2)}) copy-start(bf16[112,384]{1,0:T(8,128)(2,1)} %copy-done.17) | copy-start | bytes 258052
  85.0 11.9 %copy-start.2 = (bf16[1,96,1536]{2,1,0:T(8,128)(2,1)S(1)}, bf16[1,96,1536]{2,1,0:T(8,128)(2,1)}, u32[]{:S(2)}) copy-start(bf16[1,96,1536]{2,1,0:T(8,128)(2,1)} %param.17) | copy-start | bytes 884740
  94.8 2.1 %collective-permute-start.23 = (bf16[192,1536]{1,0:T(8,128)(2,1)S(1)}, bf16[192,1536]{1,0:T(8,128)(2,1)S(1)}, u32[]{:S(2)}, u32[]{:S(2)}) collective-permute-start(bf16[192,1536]{1,0:T(8,128)(2,1)S(1)} %get-tuple-element.26.here_ref), channel_id=1, source_target_pairs={{0,1},{1,0},{2,3},{3,2},{4,5},{5,4},{6,7},{7,6},{8,9},{9,8},{10,11... | collective-permute-start | bytes 1769480 | tf_op jit(solution)/shard_map/ppermute | solution.py:486
  99.8 6.4 %collective-permute-start.24 = (bf16[1,1536]{1,0:T(2,128)(2,1)S(1)}, bf16[1,1536]{1,0:T(2,128)(2,1)S(1)}, u32[]{:S(2)}, u32[]{:S(2)}) collective-permute-start(bf16[1,1536]{1,0:T(2,128)(2,1)S(1)} %get-tuple-element.29), channel_id=1, source_target_pairs={{0,2},{2,4},{4,6},{6,8},{8,10},{10,12},{12,14},{1,3},{3,5},{5,7},{... | collective-permute-start | bytes 9224 | tf_op jit(solution)/shard_map/ppermute | solution.py:489
  103.6 5.5 %collective-permute-start.25 = (bf16[1,1536]{1,0:T(2,128)(2,1)S(1)}, bf16[1,1536]{1,0:T(2,128)(2,1)S(1)}, u32[]{:S(2)}, u32[]{:S(2)}) collective-permute-start(bf16[1,1536]{1,0:T(2,128)(2,1)S(1)} %get-tuple-element.30), channel_id=1, source_target_pairs={{2,0},{4,2},{6,4},{8,6},{10,8},{12,10},{14,12},{3,1},{5,3},{7,5},{... | collective-permute-start | bytes 9224 | tf_op jit(solution)/shard_map/ppermute | solution.py:490

commit v2 on v1

v2 whole, which is shorter than its diff:
```python
import functools
import math

import jax
import jax.numpy as jnp
from jax import lax
from jax.experimental import pallas as pl
from jax.experimental.pallas import tpu as pltpu
from jax.sharding import PartitionSpec as P

DH = 192
EPSILON = 1e-06
SCORE_GAIN = 3.0
GELU_ROOT = 0.7978845608028654
GELU_CUBIC = 0.044715
F32 = jnp.float32
BF16 = jnp.bfloat16
HALO_ROWS = 16
CHUNK = 16
SMEM = pl.BlockSpec(memory_space=pltpu.SMEM)
MIB = 1024 * 1024


def spec():
    return pl.BlockSpec(memory_space=pltpu.VMEM)


def in_hbm():
    return pl.BlockSpec(memory_space=pltpu.HBM)


def anywhere():
    return pl.BlockSpec(memory_space=pl.ANY)


def far(value):
    return pltpu.with_memory_space_constraint(value, pltpu.HBM)


def near_core(value):
    return pltpu.with_memory_space_constraint(value, pltpu.VMEM)


def params(limit=8):
    return pltpu.CompilerParams(vmem_limit_bytes=limit * MIB)


def cost(flops, nbytes):
    return pl.CostEstimate(flops=int(flops), bytes_accessed=int(nbytes), transcendentals=0)


def dot(left, right):
    return jnp.dot(left, right, preferred_element_type=F32)


def dot_rt(left, right):
    return lax.dot_general(left, right, (((1,), (1,)), ((), ())), preferred_element_type=F32)


def dot_lt(left, right):
    return lax.dot_general(left, right, (((0,), (0,)), ((), ())), preferred_element_type=F32)


def pick(shape, test):
    row = lax.broadcasted_iota(jnp.int32, shape, 0)
    col = lax.broadcasted_iota(jnp.int32, shape, 1)
    return jnp.where(test(row, col), 1.0, 0.0).astype(BF16)


def edges_kernel(fine_any, fine_ref, edge_ref, sem):
    copy = pltpu.make_async_copy(fine_any, fine_ref, sem)
    copy.start()
    copy.wait()
    rows = fine_ref.shape[0]
    edge_ref[0:2, :] = fine_ref[rows - 2 :, :]
    edge_ref[2:3, :] = fine_ref[0:1, :]


def edges(fine):
    return pl.pallas_call(
        edges_kernel,
        out_shape=[
            jax.ShapeDtypeStruct(fine.shape, BF16),
            jax.ShapeDtypeStruct((3, fine.shape[1]), BF16),
        ],
        in_specs=[in_hbm()],
        out_specs=[spec()] * 2,
        scratch_shapes=[pltpu.SemaphoreType.DMA],
        compiler_params=params(),
        cost_estimate=cost(fine.size, 2 * fine.size),
        name="edges",
    )(far(fine))


def sided(place_ref, first_ref, second_ref, before_rows):
    even = place_ref[0] % 2 == 0
    first, second = first_ref[...].astype(F32), second_ref[...].astype(F32)
    low = lax.broadcasted_iota(jnp.int32, first.shape, 0) < before_rows
    return jnp.where(low == even, second, first).astype(BF16)


def early_kernel(cot_any, wo_any, grad_ref, cot, wo, sems):
    copies = [
        pltpu.make_async_copy(cot_any, cot, sems.at[0]),
        pltpu.make_async_copy(wo_any, wo, sems.at[1]),
    ]
    for c in copies:
        c.start()
    for c in copies:
        c.wait()
    grad_ref[...] = dot_rt(cot[...], wo[...]).astype(BF16)


def early(cot, wo):
    tok, features = cot.shape
    width = wo.shape[0]
    return pl.pallas_call(
        early_kernel,
        out_shape=jax.ShapeDtypeStruct((tok, width), BF16),
        in_specs=[in_hbm()] * 2,
        out_specs=spec(),
        scratch_shapes=[
            pltpu.VMEM((tok, features), BF16),
            pltpu.VMEM(wo.shape, BF16),
            pltpu.SemaphoreType.DMA((2,)),
        ],
        compiler_params=params(),
        cost_estimate=cost(2 * tok * features * width, 2 * wo.size),
        name="early",
    )(far(cot), far(wo))


def conv_kernel(order, place_ref, fine_ref, first_ref, second_ref, taps_any, out_ref, taps, sems):
    fine_rows, channels = fine_ref.shape
    tok = fine_rows // 2
    copies = {k: pltpu.make_async_copy(taps_any.at[k], taps.at[k], sems.at[k]) for k in order}
    for k in order:
        copies[k].start()
    side = sided(place_ref, first_ref, second_ref, 2)
    spare_rows = jnp.zeros((HALO_ROWS - side.shape[0], channels), BF16)
    block = jnp.concatenate([fine_ref[...], side, spare_rows], 0)
    total = None
    for k in order:

        def test(row, col, k=k):
            want = 2 * row + k - 2
            inside = (want >= 0) & (want < fine_rows)
            spare = jnp.where(want < 0, fine_rows + 2 + want, want + 2)
            return col == jnp.where(inside, want, spare)

        rows = dot(pick((tok, fine_rows + HALO_ROWS), test), block).astype(BF16)
        copies[k].wait()
        term = dot(rows, taps[k])
        total = term if total is None else total + term
    out_ref[...] = total.astype(BF16)


def conv_partial(place, fine, first, second, weight):
    taps, channels, features = weight.shape
    tok = fine.shape[0] // 2
    return pl.pallas_call(
        functools.partial(conv_kernel, tuple(range(taps))),
        out_shape=jax.ShapeDtypeStruct((tok, features), BF16),
        in_specs=[SMEM] + [spec()] * 3 + [in_hbm()],
        out_specs=spec(),
        scratch_shapes=[pltpu.VMEM(weight.shape, BF16), pltpu.SemaphoreType.DMA((taps,))],
        compiler_params=params(12),
        cost_estimate=cost(2 * tok * weight.size, 2 * weight.size),
        name="conv_partial",
    )(place, fine, first, second, far(weight))


def gelu_value(preact):
    tangent = jnp.tanh(GELU_ROOT * (preact + GELU_CUBIC * preact * preact * preact))
    return 0.5 * preact * (1.0 + tangent), tangent


def head_scale(value):
    lane = lax.broadcasted_iota(jnp.int32, value.shape, 1)
    square = value * value
    parts = value.shape[1] // DH
    scale = jnp.zeros_like(value)
    for h in range(parts):
        here = (lane >= h * DH) & (lane < (h + 1) * DH)
        mean = jnp.sum(jnp.where(here, square, 0.0), -1, keepdims=True) * (1.0 / DH)
        scale = jnp.where(here, lax.rsqrt(mean + EPSILON), scale)
    return scale


def head_mean(value):
    lane = lax.broadcasted_iota(jnp.int32, value.shape, 1)
    parts = value.shape[1] // DH
    out = jnp.zeros_like(value)
    for h in range(parts):
        here = (lane >= h * DH) & (lane < (h + 1) * DH)
        mean = jnp.sum(jnp.where(here, value, 0.0), -1, keepdims=True) * (1.0 / DH)
        out = jnp.where(here, mean, out)
    return out


def norm_kernel(wide_ref, mine_ref, theirs_ref, bias_ref, gain_ref, *refs):
    weights_any, (grad_ref, normed_ref, message_ref), weights, sems = refs[:3], refs[3:6], refs[6:9], refs[9]
    tok, features = mine_ref.shape
    width = message_ref.shape[1]
    half = tok // 2
    copies = [pltpu.make_async_copy(weights_any[i], weights[i], sems.at[i]) for i in range(3)]
    for c in copies:
        c.start()

    @pl.loop(0, tok // CHUNK)
    def _(i):
        at = pl.ds(pl.multiple_of(i * CHUNK, CHUNK), CHUNK)
        preact = mine_ref[at, :].astype(F32) + theirs_ref[at, :].astype(F32) + bias_ref[...]
        hidden = gelu_value(preact)[0].astype(BF16).astype(F32)
        inv = lax.rsqrt(jnp.mean(hidden * hidden, -1, keepdims=True) + EPSILON)
        normed_ref[at, :] = (hidden * inv * gain_ref[...]).astype(BF16)

    own = normed_ref[pl.ds(pl.multiple_of(wide_ref[0] * half, CHUNK), half), :]
    for j in range(features // width):
        message_ref[j * half : (j + 1) * half, :] = own[:, j * width : (j + 1) * width]
    message_ref[features // width * half :, :] = grad_ref[...]
    for c in copies:
        c.wait()


def norm(wide, mine, theirs, bias, gain, weights, grad):
    tok, features = mine.shape
    width = weights[0].shape[1]
    rows = features // width * (tok // 2) + tok
    return pl.pallas_call(
        norm_kernel,
        out_shape=[
            jax.ShapeDtypeStruct((tok, features), BF16),
            jax.ShapeDtypeStruct((rows, width), BF16),
        ]
        + [pltpu.VMEM(w.shape, BF16) for w in weights],
        in_specs=[SMEM] + [spec()] * 4 + [in_hbm()] * 3 + [spec()],
        out_specs=[spec()] * 5,
        scratch_shapes=[pltpu.SemaphoreType.DMA((3,))],
        compiler_params=params(),
        cost_estimate=cost(30 * tok * features, 6 * tok * features),
        name="norm",
    )(wide, mine, theirs, bias, gain, *[far(w) for w in weights], grad)


def project(value, place_ref, weights, qkv_ref, slice_ref, proj_ref=None):
    features, width = weights[0].shape
    count = slice_ref.shape[1]
    start = place_ref[0] * count
    slice_ref[...] = dot(value, pick((features, count), lambda r, c: r == c + start)).astype(BF16)
    for i, w in enumerate(weights):
        proj = dot(value, w[...])
        if proj_ref is not None and i < 2:
            proj_ref[:, i * width : (i + 1) * width] = proj
        if i < 2:
            proj = proj * head_scale(proj)
        qkv_ref[:, i * width : (i + 1) * width] = proj.astype(BF16)


def own_kernel(place_ref, normed_ref, grad_ref, wq_ref, wk_ref, wv_ref, qkv_ref, slice_ref, proj_ref):
    qkv_ref[:, 3 * wq_ref.shape[1] :] = grad_ref[...]
    project(normed_ref[...], place_ref, (wq_ref, wk_ref, wv_ref), qkv_ref, slice_ref, proj_ref)


def own_project(place, normed, grad, wq, wk, wv, count):
    rows, features = normed.shape
    width = wq.shape[1]
    return pl.pallas_call(
        own_kernel,
        out_shape=[
            jax.ShapeDtypeStruct((rows, 4 * width), BF16),
            jax.ShapeDtypeStruct((rows, count), BF16),
            jax.ShapeDtypeStruct((rows, 2 * width), F32),
        ],
        in_specs=[SMEM] + [spec()] * 5,
        out_specs=[spec()] * 3,
        compiler_params=params(),
        cost_estimate=cost(6 * rows * features * width, 6 * features * width),
        name="own_project",
    )(place, normed, grad, wq, wk, wv)


def others_kernel(count, half, place_ref, wide_ref, *refs):
    mine, theirs = refs[:count], refs[count : 2 * count]
    wq_ref, wk_ref, wv_ref, qkv_ref, slice_ref, lhs = refs[2 * count :]
    width = wq_ref.shape[1]
    for b in range(count):
        for ref, core in ((mine[b], wide_ref[0]), (theirs[b], 1 - wide_ref[0])):
            row = pl.ds(pl.multiple_of(b * 2 * half + core * half, CHUNK), half)
            for j in range(wq_ref.shape[0] // width):
                lhs[row, j * width : (j + 1) * width] = ref[j * half : (j + 1) * half, :]
        base = b * 2 * half
        qkv_ref[base : base + 2 * half, 3 * width :] = mine[b][mine[b].shape[0] - 2 * half :, :]
    project(lhs[...], place_ref, (wq_ref, wk_ref, wv_ref), qkv_ref, slice_ref)


def others_project(place, wide, mine, theirs, wq, wk, wv, count, half):
    features, width = wq.shape
    rows = len(mine) * 2 * half
    return pl.pallas_call(
        functools.partial(others_kernel, len(mine), half),
        out_shape=[
            jax.ShapeDtypeStruct((rows, 4 * width), BF16),
            jax.ShapeDtypeStruct((rows, count), BF16),
        ],
        in_specs=[SMEM] * 2 + [spec()] * (2 * len(mine) + 3),
        out_specs=[spec()] * 2,
        scratch_shapes=[pltpu.VMEM((rows, features), BF16)],
        compiler_params=params(),
        cost_estimate=cost(6 * rows * features * width, 6 * features * width),
        name="others_project",
    )(place, wide, *mine, *theirs, wq, wk, wv)


def attention_kernel(tok, tile, heads, qkv_rows, *refs):
    groups = len(qkv_rows)
    width = heads * DH
    total = sum(qkv_rows)
    qkv_in = refs[:groups]
    proj_ref, wq, wk, wv, wo, both_ref, dv_ref = refs[groups : groups + 7]
    qkv, dv_acc, dk_acc, dq_acc, att, sems = refs[groups + 7 :]
    loads = []
    at = 0
    for i, rows in enumerate(qkv_rows):
        loads.append(pltpu.make_async_copy(qkv_in[i], qkv.at[pl.ds(at, rows)], sems.at[len(loads)]))
        at += rows
    for c in loads:
        c.start()
    for c in loads:
        c.wait()

    scale = SCORE_GAIN / math.sqrt(DH)
    lanes = min(128, tile)

    def block(start, first, h):
        here = pl.ds(start, tile)
        cols = slice(h * DH, (h + 1) * DH)
        key = qkv[:, width + h * DH : width + (h + 1) * DH]
        val = qkv[:, 2 * width + h * DH : 2 * width + (h + 1) * DH]
        query = qkv[here, cols]
        up = qkv[here, 3 * width + h * DH : 3 * width + (h + 1) * DH]
        expo = jnp.exp(dot_rt(key, query) * scale)
        back = dot_rt(val, up)
        inv = 1.0 / jnp.sum(expo, 0, keepdims=True)
        delta = jnp.sum(expo * back, 0, keepdims=True) * inv
        prob_b = (expo * inv).astype(BF16)
        score_own = (expo[:tok] * inv * (back[:tok] - delta) * scale).astype(BF16)
        if first:
            dv_acc[:, cols] = dot(prob_b, up)
            dk_acc[:, cols] = dot(score_own, query)
        else:
            dv_acc[:, cols] += dot(prob_b, up)
            dk_acc[:, cols] += dot(score_own, query)

        def own():
            att[:, cols] = dot_lt(prob_b[:, :lanes], val)[:tok].astype(BF16)
            score = expo[:, :lanes] * inv[:, :lanes] * (back[:, :lanes] - delta[:, :lanes]) * scale
            dq_acc[:, cols] = dot_lt(score.astype(BF16), key)[:tok]

        if first:
            own()
        elif first is None:
            pl.when(start == 0)(own)

    if total <= 2048:
        for step in range(total // tile):
            for h in range(heads):
                block(step * tile, step == 0, h)
    else:
        dv_acc[...] = jnp.zeros_like(dv_acc)
        dk_acc[...] = jnp.zeros_like(dk_acc)
        for h in range(heads):

            @pl.loop(0, total // tile)
            def _(step):
                block(pl.multiple_of(step * tile, tile), None, h)

    dv_ref[...] = dv_acc[...].astype(BF16)
    both_ref[:tok, :] = dot(att[...], wo[...]).astype(BF16)
    backs = []
    for acc, lo in ((dq_acc, 0), (dk_acc, width)):
        proj = proj_ref[:, lo : lo + width]
        inv = head_scale(proj)
        normal = proj * inv
        up = acc[...].astype(BF16).astype(F32)
        backs.append((inv * (up - normal * head_mean(up * normal))).astype(BF16))
    norm_back = dot_rt(backs[0], wq[...]) + dot_rt(backs[1], wk[...]) + dot_rt(dv_ref[:tok, :], wv[...])
    both_ref[tok:, :] = norm_back.astype(BF16)


def attention(qkvs, proj, wq, wk, wv, wo, tok):
    qkv_rows = tuple(a.shape[0] for a in qkvs)
    total = sum(qkv_rows)
    features, width = wq.shape
    heads = width // DH
    tile = 256 if total <= 2048 else 128
    return pl.pallas_call(
        functools.partial(attention_kernel, tok, tile, heads, qkv_rows),
        out_shape=[
            jax.ShapeDtypeStruct((2 * tok, features), BF16),
            jax.ShapeDtypeStruct((total, width), BF16),
        ],
        in_specs=[anywhere()] * len(qkvs) + [spec()] * 5,
        out_specs=[spec()] * 2,
        scratch_shapes=[
            pltpu.VMEM((total, 4 * width), BF16),
            pltpu.VMEM((total, width), F32),
            pltpu.VMEM((tok, width), F32),
            pltpu.VMEM((tok, width), F32),
            pltpu.VMEM((tok, width), BF16),
            pltpu.SemaphoreType.DMA((len(qkvs),)),
        ],
        compiler_params=params(24 if total <= 2048 else 56),
        cost_estimate=cost(6 * total * total * width, 8 * total * width),
        name="attention",
    )(*qkvs, proj, wq, wk, wv, wo)


def finish_kernel(mine_ref, theirs_ref, bias_ref, gain_ref, cot_ref, here_ref, there_ref, *refs):
    taps_any, out_ref, pre_ref, edge_ref, taps_ref, sem = refs
    tok = out_ref.shape[0]
    copy = pltpu.make_async_copy(taps_any, taps_ref, sem)
    copy.start()

    @pl.loop(0, tok // CHUNK)
    def _(i):
        at = pl.ds(pl.multiple_of(i * CHUNK, CHUNK), CHUNK)
        low = pl.ds(pl.multiple_of(tok + i * CHUNK, CHUNK), CHUNK)
        preact = mine_ref[at, :].astype(F32) + theirs_ref[at, :].astype(F32) + bias_ref[...]
        active, tangent = gelu_value(preact)
        slope = 0.5 * (1.0 + tangent) + 0.5 * preact * (1.0 - tangent * tangent) * GELU_ROOT * (
            1.0 + 3.0 * GELU_CUBIC * preact * preact
        )
        hidden = active.astype(BF16).astype(F32)
        inv = lax.rsqrt(jnp.mean(hidden * hidden, -1, keepdims=True) + EPSILON)
        attended = here_ref[at, :].astype(F32) + there_ref[at, :].astype(F32)
        out_ref[at, :] = (hidden + attended).astype(BF16)
        gain_back = (here_ref[low, :].astype(F32) + there_ref[low, :].astype(F32)) * gain_ref[...]
        mean = jnp.mean(gain_back * hidden, -1, keepdims=True)
        back = cot_ref[at, :].astype(F32) + inv * (gain_back - hidden * (inv * inv * mean))
        pre_ref[at, :] = (back * slope).astype(BF16)

    edge_ref[0:1, :] = pre_ref[tok - 1 : tok, :]
    edge_ref[1:2, :] = pre_ref[0:1, :]
    copy.wait()


def finish(mine, theirs, bias, gain, cot, here, there, taps):
    tok, features = cot.shape
    row = jax.ShapeDtypeStruct((2, features), BF16)
    full = jax.ShapeDtypeStruct((tok, features), BF16)
    return pl.pallas_call(
        finish_kernel,
        out_shape=[full, full, row, pltpu.VMEM(taps.shape, BF16)],
        in_specs=[spec()] * 7 + [in_hbm()],
        out_specs=[spec()] * 4,
        scratch_shapes=[pltpu.SemaphoreType.DMA],
        compiler_params=params(16),
        cost_estimate=cost(40 * tok * features, 12 * tok * features),
        name="finish",
    )(mine, theirs, bias, gain, cot, here, there, far(taps))


def back_mid_kernel(pre_ref, weight_ref, out_ref):
    channels = weight_ref.shape[1]
    pre = pre_ref[...]
    out_ref[:, :channels] = dot_rt(pre, weight_ref[2])
    out_ref[:, channels:] = dot_rt(pre, weight_ref[3])


def back_mid(pre, weight):
    tok, features = pre.shape
    channels = weight.shape[1]
    return pl.pallas_call(
        back_mid_kernel,
        out_shape=jax.ShapeDtypeStruct((tok, 2 * channels), F32),
        in_specs=[spec()] * 2,
        out_specs=spec(),
        compiler_params=params(),
        cost_estimate=cost(4 * tok * channels * features, 4 * channels * features),
        name="back_mid",
    )(pre, weight)


def back_rest_kernel(place_ref, pre_ref, mid_ref, first_ref, second_ref, weight_ref, out_ref):
    tok, channels = pre_ref.shape[0], weight_ref.shape[1]
    pre = pre_ref[...]
    side = sided(place_ref, first_ref, second_ref, 1)
    after = jnp.concatenate([pre[1:], side[1:2]], 0)
    before = jnp.concatenate([side[0:1], pre[:-1]], 0)
    first = mid_ref[:, :channels] + dot_rt(after, weight_ref[0]) + dot_rt(before, weight_ref[4])
    second = mid_ref[:, channels:] + dot_rt(after, weight_ref[1])
    even = pick((2 * tok, tok), lambda r, c: r == 2 * c)
    odd = pick((2 * tok, tok), lambda r, c: r == 2 * c + 1)
    out_ref[...] = (dot(even, first.astype(BF16)) + dot(odd, second.astype(BF16))).astype(BF16)


def back_rest(place, pre, mid, first, second, weight):
    tok, features = pre.shape
    channels = weight.shape[1]
    return pl.pallas_call(
        back_rest_kernel,
        out_shape=jax.ShapeDtypeStruct((2 * tok, channels), BF16),
        in_specs=[SMEM] + [spec()] * 5,
        out_specs=spec(),
        compiler_params=params(),
        cost_estimate=cost(6 * tok * channels * features, 6 * channels * features),
        name="back_rest",
    )(place, pre, mid, first, second, weight)


def value_kernel(rows_of, scale, dv_ref, *refs):
    slices, out_ref = refs[:-1], refs[-1]
    total, at = None, 0
    for ref, rows in zip(slices, rows_of):
        term = dot_lt(ref[...], dv_ref[at : at + rows, :])
        total = term if total is None else total + term
        at += rows
    out_ref[...] = total * scale


def value_gradient(dv, slices, scale):
    rows_of = tuple(a.shape[0] for a in slices)
    return pl.pallas_call(
        functools.partial(value_kernel, rows_of, scale),
        out_shape=jax.ShapeDtypeStruct((slices[0].shape[1], dv.shape[1]), F32),
        in_specs=[spec()] * (1 + len(slices)),
        out_specs=spec(),
        compiler_params=params(),
        cost_estimate=cost(2 * dv.shape[0] * dv.shape[1] * 192, 2 * dv.size),
        name="value_gradient",
    )(dv, *slices)


def on_device(
    fine_input,
    conv_weight,
    conv_bias,
    norm_gain,
    query_weight,
    key_weight,
    value_weight,
    out_weight,
    cotangent,
):
    samples, fine_rows, channels = fine_input.shape
    tok = fine_rows // 2
    taps, _, features = conv_weight.shape
    n = lax.axis_size("seq")
    grad_scale = 1.0 / math.sqrt(samples * tok * n)
    near = [(i, i ^ 1) for i in range(n)]
    across = [(i, i + 1) for i in range(1, n - 1, 2)] + [(i + 1, i) for i in range(1, n - 1, 2)]
    cycle = list(range(0, n, 2)) + list(range(n - 1, 0, -2))
    ahead = [(cycle[i], cycle[(i + 1) % n]) for i in range(n)]
    behind = [(j, i) for i, j in ahead]
    swap = [(0, 1), (1, 0)]
    place = lax.axis_index("seq").astype(jnp.int32).reshape(1)
    wide = lax.axis_index("wide").astype(jnp.int32).reshape(1)
    bias, gain = conv_bias.reshape(1, features), norm_gain.reshape(1, features)
    fine, cot = fine_input[0], cotangent[0]
    count, core_rows = features // n, tok // 2
    weights = (query_weight, key_weight, value_weight)

    fine_here, edge = edges(fine)
    edge_near, edge_across = lax.ppermute(edge, "seq", near), lax.ppermute(edge, "seq", across)
    att_grad = early(cot, out_weight)
    mine = conv_partial(place, fine_here, edge_near, edge_across, conv_weight)
    theirs = lax.ppermute(mine, "wide", swap)
    normed, message, *weights = norm(wide, mine, theirs, bias, gain, weights, att_grad)
    weights = [near_core(w) for w in weights]

    qkvs, slices = [], []
    cw = ccw = message
    ready = proj = None
    for k in range(1, n // 2 + 1):
        if k > 1:
            cw, ccw, qkvs[-1] = lax.optimization_barrier((cw, ccw, qkvs[-1]))
        if k < n // 2:
            cw, ccw = lax.ppermute(cw, "seq", ahead), lax.ppermute(ccw, "seq", behind)
            blocks = [cw, ccw]
        else:
            blocks = [lax.ppermute(cw, "seq", ahead)]
        sisters = [lax.ppermute(a, "wide", swap) for a in blocks]
        if k == 1:
            qkv, piece, proj = own_project(place, normed, att_grad, *weights, count)
        else:
            qkv, piece = others_project(place, wide, *ready, *weights, count, core_rows)
        qkvs.append(qkv)
        slices.append(piece)
        ready = (blocks, sisters)
    qkv, piece = others_project(place, wide, *ready, *weights, count, core_rows)
    qkvs.append(qkv)
    slices.append(piece)

    both, dv = attention(qkvs, proj, *weights, out_weight, tok)
    there = lax.ppermute(both, "wide", swap)
    value_grad = value_gradient(dv, slices, grad_scale)
    section_out, pre_back, edge, taps_here = finish(
        mine, theirs, bias, gain, cot, both, there, conv_weight
    )
    edge_near, edge_across = lax.ppermute(edge, "seq", near), lax.ppermute(edge, "seq", across)
    taps_here = near_core(taps_here)
    mid = back_mid(pre_back, taps_here)
    input_grad = back_rest(place, pre_back, mid, edge_near, edge_across, taps_here)
    return (section_out[None], input_grad[None], value_grad.T)


def solution(mesh):
    in_specs = (
        P("groups", "seq", "wide"),
        P(None, "wide", None),
        P(),
        P(),
        P(None, "wide"),
        P(None, "wide"),
        P(None, "wide"),
        P("wide", None),
        P("groups", "seq", None),
    )
    out_specs = (P("groups", "seq", None), P("groups", "seq", "wide"), P(("groups", "wide"), "seq"))
    return jax.shard_map(
        on_device, mesh=mesh, in_specs=in_specs, out_specs=out_specs, check_vma=False
    )
```

time: 116 us -> 73.4 us (0.63)
  the two profiles are of different devices: /device:TPU:0 before, /device:TPU:4 now
where the time goes in v2:
time: 73.4 us; the launch traced here: 72.2 us
  Pallas kernels  26.6 us (36%)
  waiting for transfers between devices  26.6 us (36%)
  starting transfers between devices  17.9 us (24%)
  between operations  0.84 us (1%)
    ppermute x6, waiting for transfers between devices, on_device(): cw, ccw = (lax.ppermute(cw, 'seq', ahead), lax.ppermute(ccw, 'seq', behind))  15.1 us
    ppermute x2, starting transfers between devices, on_device(): lax.ppermute(edge, 'seq', across)  8.08 us
    ppermute x6, starting transfers between devices, on_device(): cw, ccw = (lax.ppermute(cw, 'seq', ahead), lax.ppermute(ccw, 'seq', behind))  6.18 us
    pallas_call x1, Pallas kernels, attention(): pl.pallas_call(functools.partial(attention_kernel, tok, tile, heads, qkv_...  5.38 us
    pallas_call x4, Pallas kernels, others_project(): pl.pallas_call(functools.partial(others_kernel, len(mine), half), out_sha...  4.7 us
    ppermute x1, waiting for transfers between devices, on_device(): blocks = [lax.ppermute(cw, 'seq', ahead)]  4.5 us
    ppermute x2, waiting for transfers between devices, on_device(): lax.ppermute(edge, 'seq', across)  3.74 us
    pallas_call x1, Pallas kernels, conv_partial(): pl.pallas_call(functools.partial(conv_kernel, tuple(range(taps))), out_sh...  3.4 us
  transfers between devices with their start and end apart: 20, of which 13 were waited for; matrix products, arithmetic and copies ran while one was open for 0% of the time, Pallas kernels for 12%

profile of v2, /device:TPU:4, one launch (start us, length us, event | category | flops | bytes accessed | tf_op | source)
XLA Modules:
  0.0 72.2 jit_solution(3095084478410980315)
XLA Ops:
  0.6 0.9 %edges.1 = (bf16[192,384]{1,0:T(8,128)(2,1)S(1)}, bf16[3,384]{1,0:T(4,128)(2,1)S(1)}) custom-call(bf16[192,384]{1,0:T(8,128)(2,1)} %bitcast.11), custom_call_target="tpu_custom_call" | custom-call | flops 73728 | bytes 147456 | tf_op jit(solution)/shard_map/edges/pallas_call | solution.py:80
  1.6 3.4 %collective-permute-start.1 = (bf16[3,384]{1,0:T(4,128)(2,1)S(1)}, bf16[3,384]{1,0:T(4,128)(2,1)S(1)}, u32[]{:S(2)}, u32[]{:S(2)}) collective-permute-start(bf16[3,384]{1,0:T(4,128)(2,1)S(1)} %get-tuple-element.36), channel_id=1, source_target_pairs={{2,4},{6,8},{10,12},{4,2},{8,6},{12,10},{3,5},{7,9},{11,13},{5,3},... | collective-permute-start | bytes 6920 | tf_op jit(solution)/shard_map/ppermute | solution.py:565
  5.0 0.1 collective-permute-start
  5.1 2.9 %collective-permute-done.1.second_ref = bf16[3,384]{1,0:T(4,128)(2,1)S(1)} collective-permute-done((bf16[3,384]{1,0:T(4,128)(2,1)S(1)}, bf16[3,384]{1,0:T(4,128)(2,1)S(1)}, u32[]{:S(2)}, u32[]{:S(2)}) %collective-permute-start.1) | collective-permute-done | bytes 2336 | tf_op jit(solution)/shard_map/ppermute | solution.py:565
  8.0 0.7 collective-permute-done.first_ref
  8.7 0.0 copy-start.2
  8.7 0.0 copy-start.3
  8.7 3.4 %conv_partial.1.mine_ref = bf16[96,1536]{1,0:T(8,128)(2,1)S(1)} custom-call(s32[1]{0:T(128)} %bitcast.place_ref, bf16[192,384]{1,0:T(8,128)(2,1)S(1)} %get-tuple-element.35.fine_ref, bf16[3,384]{1,0:T(4,128)(2,1)S(1)} %collective-permute-done.first_ref, bf16[3,384]{1,0:T(4,128)(2,1)S(1)} %collective-permute-done.1.second_ref, bf16[5,384,1536]{2,1,0:T(8,128)(2,1)} %refs_0_.3), custom_call_target="tpu_custom_call" | custom-call | flops 566231040 | bytes 5898240 | tf_op jit(solution)/shard_map/conv_partial/pallas_call | solution.py:161
  12.1 0.1 collective-permute-start.2
  12.2 0.0 copy-done.2
  12.2 0.0 copy-done.3
  12.2 1.9 %early.1.refs_3_.grad_ref = bf16[96,384]{1,0:T(8,128)(2,1)S(1)} custom-call(bf16[96,1536]{1,0:T(8,128)(2,1)} %bitcast.7, bf16[384,1536]{1,0:T(8,128)(2,1)} %refs_9_.1), custom_call_target="tpu_custom_call" | custom-call | flops 113246208 | bytes 1179648 | tf_op jit(solution)/shard_map/early/pallas_call | solution.py:117
  14.1 0.0 collective-permute-done.2.theirs_ref
  14.1 2.0 %norm.1 = (bf16[96,1536]{1,0:T(8,128)(2,1)S(1)}, bf16[288,384]{1,0:T(8,128)(2,1)S(1)}, bf16[1536,384]{1,0:T(8,128)(2,1)S(1)}, bf16[1536,384]{1,0:T(8,128)(2,1)S(1)}, bf16[1536,384]{1,0:T(8,128)(2,1)S(1)}) custom-call(s32[1]{0:T(128)} %bitcast.3.wide_ref, bf16[96,1536]{1,0:T(8,128)(2,1)S(1)} %conv_partial.1.mine_ref, ...), custom_call_target="tpu_custom_call" | custom-call | flops 4423680 | bytes 884736 | tf_op jit(solution)/shard_map/norm/pallas_call | solution.py:230
  16.1 1.6 %collective-permute-start.4 = (bf16[288,384]{1,0:T(8,128)(2,1)S(1)}, bf16[288,384]{1,0:T(8,128)(2,1)S(1)}, u32[]{:S(2)}, u32[]{:S(2)}) collective-permute-start(bf16[288,384]{1,0:T(8,128)(2,1)S(1)} %get-tuple-element.37), channel_id=1, source_target_pairs={{4,0},{8,4},{12,8},{14,12},{10,14},{6,10},{2,6},{0,2},{5,1},{9,5},... | collective-permute-start | bytes 663560 | tf_op jit(solution)/shard_map/ppermute | solution.py:579
  17.8 0.4 collective-permute-start.3
  18.2 0.9 %own_project.1 = (bf16[96,1536]{1,0:T(8,128)(2,1)S(1)}, bf16[96,192]{1,0:T(8,128)(2,1)S(1)}, f32[96,768]{1,0:T(8,128)S(1)}) custom-call(s32[1]{0:T(128)} %bitcast.place_ref, bf16[96,1536]{1,0:T(8,128)(2,1)S(1)} %get-tuple-element.38.normed_ref, bf16[96,384]{1,0:T(8,128)(2,1)S(1)} %early.1.refs_3_.grad_ref, ...), custom_call_target="tpu_custom_call" | custom-call | flops 339738624 | bytes 3538944 | tf_op jit(solution)/shard_map/own_project/pallas_call | solution.py:268
  19.1 4.9 %collective-permute-done.4.refs_1_ = bf16[288,384]{1,0:T(8,128)(2,1)S(1)} collective-permute-done((bf16[288,384]{1,0:T(8,128)(2,1)S(1)}, bf16[288,384]{1,0:T(8,128)(2,1)S(1)}, u32[]{:S(2)}, u32[]{:S(2)}) %collective-permute-start.4) | collective-permute-done | bytes 221216 | tf_op jit(solution)/shard_map/ppermute | solution.py:579
  24.0 1.3 %collective-permute-done.3.refs_0_ = bf16[288,384]{1,0:T(8,128)(2,1)S(1)} collective-permute-done((bf16[288,384]{1,0:T(8,128)(2,1)S(1)}, bf16[288,384]{1,0:T(8,128)(2,1)S(1)}, u32[]{:S(2)}, u32[]{:S(2)}) %collective-permute-start.3) | collective-permute-done | bytes 221216 | tf_op jit(solution)/shard_map/ppermute | solution.py:579
  25.3 0.4 collective-permute-start.5
  25.8 1.6 %collective-permute-start.6 = (bf16[288,384]{1,0:T(8,128)(2,1)S(1)}, bf16[288,384]{1,0:T(8,128)(2,1)S(1)}, u32[]{:S(2)}, u32[]{:S(2)}) collective-permute-start(bf16[288,384]{1,0:T(8,128)(2,1)S(1)} %collective-permute-done.4.refs_1_), channel_id=1, source_target_pairs={{4,0},{8,4},{12,8},{14,12},{10,14},{6,10},{2,6},{0,2},{5,1},{9,5},... | collective-permute-start | bytes 663560 | tf_op jit(solution)/shard_map/ppermute | solution.py:579
  27.3 0.0 collective-permute-start.8
  27.3 0.5 collective-permute-start.7
  27.8 4.2 %collective-permute-done.5.refs_0_ = bf16[288,384]{1,0:T(8,128)(2,1)S(1)} collective-permute-done((bf16[288,384]{1,0:T(8,128)(2,1)S(1)}, bf16[288,384]{1,0:T(8,128)(2,1)S(1)}, u32[]{:S(2)}, u32[]{:S(2)}) %collective-permute-start.5) | collective-permute-done | bytes 221216 | tf_op jit(solution)/shard_map/ppermute | solution.py:579
  32.0 0.0 collective-permute-start.11
  32.0 0.2 collective-permute-done.6.refs_1_
  32.2 0.3 collective-permute-start.12
  32.5 0.0 collective-permute-done.8.refs_3_
  32.5 0.0 collective-permute-done.7.refs_2_
  32.5 1.3 %others_project.4 = (bf16[192,1536]{1,0:T(8,128)(2,1)S(1)}, bf16[192,192]{1,0:T(8,128)(2,1)S(1)}) custom-call(s32[1]{0:T(128)} %bitcast.place_ref, s32[1]{0:T(128)} %bitcast.3.wide_ref, bf16[288,384]{1,0:T(8,128)(2,1)S(1)} %collective-permute-done.3.refs_0_, bf16[288,384]{1,0:T(8,128)(2,1)S(1)} %collective-permute-done.4.refs_1_, ...), custom_call_target="tpu_custom_call" | custom-call | flops 679477248 | bytes 3538944 | tf_op jit(solution)/shard_map/others_project/pallas_call | solution.py:300
  33.8 0.5 collective-permute-start.9
  34.3 1.6 %collective-permute-start.10 = (bf16[288,384]{1,0:T(8,128)(2,1)S(1)}, bf16[288,384]{1,0:T(8,128)(2,1)S(1)}, u32[]{:S(2)}, u32[]{:S(2)}) collective-permute-start(bf16[288,384]{1,0:T(8,128)(2,1)S(1)} %collective-permute-done.6.refs_1_), channel_id=1, source_target_pairs={{4,0},{8,4},{12,8},{14,12},{10,14},{6,10},{2,6},{0,2},{5,1},{9,5},... | collective-permute-start | bytes 663560 | tf_op jit(solution)/shard_map/ppermute | solution.py:579
  35.9 0.0 collective-permute-done.11.refs_2_
  35.9 0.0 collective-permute-done.12.refs_3_
  35.9 1.3 %others_project.5 = (bf16[192,1536]{1,0:T(8,128)(2,1)S(1)}, bf16[192,192]{1,0:T(8,128)(2,1)S(1)}) custom-call(s32[1]{0:T(128)} %bitcast.place_ref, s32[1]{0:T(128)} %bitcast.3.wide_ref, bf16[288,384]{1,0:T(8,128)(2,1)S(1)} %collective-permute-done.5.refs_0_, bf16[288,384]{1,0:T(8,128)(2,1)S(1)} %collective-permute-done.6.refs_1_, ...), custom_call_target="tpu_custom_call" | custom-call | flops 679477248 | bytes 3538944 | tf_op jit(solution)/shard_map/others_project/pallas_call | solution.py:300
  37.2 4.2 %collective-permute-done.9.refs_0_ = bf16[288,384]{1,0:T(8,128)(2,1)S(1)} collective-permute-done((bf16[288,384]{1,0:T(8,128)(2,1)S(1)}, bf16[288,384]{1,0:T(8,128)(2,1)S(1)}, u32[]{:S(2)}, u32[]{:S(2)}) %collective-permute-start.9) | collective-permute-done | bytes 221216 | tf_op jit(solution)/shard_map/ppermute | solution.py:579
  41.4 0.3 collective-permute-done.10.refs_1_
  41.7 1.5 %collective-permute-start.15 = (bf16[288,384]{1,0:T(8,128)(2,1)S(1)}, bf16[288,384]{1,0:T(8,128)(2,1)S(1)}, u32[]{:S(2)}, u32[]{:S(2)}) collective-permute-start(bf16[288,384]{1,0:T(8,128)(2,1)S(1)} %collective-permute-done.9.refs_0_), channel_id=1, source_target_pairs={{0,4},{4,8},{8,12},{12,14},{14,10},{10,6},{6,2},{2,0},{1,5},{5,9},... | collective-permute-start | bytes 663560 | tf_op jit(solution)/shard_map/ppermute | solution.py:582
  43.2 0.0 collective-permute-start.13
  43.2 0.5 collective-permute-start.14
  43.7 4.5 %collective-permute-done.15.refs_0_ = bf16[288,384]{1,0:T(8,128)(2,1)S(1)} collective-permute-done((bf16[288,384]{1,0:T(8,128)(2,1)S(1)}, bf16[288,384]{1,0:T(8,128)(2,1)S(1)}, u32[]{:S(2)}, u32[]{:S(2)}) %collective-permute-start.15) | collective-permute-done | bytes 221216 | tf_op jit(solution)/shard_map/ppermute | solution.py:582
  48.2 0.0 collective-permute-start.16
  48.2 0.0 collective-permute-done.13.refs_2_
  48.2 0.0 collective-permute-done.14.refs_3_
  48.3 1.3 %others_project.6 = (bf16[192,1536]{1,0:T(8,128)(2,1)S(1)}, bf16[192,192]{1,0:T(8,128)(2,1)S(1)}) custom-call(s32[1]{0:T(128)} %bitcast.place_ref, s32[1]{0:T(128)} %bitcast.3.wide_ref, bf16[288,384]{1,0:T(8,128)(2,1)S(1)} %collective-permute-done.9.refs_0_, bf16[288,384]{1,0:T(8,128)(2,1)S(1)} %collective-permute-done.10.refs_1_, ...), custom_call_target="tpu_custom_call" | custom-call | flops 679477248 | bytes 3538944 | tf_op jit(solution)/shard_map/others_project/pallas_call | solution.py:300
  49.5 0.0 copy-start
  49.6 0.2 collective-permute-done.16.refs_1_
  49.7 0.8 %others_project.7 = (bf16[96,1536]{1,0:T(8,128)(2,1)S(1)}, bf16[96,192]{1,0:T(8,128)(2,1)S(1)}) custom-call(s32[1]{0:T(128)} %bitcast.place_ref, s32[1]{0:T(128)} %bitcast.3.wide_ref, bf16[288,384]{1,0:T(8,128)(2,1)S(1)} %collective-permute-done.15.refs_0_, bf16[288,384]{1,0:T(8,128)(2,1)S(1)} %collective-permute-done.16.refs_1_, ...), custom_call_target="tpu_custom_call" | custom-call | flops 339738624 | bytes 3538944 | tf_op jit(solution)/shard_map/others_project/pallas_call | solution.py:300
  50.6 0.2 copy-done
  50.8 5.4 %attention.1 = (bf16[192,1536]{1,0:T(8,128)(2,1)S(1)}, bf16[768,384]{1,0:T(8,128)(2,1)S(1)}) custom-call(bf16[96,1536]{1,0:T(8,128)(2,1)S(1)} %get-tuple-element.43.refs_0_, bf16[192,1536]{1,0:T(8,128)(2,1)S(1)} %get-tuple-element.47.refs_1_, bf16[192,1536]{1,0:T(8,128)(2,1)S(1)} %get-tuple-element.51.refs_2_, ...), custom_call_target="tpu_custom_call" | custom-call | flops 1358954496 | bytes 2359296 | tf_op jit(solution)/shard_map/attention/pallas_call | solution.py:397
  56.2 0.0 copy-start.1
  56.2 0.6 collective-permute-start.17
  56.8 1.1 %value_gradient.1 = f32[192,384]{1,0:T(8,128)} custom-call(bf16[768,384]{1,0:T(8,128)(2,1)S(1)} %get-tuple-element.61.dv_ref, bf16[96,192]{1,0:T(8,128)(2,1)S(1)} %get-tuple-element.62.refs_0_, bf16[192,192]{1,0:T(8,128)(2,1)S(1)} %get-tuple-element.63.refs_1_, bf16[192,192]{1,0:T(8,128)(2,1)S(1)} %get-tuple-element.64.refs_2_, ...), custom_call_target="tpu_custom_call" | custom-call | flops 113246208 | bytes 589824 | tf_op jit(solution)/shard_map/value_gradient/pallas_call | solution.py:524
  57.9 0.5 collective-permute-done.17.there_ref
  58.4 0.0 copy-done.1
  58.4 3.4 %finish.1 = (bf16[96,1536]{1,0:T(8,128)(2,1)}, bf16[96,1536]{1,0:T(8,128)(2,1)S(1)}, bf16[2,1536]{1,0:T(2,128)(2,1)S(1)}, bf16[5,384,1536]{2,1,0:T(8,128)(2,1)S(1)}) custom-call(bf16[96,1536]{1,0:T(8,128)(2,1)S(1)} %conv_partial.1.mine_ref, bf16[96,1536]{1,0:T(8,128)(2,1)S(1)} %collective-permute-done.2.theirs_ref, f32[1,1536]{1,0:T(1,128)S(1)} %reshape.19.bias_ref, ...), custom_call_target="tpu_custom_call" | custom-call | flops 5898240 | bytes 1769472 | tf_op jit(solution)/shard_map/finish/pallas_call | solution.py:452
  61.8 4.7 %collective-permute-start.19 = (bf16[2,1536]{1,0:T(2,128)(2,1)S(1)}, bf16[2,1536]{1,0:T(2,128)(2,1)S(1)}, u32[]{:S(2)}, u32[]{:S(2)}) collective-permute-start(bf16[2,1536]{1,0:T(2,128)(2,1)S(1)} %get-tuple-element.60), channel_id=1, source_target_pairs={{2,4},{6,8},{10,12},{4,2},{8,6},{12,10},{3,5},{7,9},{11,13},{5,3},... | collective-permute-start | bytes 18440 | tf_op jit(solution)/shard_map/ppermute | solution.py:601
  66.5 0.1 collective-permute-start.18
  66.6 0.8 %back_mid.1.mid_ref = f32[96,768]{1,0:T(8,128)S(1)} custom-call(bf16[96,1536]{1,0:T(8,128)(2,1)S(1)} %get-tuple-element.58.pre_ref, bf16[5,384,1536]{2,1,0:T(8,128)(2,1)S(1)} %get-tuple-element.59.weight_ref), custom_call_target="tpu_custom_call" | custom-call | flops 226492416 | bytes 2359296 | tf_op jit(solution)/shard_map/back_mid/pallas_call | solution.py:474
  67.4 0.9 %collective-permute-done.19.second_ref = bf16[2,1536]{1,0:T(2,128)(2,1)S(1)} collective-permute-done((bf16[2,1536]{1,0:T(2,128)(2,1)S(1)}, bf16[2,1536]{1,0:T(2,128)(2,1)S(1)}, u32[]{:S(2)}, u32[]{:S(2)}) %collective-permute-start.19) | collective-permute-done | bytes 6176 | tf_op jit(solution)/shard_map/ppermute | solution.py:601
  68.3 1.9 %collective-permute-done.18.first_ref = bf16[2,1536]{1,0:T(2,128)(2,1)S(1)} collective-permute-done((bf16[2,1536]{1,0:T(2,128)(2,1)S(1)}, bf16[2,1536]{1,0:T(2,128)(2,1)S(1)}, u32[]{:S(2)}, u32[]{:S(2)}) %collective-permute-start.18) | collective-permute-done | bytes 6176 | tf_op jit(solution)/shard_map/ppermute | solution.py:601
  70.2 2.0 %back_rest.1 = bf16[192,384]{1,0:T(8,128)(2,1)} custom-call(s32[1]{0:T(128)} %bitcast.place_ref, bf16[96,1536]{1,0:T(8,128)(2,1)S(1)} %get-tuple-element.58.pre_ref, f32[96,768]{1,0:T(8,128)S(1)} %back_mid.1.mid_ref, bf16[2,1536]{1,0:T(2,128)(2,1)S(1)} %collective-permute-done.18.first_ref, bf16[2,1536]{1,0:T(2,128)(2,1)S(1)} %collective-permute-done.19.second_ref, ...), custom_call_target="tpu_custom_call" | custom-call | flops 339738624 | bytes 3538944 | tf_op jit(solution)/shard_map/back_rest/pallas_call | solution.py:501
  (2 shorter events, 0.0 us)
Async XLA Ops:
  1.6 6.4 %collective-permute-start.1 = (bf16[3,384]{1,0:T(4,128)(2,1)S(1)}, bf16[3,384]{1,0:T(4,128)(2,1)S(1)}, u32[]{:S(2)}, u32[]{:S(2)}) collective-permute-start(bf16[3,384]{1,0:T(4,128)(2,1)S(1)} %get-tuple-element.36), channel_id=1, source_target_pairs={{2,4},{6,8},{10,12},{4,2},{8,6},{12,10},{3,5},{7,9},{11,13},{5,3},... | collective-permute-start | bytes 6920 | tf_op jit(solution)/shard_map/ppermute | solution.py:565
  5.0 3.7 %collective-permute-start = (bf16[3,384]{1,0:T(4,128)(2,1)S(1)}, bf16[3,384]{1,0:T(4,128)(2,1)S(1)}, u32[]{:S(2)}, u32[]{:S(2)}) collective-permute-start(bf16[3,384]{1,0:T(4,128)(2,1)S(1)} %get-tuple-element.36), channel_id=1, source_target_pairs={{0,2},{2,0},{4,6},{6,4},{8,10},{10,8},{12,14},{14,12},{1,3},{3,1},... | collective-permute-start | bytes 6920 | tf_op jit(solution)/shard_map/ppermute | solution.py:565
  8.7 3.5 %copy-start.2 = (f32[1536]{0:T(1024)S(1)}, f32[1536]{0:T(1024)}, u32[]{:S(2)}) copy-start(f32[1536]{0:T(1024)} %param.11) | copy-start | bytes 18436
  8.7 3.5 %copy-start.3 = (f32[1536]{0:T(1024)S(1)}, f32[1536]{0:T(1024)}, u32[]{:S(2)}) copy-start(f32[1536]{0:T(1024)} %param.12) | copy-start | bytes 18436
  12.1 2.0 %collective-permute-start.2 = (bf16[96,1536]{1,0:T(8,128)(2,1)S(1)}, bf16[96,1536]{1,0:T(8,128)(2,1)S(1)}, u32[]{:S(2)}, u32[]{:S(2)}) collective-permute-start(bf16[96,1536]{1,0:T(8,128)(2,1)S(1)} %conv_partial.1.mine_ref), channel_id=1, source_target_pairs={{0,1},{1,0},{2,3},{3,2},{4,5},{5,4},{6,7},{7,6},{8,9},{9,8},{10,11... | collective-permute-start | bytes 884744 | tf_op jit(solution)/shard_map/ppermute | solution.py:568
  16.1 7.9 %collective-permute-start.4 = (bf16[288,384]{1,0:T(8,128)(2,1)S(1)}, bf16[288,384]{1,0:T(8,128)(2,1)S(1)}, u32[]{:S(2)}, u32[]{:S(2)}) collective-permute-start(bf16[288,384]{1,0:T(8,128)(2,1)S(1)} %get-tuple-element.37), channel_id=1, source_target_pairs={{4,0},{8,4},{12,8},{14,12},{10,14},{6,10},{2,6},{0,2},{5,1},{9,5},... | collective-permute-start | bytes 663560 | tf_op jit(solution)/shard_map/ppermute | solution.py:579
  17.8 7.5 %collective-permute-start.3 = (bf16[288,384]{1,0:T(8,128)(2,1)S(1)}, bf16[288,384]{1,0:T(8,128)(2,1)S(1)}, u32[]{:S(2)}, u32[]{:S(2)}) collective-permute-start(bf16[288,384]{1,0:T(8,128)(2,1)S(1)} %get-tuple-element.37), channel_id=1, source_target_pairs={{0,4},{4,8},{8,12},{12,14},{14,10},{10,6},{6,2},{2,0},{1,5},{5,9},... | collective-permute-start | bytes 663560 | tf_op jit(solution)/shard_map/ppermute | solution.py:579
  25.3 6.7 %collective-permute-start.5 = (bf16[288,384]{1,0:T(8,128)(2,1)S(1)}, bf16[288,384]{1,0:T(8,128)(2,1)S(1)}, u32[]{:S(2)}, u32[]{:S(2)}) collective-permute-start(bf16[288,384]{1,0:T(8,128)(2,1)S(1)} %collective-permute-done.3.refs_0_), channel_id=1, source_target_pairs={{0,4},{4,8},{8,12},{12,14},{14,10},{10,6},{6,2},{2,0},{1,5},{5,9},... | collective-permute-start | bytes 663560 | tf_op jit(solution)/shard_map/ppermute | solution.py:579
  25.8 6.4 %collective-permute-start.6 = (bf16[288,384]{1,0:T(8,128)(2,1)S(1)}, bf16[288,384]{1,0:T(8,128)(2,1)S(1)}, u32[]{:S(2)}, u32[]{:S(2)}) collective-permute-start(bf16[288,384]{1,0:T(8,128)(2,1)S(1)} %collective-permute-done.4.refs_1_), channel_id=1, source_target_pairs={{4,0},{8,4},{12,8},{14,12},{10,14},{6,10},{2,6},{0,2},{5,1},{9,5},... | collective-permute-start | bytes 663560 | tf_op jit(solution)/shard_map/ppermute | solution.py:579
  27.3 5.2 %collective-permute-start.8 = (bf16[288,384]{1,0:T(8,128)(2,1)S(1)}, bf16[288,384]{1,0:T(8,128)(2,1)S(1)}, u32[]{:S(2)}, u32[]{:S(2)}) collective-permute-start(bf16[288,384]{1,0:T(8,128)(2,1)S(1)} %collective-permute-done.4.refs_1_), channel_id=1, source_target_pairs={{0,1},{1,0},{2,3},{3,2},{4,5},{5,4},{6,7},{7,6},{8,9},{9,8},{10,11... | collective-permute-start | bytes 663560 | tf_op jit(solution)/shard_map/ppermute | solution.py:583
  27.3 5.2 %collective-permute-start.7 = (bf16[288,384]{1,0:T(8,128)(2,1)S(1)}, bf16[288,384]{1,0:T(8,128)(2,1)S(1)}, u32[]{:S(2)}, u32[]{:S(2)}) collective-permute-start(bf16[288,384]{1,0:T(8,128)(2,1)S(1)} %collective-permute-done.3.refs_0_), channel_id=1, source_target_pairs={{0,1},{1,0},{2,3},{3,2},{4,5},{5,4},{6,7},{7,6},{8,9},{9,8},{10,11... | collective-permute-start | bytes 663560 | tf_op jit(solution)/shard_map/ppermute | solution.py:583
  32.0 3.9 %collective-permute-start.11 = (bf16[288,384]{1,0:T(8,128)(2,1)S(1)}, bf16[288,384]{1,0:T(8,128)(2,1)S(1)}, u32[]{:S(2)}, u32[]{:S(2)}) collective-permute-start(bf16[288,384]{1,0:T(8,128)(2,1)S(1)} %collective-permute-done.5.refs_0_), channel_id=1, source_target_pairs={{0,1},{1,0},{2,3},{3,2},{4,5},{5,4},{6,7},{7,6},{8,9},{9,8},{10,11... | collective-permute-start | bytes 663560 | tf_op jit(solution)/shard_map/ppermute | solution.py:583
  32.2 3.7 %collective-permute-start.12 = (bf16[288,384]{1,0:T(8,128)(2,1)S(1)}, bf16[288,384]{1,0:T(8,128)(2,1)S(1)}, u32[]{:S(2)}, u32[]{:S(2)}) collective-permute-start(bf16[288,384]{1,0:T(8,128)(2,1)S(1)} %collective-permute-done.6.refs_1_), channel_id=1, source_target_pairs={{0,1},{1,0},{2,3},{3,2},{4,5},{5,4},{6,7},{7,6},{8,9},{9,8},{10,11... | collective-permute-start | bytes 663560 | tf_op jit(solution)/shard_map/ppermute | solution.py:583
  33.8 7.5 %collective-permute-start.9 = (bf16[288,384]{1,0:T(8,128)(2,1)S(1)}, bf16[288,384]{1,0:T(8,128)(2,1)S(1)}, u32[]{:S(2)}, u32[]{:S(2)}) collective-permute-start(bf16[288,384]{1,0:T(8,128)(2,1)S(1)} %collective-permute-done.5.refs_0_), channel_id=1, source_target_pairs={{0,4},{4,8},{8,12},{12,14},{14,10},{10,6},{6,2},{2,0},{1,5},{5,9},... | collective-permute-start | bytes 663560 | tf_op jit(solution)/shard_map/ppermute | solution.py:579
  34.3 7.4 %collective-permute-start.10 = (bf16[288,384]{1,0:T(8,128)(2,1)S(1)}, bf16[288,384]{1,0:T(8,128)(2,1)S(1)}, u32[]{:S(2)}, u32[]{:S(2)}) collective-permute-start(bf16[288,384]{1,0:T(8,128)(2,1)S(1)} %collective-permute-done.6.refs_1_), channel_id=1, source_target_pairs={{4,0},{8,4},{12,8},{14,12},{10,14},{6,10},{2,6},{0,2},{5,1},{9,5},... | collective-permute-start | bytes 663560 | tf_op jit(solution)/shard_map/ppermute | solution.py:579
  41.7 6.5 %collective-permute-start.15 = (bf16[288,384]{1,0:T(8,128)(2,1)S(1)}, bf16[288,384]{1,0:T(8,128)(2,1)S(1)}, u32[]{:S(2)}, u32[]{:S(2)}) collective-permute-start(bf16[288,384]{1,0:T(8,128)(2,1)S(1)} %collective-permute-done.9.refs_0_), channel_id=1, source_target_pairs={{0,4},{4,8},{8,12},{12,14},{14,10},{10,6},{6,2},{2,0},{1,5},{5,9},... | collective-permute-start | bytes 663560 | tf_op jit(solution)/shard_map/ppermute | solution.py:582
  43.2 5.0 %collective-permute-start.13 = (bf16[288,384]{1,0:T(8,128)(2,1)S(1)}, bf16[288,384]{1,0:T(8,128)(2,1)S(1)}, u32[]{:S(2)}, u32[]{:S(2)}) collective-permute-start(bf16[288,384]{1,0:T(8,128)(2,1)S(1)} %collective-permute-done.9.refs_0_), channel_id=1, source_target_pairs={{0,1},{1,0},{2,3},{3,2},{4,5},{5,4},{6,7},{7,6},{8,9},{9,8},{10,11... | collective-permute-start | bytes 663560 | tf_op jit(solution)/shard_map/ppermute | solution.py:583
  43.2 5.0 %collective-permute-start.14 = (bf16[288,384]{1,0:T(8,128)(2,1)S(1)}, bf16[288,384]{1,0:T(8,128)(2,1)S(1)}, u32[]{:S(2)}, u32[]{:S(2)}) collective-permute-start(bf16[288,384]{1,0:T(8,128)(2,1)S(1)} %collective-permute-done.10.refs_1_), channel_id=1, source_target_pairs={{0,1},{1,0},{2,3},{3,2},{4,5},{5,4},{6,7},{7,6},{8,9},{9,8},{10,11... | collective-permute-start | bytes 663560 | tf_op jit(solution)/shard_map/ppermute | solution.py:583
  48.2 1.5 %collective-permute-start.16 = (bf16[288,384]{1,0:T(8,128)(2,1)S(1)}, bf16[288,384]{1,0:T(8,128)(2,1)S(1)}, u32[]{:S(2)}, u32[]{:S(2)}) collective-permute-start(bf16[288,384]{1,0:T(8,128)(2,1)S(1)} %collective-permute-done.15.refs_0_), channel_id=1, source_target_pairs={{0,1},{1,0},{2,3},{3,2},{4,5},{5,4},{6,7},{7,6},{8,9},{9,8},{10,11... | collective-permute-start | bytes 663560 | tf_op jit(solution)/shard_map/ppermute | solution.py:583
  49.5 1.3 %copy-start = (bf16[384,1536]{1,0:T(8,128)(2,1)S(1)}, bf16[384,1536]{1,0:T(8,128)(2,1)}, u32[]{:S(2)}) copy-start(bf16[384,1536]{1,0:T(8,128)(2,1)} %refs_9_.1) | copy-start | bytes 3538948
  56.2 2.2 %copy-start.1 = (bf16[1,96,1536]{2,1,0:T(8,128)(2,1)S(1)}, bf16[1,96,1536]{2,1,0:T(8,128)(2,1)}, u32[]{:S(2)}) copy-start(bf16[1,96,1536]{2,1,0:T(8,128)(2,1)} %param.17) | copy-start | bytes 884740
  56.2 2.2 %collective-permute-start.17 = (bf16[192,1536]{1,0:T(8,128)(2,1)S(1)}, bf16[192,1536]{1,0:T(8,128)(2,1)S(1)}, u32[]{:S(2)}, u32[]{:S(2)}) collective-permute-start(bf16[192,1536]{1,0:T(8,128)(2,1)S(1)} %get-tuple-element.56.here_ref), channel_id=1, source_target_pairs={{0,1},{1,0},{2,3},{3,2},{4,5},{5,4},{6,7},{7,6},{8,9},{9,8},{10,11... | collective-permute-start | bytes 1769480 | tf_op jit(solution)/shard_map/ppermute | solution.py:596
  61.8 6.4 %collective-permute-start.19 = (bf16[2,1536]{1,0:T(2,128)(2,1)S(1)}, bf16[2,1536]{1,0:T(2,128)(2,1)S(1)}, u32[]{:S(2)}, u32[]{:S(2)}) collective-permute-start(bf16[2,1536]{1,0:T(2,128)(2,1)S(1)} %get-tuple-element.60), channel_id=1, source_target_pairs={{2,4},{6,8},{10,12},{4,2},{8,6},{12,10},{3,5},{7,9},{11,13},{5,3},... | collective-permute-start | bytes 18440 | tf_op jit(solution)/shard_map/ppermute | solution.py:601
  66.5 3.7 %collective-permute-start.18 = (bf16[2,1536]{1,0:T(2,128)(2,1)S(1)}, bf16[2,1536]{1,0:T(2,128)(2,1)S(1)}, u32[]{:S(2)}, u32[]{:S(2)}) collective-permute-start(bf16[2,1536]{1,0:T(2,128)(2,1)S(1)} %get-tuple-element.60), channel_id=1, source_target_pairs={{0,2},{2,0},{4,6},{6,4},{8,10},{10,8},{12,14},{14,12},{1,3},{3,1},... | collective-permute-start | bytes 18440 | tf_op jit(solution)/shard_map/ppermute | solution.py:601

commit v3 on v2

--- a/solution.py
+++ b/solution.py
@@ -130,44 +130,68 @@
     )(far(cot), far(wo))
 
 
-def conv_kernel(order, place_ref, fine_ref, first_ref, second_ref, taps_any, out_ref, taps, sems):
+def conv_kernel(order, fine_ref, taps_any, out_ref, taps, sems):
     fine_rows, channels = fine_ref.shape
     tok = fine_rows // 2
     copies = {k: pltpu.make_async_copy(taps_any.at[k], taps.at[k], sems.at[k]) for k in order}
     for k in order:
         copies[k].start()
-    side = sided(place_ref, first_ref, second_ref, 2)
-    spare_rows = jnp.zeros((HALO_ROWS - side.shape[0], channels), BF16)
-    block = jnp.concatenate([fine_ref[...], side, spare_rows], 0)
+    block = fine_ref[...]
     total = None
     for k in order:
-
-        def test(row, col, k=k):
-            want = 2 * row + k - 2
-            inside = (want >= 0) & (want < fine_rows)
-            spare = jnp.where(want < 0, fine_rows + 2 + want, want + 2)
-            return col == jnp.where(inside, want, spare)
-
-        rows = dot(pick((tok, fine_rows + HALO_ROWS), test), block).astype(BF16)
+        rows = dot(pick((tok, fine_rows), lambda r, c, k=k: c == 2 * r + k - 2), block).astype(BF16)
         copies[k].wait()
         term = dot(rows, taps[k])
         total = term if total is None else total + term
-    out_ref[...] = total.astype(BF16)
-
-
-def conv_partial(place, fine, first, second, weight):
+    out_ref[...] = total
+
+
+def conv_inner(fine, weight):
     taps, channels, features = weight.shape
     tok = fine.shape[0] // 2
     return pl.pallas_call(
         functools.partial(conv_kernel, tuple(range(taps))),
-        out_shape=jax.ShapeDtypeStruct((tok, features), BF16),
-        in_specs=[SMEM] + [spec()] * 3 + [in_hbm()],
+        out_shape=jax.ShapeDtypeStruct((tok, features), F32),
+        in_specs=[spec(), in_hbm()],
         out_specs=spec(),
         scratch_shapes=[pltpu.VMEM(weight.shape, BF16), pltpu.SemaphoreType.DMA((taps,))],
         compiler_params=params(12),
         cost_estimate=cost(2 * tok * weight.size, 2 * weight.size),
-        name="conv_partial",
-    )(place, fine, first, second, far(weight))
+        name="conv_inner",
+    )(fine, far(weight))
+
+
+def conv_edge_kernel(place_ref, inner_ref, first_ref, second_ref, taps_any, out_ref, taps, sems):
+    tok = inner_ref.shape[0]
+    copies = [pltpu.make_async_copy(taps_any.at[k], taps.at[i], sems.at[i]) for i, k in enumerate((0, 1, 4))]
+    for c in copies:
+        c.start()
+    side = sided(place_ref, first_ref, second_ref, 2)
+    blank = jnp.zeros((CHUNK - 1, side.shape[1]), BF16)
+    terms = []
+    for i in range(3):
+        copies[i].wait()
+        terms.append(dot(jnp.concatenate([side[i : i + 1], blank], 0), taps[i])[0:1])
+    row = lax.broadcasted_iota(jnp.int32, (CHUNK, 1), 0)
+    top = inner_ref[:CHUNK, :] + jnp.where(row == 0, terms[0] + terms[1], 0.0)
+    low = inner_ref[tok - CHUNK :, :] + jnp.where(row == CHUNK - 1, terms[2], 0.0)
+    out_ref[:CHUNK, :] = top.astype(BF16)
+    out_ref[CHUNK : tok - CHUNK, :] = inner_ref[CHUNK : tok - CHUNK, :].astype(BF16)
+    out_ref[tok - CHUNK :, :] = low.astype(BF16)
+
+
+def conv_edge(place, inner, first, second, weight):
+    taps, channels, features = weight.shape
+    return pl.pallas_call(
+        conv_edge_kernel,
+        out_shape=jax.ShapeDtypeStruct(inner.shape, BF16),
+        in_specs=[SMEM] + [spec()] * 3 + [in_hbm()],
+        out_specs=spec(),
+        scratch_shapes=[pltpu.VMEM((3, channels, features), BF16), pltpu.SemaphoreType.DMA((3,))],
+        compiler_params=params(8),
+        cost_estimate=cost(96 * channels * features, 6 * channels * features),
+        name="conv_edge",
+    )(place, inner, first, second, far(weight))
 
 
 def gelu_value(preact):
@@ -339,7 +363,7 @@
         val = qkv[:, 2 * width + h * DH : 2 * width + (h + 1) * DH]
         query = qkv[here, cols]
         up = qkv[here, 3 * width + h * DH : 3 * width + (h + 1) * DH]
-        expo = jnp.exp(dot_rt(key, query) * scale)
+        expo = jnp.exp2(dot_rt(key, query) * (scale * math.log2(math.e)))
         back = dot_rt(val, up)
         inv = 1.0 / jnp.sum(expo, 0, keepdims=True)
         delta = jnp.sum(expo * back, 0, keepdims=True) * inv
@@ -416,70 +440,97 @@
     )(*qkvs, proj, wq, wk, wv, wo)
 
 
-def finish_kernel(mine_ref, theirs_ref, bias_ref, gain_ref, cot_ref, here_ref, there_ref, *refs):
+def local_kernel(mine_ref, theirs_ref, bias_ref, hidden_ref, slope_ref):
+    @pl.loop(0, mine_ref.shape[0] // CHUNK)
+    def _(i):
+        at = pl.ds(pl.multiple_of(i * CHUNK, CHUNK), CHUNK)
+        preact = mine_ref[at, :].astype(F32) + theirs_ref[at, :].astype(F32) + bias_ref[...]
+        active, tangent = gelu_value(preact)
+        hidden_ref[at, :] = active.astype(BF16)
+        slope_ref[at, :] = 0.5 * (1.0 + tangent) + 0.5 * preact * (1.0 - tangent * tangent) * GELU_ROOT * (
+            1.0 + 3.0 * GELU_CUBIC * preact * preact
+        )
+
+
+def local_terms(mine, theirs, bias):
+    return pl.pallas_call(
+        local_kernel,
+        out_shape=[jax.ShapeDtypeStruct(mine.shape, BF16), jax.ShapeDtypeStruct(mine.shape, F32)],
+        in_specs=[spec()] * 3,
+        out_specs=[spec()] * 2,
+        compiler_params=params(),
+        cost_estimate=cost(40 * mine.size, 10 * mine.size),
+        name="local_terms",
+    )(mine, theirs, bias)
+
+
+def finish_kernel(hidden_ref, slope_ref, gain_ref, cot_ref, here_ref, there_ref, *refs):
     taps_any, out_ref, pre_ref, edge_ref, taps_ref, sem = refs
     tok = out_ref.shape[0]
-    copy = pltpu.make_async_copy(taps_any, taps_ref, sem)
+    copy = pltpu.make_async_copy(taps_any.at[pl.ds(2, 2)], taps_ref, sem)
     copy.start()
 
     @pl.loop(0, tok // CHUNK)
     def _(i):
         at = pl.ds(pl.multiple_of(i * CHUNK, CHUNK), CHUNK)
         low = pl.ds(pl.multiple_of(tok + i * CHUNK, CHUNK), CHUNK)
-        preact = mine_ref[at, :].astype(F32) + theirs_ref[at, :].astype(F32) + bias_ref[...]
-        active, tangent = gelu_value(preact)
-        slope = 0.5 * (1.0 + tangent) + 0.5 * preact * (1.0 - tangent * tangent) * GELU_ROOT * (
-            1.0 + 3.0 * GELU_CUBIC * preact * preact
-        )
-        hidden = active.astype(BF16).astype(F32)
+        hidden = hidden_ref[at, :].astype(F32)
         inv = lax.rsqrt(jnp.mean(hidden * hidden, -1, keepdims=True) + EPSILON)
-        attended = here_ref[at, :].astype(F32) + there_ref[at, :].astype(F32)
-        out_ref[at, :] = (hidden + attended).astype(BF16)
+        out_ref[at, :] = (hidden + (here_ref[at, :].astype(F32) + there_ref[at, :].astype(F32))).astype(BF16)
         gain_back = (here_ref[low, :].astype(F32) + there_ref[low, :].astype(F32)) * gain_ref[...]
         mean = jnp.mean(gain_back * hidden, -1, keepdims=True)
         back = cot_ref[at, :].astype(F32) + inv * (gain_back - hidden * (inv * inv * mean))
-        pre_ref[at, :] = (back * slope).astype(BF16)
+        pre_ref[at, :] = (back * slope_ref[at, :]).astype(BF16)
 
     edge_ref[0:1, :] = pre_ref[tok - 1 : tok, :]
     edge_ref[1:2, :] = pre_ref[0:1, :]
     copy.wait()
 
 
-def finish(mine, theirs, bias, gain, cot, here, there, taps):
+def finish(hidden, slope, gain, cot, here, there, taps):
     tok, features = cot.shape
     row = jax.ShapeDtypeStruct((2, features), BF16)
     full = jax.ShapeDtypeStruct((tok, features), BF16)
     return pl.pallas_call(
         finish_kernel,
-        out_shape=[full, full, row, pltpu.VMEM(taps.shape, BF16)],
-        in_specs=[spec()] * 7 + [in_hbm()],
+        out_shape=[full, full, row, pltpu.VMEM((2,) + taps.shape[1:], BF16)],
+        in_specs=[spec()] * 6 + [in_hbm()],
         out_specs=[spec()] * 4,
         scratch_shapes=[pltpu.SemaphoreType.DMA],
         compiler_params=params(16),
         cost_estimate=cost(40 * tok * features, 12 * tok * features),
         name="finish",
-    )(mine, theirs, bias, gain, cot, here, there, far(taps))
-
-
-def back_mid_kernel(pre_ref, weight_ref, out_ref):
+    )(hidden, slope, gain, cot, here, there, far(taps))
+
+
+def back_mid_kernel(pre_ref, weight_ref, taps_any, out_ref, taps_ref, sems):
     channels = weight_ref.shape[1]
+    copies = [pltpu.make_async_copy(taps_any.at[k], taps_ref.at[i], sems.at[i]) for i, k in enumerate((0, 1, 4))]
+    for c in copies:
+        c.start()
     pre = pre_ref[...]
-    out_ref[:, :channels] = dot_rt(pre, weight_ref[2])
-    out_ref[:, channels:] = dot_rt(pre, weight_ref[3])
-
-
-def back_mid(pre, weight):
+    out_ref[:, :channels] = dot_rt(pre, weight_ref[0])
+    out_ref[:, channels:] = dot_rt(pre, weight_ref[1])
+    for c in copies:
+        c.wait()
+
+
+def back_mid(pre, weight, taps):
     tok, features = pre.shape
     channels = weight.shape[1]
     return pl.pallas_call(
         back_mid_kernel,
-        out_shape=jax.ShapeDtypeStruct((tok, 2 * channels), F32),
-        in_specs=[spec()] * 2,
-        out_specs=spec(),
-        compiler_params=params(),
-        cost_estimate=cost(4 * tok * channels * features, 4 * channels * features),
+        out_shape=[
+            jax.ShapeDtypeStruct((tok, 2 * channels), F32),
+            pltpu.VMEM((3,) + taps.shape[1:], BF16),
+        ],
+        in_specs=[spec()] * 2 + [in_hbm()],
+        out_specs=[spec()] * 2,
+        scratch_shapes=[pltpu.SemaphoreType.DMA((3,))],
+        compiler_params=params(),
+        cost_estimate=cost(4 * tok * channels * features, 10 * channels * features),
         name="back_mid",
-    )(pre, weight)
+    )(pre, weight, far(taps))
 
 
 def back_rest_kernel(place_ref, pre_ref, mid_ref, first_ref, second_ref, weight_ref, out_ref):
@@ -488,7 +539,7 @@
     side = sided(place_ref, first_ref, second_ref, 1)
     after = jnp.concatenate([pre[1:], side[1:2]], 0)
     before = jnp.concatenate([side[0:1], pre[:-1]], 0)
-    first = mid_ref[:, :channels] + dot_rt(after, weight_ref[0]) + dot_rt(before, weight_ref[4])
+    first = mid_ref[:, :channels] + dot_rt(after, weight_ref[0]) + dot_rt(before, weight_ref[2])
     second = mid_ref[:, channels:] + dot_rt(after, weight_ref[1])
     even = pick((2 * tok, tok), lambda r, c: r == 2 * c)
     odd = pick((2 * tok, tok), lambda r, c: r == 2 * c + 1)
@@ -564,17 +615,25 @@
     fine_here, edge = edges(fine)
     edge_near, edge_across = lax.ppermute(edge, "seq", near), lax.ppermute(edge, "seq", across)
     att_grad = early(cot, out_weight)
-    mine = conv_partial(place, fine_here, edge_near, edge_across, conv_weight)
+    inner = conv_inner(fine_here, conv_weight)
+    mine = conv_edge(place, inner, edge_near, edge_across, conv_weight)
     theirs = lax.ppermute(mine, "wide", swap)
     normed, message, *weights = norm(wide, mine, theirs, bias, gain, weights, att_grad)
     weights = [near_core(w) for w in weights]
 
+    local = local_terms(mine, theirs, bias)
     qkvs, slices = [], []
     cw = ccw = message
     ready = proj = None
     for k in range(1, n // 2 + 1):
-        if k > 1:
-            cw, ccw, qkvs[-1] = lax.optimization_barrier((cw, ccw, qkvs[-1]))
+        if k == 2:
+            cw, ccw, qkvs[0] = lax.optimization_barrier((cw, ccw, qkvs[0]))
+        elif k == 3:
+            cw, ccw, local = lax.optimization_barrier((cw, ccw, local))
+        elif k > 3:
+            cw, ccw, qkvs[k - 3], qkvs[k - 2] = lax.optimization_barrier(
+                (cw, ccw, qkvs[k - 3], qkvs[k - 2])
+            )
         if k < n // 2:
             cw, ccw = lax.ppermute(cw, "seq", ahead), lax.ppermute(ccw, "seq", behind)
             blocks = [cw, ccw]
@@ -596,12 +655,13 @@
     there = lax.ppermute(both, "wide", swap)
     value_grad = value_gradient(dv, slices, grad_scale)
     section_out, pre_back, edge, taps_here = finish(
-        mine, theirs, bias, gain, cot, both, there, conv_weight
+        *local, gain, cot, both, there, conv_weight
     )
     edge_near, edge_across = lax.ppermute(edge, "seq", near), lax.ppermute(edge, "seq", across)
     taps_here = near_core(taps_here)
-    mid = back_mid(pre_back, taps_here)
-    input_grad = back_rest(place, pre_back, mid, edge_near, edge_across, taps_here)
+    mid, taps_side = back_mid(pre_back, taps_here, conv_weight)
+    taps_side = near_core(taps_side)
+    input_grad = back_rest(place, pre_back, mid, edge_near, edge_across, taps_side)
     return (section_out[None], input_grad[None], value_grad.T)
 
 

time: 73.4 us -> 72.8 us (level)
  the two profiles are of different devices: /device:TPU:4 before, /device:TPU:0 now
where the time goes in v3:
time: 72.8 us; the launch traced here: 72.5 us
  Pallas kernels  30 us (41%)
  waiting for transfers between devices  20.7 us (28%)
  starting transfers between devices  20.6 us (28%)
  between operations  0.91 us (1%)
    ppermute x6, waiting for transfers between devices, on_device(): cw, ccw = (lax.ppermute(cw, 'seq', ahead), lax.ppermute(ccw, 'seq', behind))  15.2 us
    ppermute x2, starting transfers between devices, on_device(): lax.ppermute(edge, 'seq', near)  10 us
    ppermute x6, starting transfers between devices, on_device(): cw, ccw = (lax.ppermute(cw, 'seq', ahead), lax.ppermute(ccw, 'seq', behind))  6.18 us
    pallas_call x1, Pallas kernels, attention(): pl.pallas_call(functools.partial(attention_kernel, tok, tile, heads, qkv_...  5.39 us
    ppermute x1, waiting for transfers between devices, on_device(): blocks = [lax.ppermute(cw, 'seq', ahead)]  4.8 us
    pallas_call x4, Pallas kernels, others_project(): pl.pallas_call(functools.partial(others_kernel, len(mine), half), out_sha...  4.69 us
    pallas_call x1, Pallas kernels, conv_inner(): pl.pallas_call(functools.partial(conv_kernel, tuple(range(taps))), out_sh...  3.38 us
    pallas_call x1, Pallas kernels, back_mid(): pl.pallas_call(back_mid_kernel, out_shape=[jax.ShapeDtypeStruct((tok, 2 *...  2.39 us
  transfers between devices with their start and end apart: 20, of which 9 were waited for; matrix products, arithmetic and copies ran while one was open for 0% of the time, Pallas kernels for 19%

profile of v3, /device:TPU:0, one launch (start us, length us, event | category | flops | bytes accessed | tf_op | source)
XLA Modules:
  0.0 72.5 jit_solution(4215460285483289472)
XLA Ops:
  0.6 0.9 %edges.1 = (bf16[192,384]{1,0:T(8,128)(2,1)S(1)}, bf16[3,384]{1,0:T(4,128)(2,1)S(1)}) custom-call(bf16[192,384]{1,0:T(8,128)(2,1)} %bitcast.10), custom_call_target="tpu_custom_call" | custom-call | flops 73728 | bytes 147456 | tf_op jit(solution)/shard_map/edges/pallas_call | solution.py:80
  1.6 0.7 collective-permute-start.1
  2.2 5.8 %collective-permute-start = (bf16[3,384]{1,0:T(4,128)(2,1)S(1)}, bf16[3,384]{1,0:T(4,128)(2,1)S(1)}, u32[]{:S(2)}, u32[]{:S(2)}) collective-permute-start(bf16[3,384]{1,0:T(4,128)(2,1)S(1)} %get-tuple-element.42), channel_id=1, source_target_pairs={{0,2},{2,0},{4,6},{6,4},{8,10},{10,8},{12,14},{14,12},{1,3},{3,1},... | collective-permute-start | bytes 6920 | tf_op jit(solution)/shard_map/ppermute | solution.py:616
  8.0 3.4 %conv_inner.1.inner_ref = f32[96,1536]{1,0:T(8,128)S(1)} custom-call(bf16[192,384]{1,0:T(8,128)(2,1)S(1)} %get-tuple-element.41.fine_ref, bf16[5,384,1536]{2,1,0:T(8,128)(2,1)} %taps_any.5), custom_call_target="tpu_custom_call" | custom-call | flops 566231040 | bytes 5898240 | tf_op jit(solution)/shard_map/conv_inner/pallas_call | solution.py:152
  11.4 0.0 collective-permute-done.1.second_ref
  11.4 0.0 collective-permute-done.first_ref
  11.4 0.0 copy-start.2
  11.5 0.0 copy-start.3
  11.5 2.3 %conv_edge.1.mine_ref = bf16[96,1536]{1,0:T(8,128)(2,1)S(1)} custom-call(s32[1]{0:T(128)} %bitcast.1.place_ref, f32[96,1536]{1,0:T(8,128)S(1)} %conv_inner.1.inner_ref, bf16[3,384]{1,0:T(4,128)(2,1)S(1)} %collective-permute-done.first_ref, bf16[3,384]{1,0:T(4,128)(2,1)S(1)} %collective-permute-done.1.second_ref, bf16[5,384,1536]{2,1,0:T(8,128)(2,1)} %taps_any.5), custom_call_target="tpu_custom_call" | custom-call | flops 56623104 | bytes 3538944 | tf_op jit(solution)/shard_map/conv_edge/pallas_call | solution.py:185
  13.8 0.1 collective-permute-start.2
  13.9 0.0 copy-done.2
  13.9 0.0 copy-done.3
  13.9 1.9 %early.1.refs_3_.grad_ref = bf16[96,384]{1,0:T(8,128)(2,1)S(1)} custom-call(bf16[96,1536]{1,0:T(8,128)(2,1)} %bitcast.7, bf16[384,1536]{1,0:T(8,128)(2,1)} %refs_9_.1), custom_call_target="tpu_custom_call" | custom-call | flops 113246208 | bytes 1179648 | tf_op jit(solution)/shard_map/early/pallas_call | solution.py:117
  15.8 0.0 collective-permute-done.2.theirs_ref
  15.8 2.0 %norm.1 = (bf16[96,1536]{1,0:T(8,128)(2,1)S(1)}, bf16[288,384]{1,0:T(8,128)(2,1)S(1)}, bf16[1536,384]{1,0:T(8,128)(2,1)S(1)}, bf16[1536,384]{1,0:T(8,128)(2,1)S(1)}, bf16[1536,384]{1,0:T(8,128)(2,1)S(1)}) custom-call(s32[1]{0:T(128)} %bitcast.wide_ref, bf16[96,1536]{1,0:T(8,128)(2,1)S(1)} %conv_edge.1.mine_ref, ...), custom_call_target="tpu_custom_call" | custom-call | flops 4423680 | bytes 884736 | tf_op jit(solution)/shard_map/norm/pallas_call | solution.py:254
  17.9 0.2 collective-permute-start.4
  18.1 1.8 %collective-permute-start.3 = (bf16[288,384]{1,0:T(8,128)(2,1)S(1)}, bf16[288,384]{1,0:T(8,128)(2,1)S(1)}, u32[]{:S(2)}, u32[]{:S(2)}) collective-permute-start(bf16[288,384]{1,0:T(8,128)(2,1)S(1)} %get-tuple-element.43), channel_id=1, source_target_pairs={{0,4},{4,8},{8,12},{12,14},{14,10},{10,6},{6,2},{2,0},{1,5},{5,9},... | collective-permute-start | bytes 663560 | tf_op jit(solution)/shard_map/ppermute | solution.py:638
  19.9 0.9 %own_project.1 = (bf16[96,1536]{1,0:T(8,128)(2,1)S(1)}, bf16[96,192]{1,0:T(8,128)(2,1)S(1)}, f32[96,768]{1,0:T(8,128)S(1)}) custom-call(s32[1]{0:T(128)} %bitcast.1.place_ref, bf16[96,1536]{1,0:T(8,128)(2,1)S(1)} %get-tuple-element.44.normed_ref, bf16[96,384]{1,0:T(8,128)(2,1)S(1)} %early.1.refs_3_.grad_ref, ...), custom_call_target="tpu_custom_call" | custom-call | flops 339738624 | bytes 3538944 | tf_op jit(solution)/shard_map/own_project/pallas_call | solution.py:292
  20.8 4.9 %collective-permute-done.4.refs_1_ = bf16[288,384]{1,0:T(8,128)(2,1)S(1)} collective-permute-done((bf16[288,384]{1,0:T(8,128)(2,1)S(1)}, bf16[288,384]{1,0:T(8,128)(2,1)S(1)}, u32[]{:S(2)}, u32[]{:S(2)}) %collective-permute-start.4) | collective-permute-done | bytes 221216 | tf_op jit(solution)/shard_map/ppermute | solution.py:638
  25.7 0.1 collective-permute-done.3.refs_0_
  25.8 1.7 %collective-permute-start.5 = (bf16[288,384]{1,0:T(8,128)(2,1)S(1)}, bf16[288,384]{1,0:T(8,128)(2,1)S(1)}, u32[]{:S(2)}, u32[]{:S(2)}) collective-permute-start(bf16[288,384]{1,0:T(8,128)(2,1)S(1)} %collective-permute-done.3.refs_0_), channel_id=1, source_target_pairs={{0,4},{4,8},{8,12},{12,14},{14,10},{10,6},{6,2},{2,0},{1,5},{5,9},... | collective-permute-start | bytes 663560 | tf_op jit(solution)/shard_map/ppermute | solution.py:638
  27.5 0.3 collective-permute-start.6
  27.8 0.0 collective-permute-start.10
  27.8 0.5 collective-permute-start.9
  28.3 4.4 %collective-permute-done.5.refs_0_ = bf16[288,384]{1,0:T(8,128)(2,1)S(1)} collective-permute-done((bf16[288,384]{1,0:T(8,128)(2,1)S(1)}, bf16[288,384]{1,0:T(8,128)(2,1)S(1)}, u32[]{:S(2)}, u32[]{:S(2)}) %collective-permute-start.5) | collective-permute-done | bytes 221216 | tf_op jit(solution)/shard_map/ppermute | solution.py:638
  32.8 0.0 collective-permute-start.11
  32.8 1.3 %collective-permute-done.6.refs_1_ = bf16[288,384]{1,0:T(8,128)(2,1)S(1)} collective-permute-done((bf16[288,384]{1,0:T(8,128)(2,1)S(1)}, bf16[288,384]{1,0:T(8,128)(2,1)S(1)}, u32[]{:S(2)}, u32[]{:S(2)}) %collective-permute-start.6) | collective-permute-done | bytes 221216 | tf_op jit(solution)/shard_map/ppermute | solution.py:638
  34.1 0.0 collective-permute-start.12
  34.1 0.5 local_terms.1
  34.6 1.6 %collective-permute-start.7 = (bf16[288,384]{1,0:T(8,128)(2,1)S(1)}, bf16[288,384]{1,0:T(8,128)(2,1)S(1)}, u32[]{:S(2)}, u32[]{:S(2)}) collective-permute-start(bf16[288,384]{1,0:T(8,128)(2,1)S(1)} %collective-permute-done.5.refs_0_), channel_id=1, source_target_pairs={{0,4},{4,8},{8,12},{12,14},{14,10},{10,6},{6,2},{2,0},{1,5},{5,9},... | collective-permute-start | bytes 663560 | tf_op jit(solution)/shard_map/ppermute | solution.py:638
  36.2 0.0 collective-permute-done.10.refs_3_
  36.2 0.4 collective-permute-start.8
  36.7 0.0 collective-permute-done.9.refs_2_
  36.7 1.3 %others_project.4 = (bf16[192,1536]{1,0:T(8,128)(2,1)S(1)}, bf16[192,192]{1,0:T(8,128)(2,1)S(1)}) custom-call(s32[1]{0:T(128)} %bitcast.1.place_ref, s32[1]{0:T(128)} %bitcast.wide_ref, bf16[288,384]{1,0:T(8,128)(2,1)S(1)} %collective-permute-done.3.refs_0_, bf16[288,384]{1,0:T(8,128)(2,1)S(1)} %collective-permute-done.4.refs_1_, ...), custom_call_target="tpu_custom_call" | custom-call | flops 679477248 | bytes 3538944 | tf_op jit(solution)/shard_map/others_project/pallas_call | solution.py:324
  38.0 0.0 collective-permute-done.11.refs_2_
  38.0 0.0 collective-permute-done.12.refs_3_
  38.0 1.3 %others_project.5 = (bf16[192,1536]{1,0:T(8,128)(2,1)S(1)}, bf16[192,192]{1,0:T(8,128)(2,1)S(1)}) custom-call(s32[1]{0:T(128)} %bitcast.1.place_ref, s32[1]{0:T(128)} %bitcast.wide_ref, bf16[288,384]{1,0:T(8,128)(2,1)S(1)} %collective-permute-done.5.refs_0_, bf16[288,384]{1,0:T(8,128)(2,1)S(1)} %collective-permute-done.6.refs_1_, ...), custom_call_target="tpu_custom_call" | custom-call | flops 679477248 | bytes 3538944 | tf_op jit(solution)/shard_map/others_project/pallas_call | solution.py:324
  39.3 3.2 %collective-permute-done.7.refs_0_ = bf16[288,384]{1,0:T(8,128)(2,1)S(1)} collective-permute-done((bf16[288,384]{1,0:T(8,128)(2,1)S(1)}, bf16[288,384]{1,0:T(8,128)(2,1)S(1)}, u32[]{:S(2)}, u32[]{:S(2)}) %collective-permute-start.7) | collective-permute-done | bytes 221216 | tf_op jit(solution)/shard_map/ppermute | solution.py:638
  42.5 1.3 %collective-permute-done.8.refs_1_ = bf16[288,384]{1,0:T(8,128)(2,1)S(1)} collective-permute-done((bf16[288,384]{1,0:T(8,128)(2,1)S(1)}, bf16[288,384]{1,0:T(8,128)(2,1)S(1)}, u32[]{:S(2)}, u32[]{:S(2)}) %collective-permute-start.8) | collective-permute-done | bytes 221216 | tf_op jit(solution)/shard_map/ppermute | solution.py:638
  43.8 1.4 %collective-permute-start.15 = (bf16[288,384]{1,0:T(8,128)(2,1)S(1)}, bf16[288,384]{1,0:T(8,128)(2,1)S(1)}, u32[]{:S(2)}, u32[]{:S(2)}) collective-permute-start(bf16[288,384]{1,0:T(8,128)(2,1)S(1)} %collective-permute-done.7.refs_0_), channel_id=1, source_target_pairs={{0,4},{4,8},{8,12},{12,14},{14,10},{10,6},{6,2},{2,0},{1,5},{5,9},... | collective-permute-start | bytes 663560 | tf_op jit(solution)/shard_map/ppermute | solution.py:641
  45.2 0.0 collective-permute-start.13
  45.2 0.5 collective-permute-start.14
  45.7 4.8 %collective-permute-done.15.refs_0_ = bf16[288,384]{1,0:T(8,128)(2,1)S(1)} collective-permute-done((bf16[288,384]{1,0:T(8,128)(2,1)S(1)}, bf16[288,384]{1,0:T(8,128)(2,1)S(1)}, u32[]{:S(2)}, u32[]{:S(2)}) %collective-permute-start.15) | collective-permute-done | bytes 221216 | tf_op jit(solution)/shard_map/ppermute | solution.py:641
  50.5 0.0 collective-permute-start.16
  50.5 0.0 collective-permute-done.13.refs_2_
  50.5 0.0 collective-permute-done.14.refs_3_
  50.5 1.3 %others_project.6 = (bf16[192,1536]{1,0:T(8,128)(2,1)S(1)}, bf16[192,192]{1,0:T(8,128)(2,1)S(1)}) custom-call(s32[1]{0:T(128)} %bitcast.1.place_ref, s32[1]{0:T(128)} %bitcast.wide_ref, bf16[288,384]{1,0:T(8,128)(2,1)S(1)} %collective-permute-done.7.refs_0_, bf16[288,384]{1,0:T(8,128)(2,1)S(1)} %collective-permute-done.8.refs_1_, ...), custom_call_target="tpu_custom_call" | custom-call | flops 679477248 | bytes 3538944 | tf_op jit(solution)/shard_map/others_project/pallas_call | solution.py:324
  51.8 0.0 copy-start
  51.8 0.2 collective-permute-done.16.refs_1_
  52.0 0.8 %others_project.7 = (bf16[96,1536]{1,0:T(8,128)(2,1)S(1)}, bf16[96,192]{1,0:T(8,128)(2,1)S(1)}) custom-call(s32[1]{0:T(128)} %bitcast.1.place_ref, s32[1]{0:T(128)} %bitcast.wide_ref, bf16[288,384]{1,0:T(8,128)(2,1)S(1)} %collective-permute-done.15.refs_0_, bf16[288,384]{1,0:T(8,128)(2,1)S(1)} %collective-permute-done.16.refs_1_, ...), custom_call_target="tpu_custom_call" | custom-call | flops 339738624 | bytes 3538944 | tf_op jit(solution)/shard_map/others_project/pallas_call | solution.py:324
  52.9 0.3 copy-done
  53.1 5.4 %attention.1 = (bf16[192,1536]{1,0:T(8,128)(2,1)S(1)}, bf16[768,384]{1,0:T(8,128)(2,1)S(1)}) custom-call(bf16[96,1536]{1,0:T(8,128)(2,1)S(1)} %get-tuple-element.55.refs_0_, bf16[192,1536]{1,0:T(8,128)(2,1)S(1)} %get-tuple-element.60.refs_1_, bf16[192,1536]{1,0:T(8,128)(2,1)S(1)} %get-tuple-element.61.refs_2_, ...), custom_call_target="tpu_custom_call" | custom-call | flops 1358954496 | bytes 2359296 | tf_op jit(solution)/shard_map/attention/pallas_call | solution.py:421
  58.5 0.0 copy-start.1
  58.5 0.6 collective-permute-start.17
  59.1 1.1 %value_gradient.1 = f32[192,384]{1,0:T(8,128)} custom-call(bf16[768,384]{1,0:T(8,128)(2,1)S(1)} %get-tuple-element.73.dv_ref, bf16[96,192]{1,0:T(8,128)(2,1)S(1)} %get-tuple-element.74.refs_0_, bf16[192,192]{1,0:T(8,128)(2,1)S(1)} %get-tuple-element.75.refs_1_, bf16[192,192]{1,0:T(8,128)(2,1)S(1)} %get-tuple-element.76.refs_2_, ...), custom_call_target="tpu_custom_call" | custom-call | flops 113246208 | bytes 589824 | tf_op jit(solution)/shard_map/value_gradient/pallas_call | solution.py:575
  60.2 0.5 collective-permute-done.17.there_ref
  60.7 0.0 copy-done.1
  60.7 2.4 %finish.1 = (bf16[96,1536]{1,0:T(8,128)(2,1)}, bf16[96,1536]{1,0:T(8,128)(2,1)S(1)}, bf16[2,1536]{1,0:T(2,128)(2,1)S(1)}, bf16[2,384,1536]{2,1,0:T(8,128)(2,1)S(1)}) custom-call(bf16[96,1536]{1,0:T(8,128)(2,1)S(1)} %get-tuple-element.53.hidden_ref, f32[96,1536]{1,0:T(8,128)S(1)} %get-tuple-element.54.slope_ref, f32[1,1536]{1,0:T(1,128)S(1)} %reshape.21.gain_ref, ...), custom_call_target="tpu_custom_call" | custom-call | flops 5898240 | bytes 1769472 | tf_op jit(solution)/shard_map/finish/pallas_call | solution.py:494
  63.1 0.7 collective-permute-start.19
  63.8 4.2 %collective-permute-start.18 = (bf16[2,1536]{1,0:T(2,128)(2,1)S(1)}, bf16[2,1536]{1,0:T(2,128)(2,1)S(1)}, u32[]{:S(2)}, u32[]{:S(2)}) collective-permute-start(bf16[2,1536]{1,0:T(2,128)(2,1)S(1)} %get-tuple-element.71), channel_id=1, source_target_pairs={{0,2},{2,0},{4,6},{6,4},{8,10},{10,8},{12,14},{14,12},{1,3},{3,1},... | collective-permute-start | bytes 18440 | tf_op jit(solution)/shard_map/ppermute | solution.py:660
  68.0 2.4 %back_mid.1 = (f32[96,768]{1,0:T(8,128)S(1)}, bf16[3,384,1536]{2,1,0:T(8,128)(2,1)S(1)}) custom-call(bf16[96,1536]{1,0:T(8,128)(2,1)S(1)} %get-tuple-element.68.pre_ref, bf16[2,384,1536]{2,1,0:T(8,128)(2,1)S(1)} %get-tuple-element.69.weight_ref, bf16[5,384,1536]{2,1,0:T(8,128)(2,1)} %taps_any.5), custom_call_target="tpu_custom_call" | custom-call | flops 226492416 | bytes 5898240 | tf_op jit(solution)/shard_map/back_mid/pallas_call | solution.py:521
  70.4 0.0 collective-permute-done.19.second_ref
  70.4 0.0 collective-permute-done.18.first_ref
  70.4 2.0 %back_rest.1 = bf16[192,384]{1,0:T(8,128)(2,1)} custom-call(s32[1]{0:T(128)} %bitcast.1.place_ref, bf16[96,1536]{1,0:T(8,128)(2,1)S(1)} %get-tuple-element.68.pre_ref, f32[96,768]{1,0:T(8,128)S(1)} %get-tuple-element.70.mid_ref, bf16[2,1536]{1,0:T(2,128)(2,1)S(1)} %collective-permute-done.18.first_ref, ...), custom_call_target="tpu_custom_call" | custom-call | flops 339738624 | bytes 3538944 | tf_op jit(solution)/shard_map/back_rest/pallas_call | solution.py:552
  (2 shorter events, 0.0 us)
Async XLA Ops:
  1.6 9.9 %collective-permute-start.1 = (bf16[3,384]{1,0:T(4,128)(2,1)S(1)}, bf16[3,384]{1,0:T(4,128)(2,1)S(1)}, u32[]{:S(2)}, u32[]{:S(2)}) collective-permute-start(bf16[3,384]{1,0:T(4,128)(2,1)S(1)} %get-tuple-element.42), channel_id=1, source_target_pairs={{2,4},{6,8},{10,12},{4,2},{8,6},{12,10},{3,5},{7,9},{11,13},{5,3},... | collective-permute-start | bytes 6920 | tf_op jit(solution)/shard_map/ppermute | solution.py:616
  2.2 9.2 %collective-permute-start = (bf16[3,384]{1,0:T(4,128)(2,1)S(1)}, bf16[3,384]{1,0:T(4,128)(2,1)S(1)}, u32[]{:S(2)}, u32[]{:S(2)}) collective-permute-start(bf16[3,384]{1,0:T(4,128)(2,1)S(1)} %get-tuple-element.42), channel_id=1, source_target_pairs={{0,2},{2,0},{4,6},{6,4},{8,10},{10,8},{12,14},{14,12},{1,3},{3,1},... | collective-permute-start | bytes 6920 | tf_op jit(solution)/shard_map/ppermute | solution.py:616
  11.4 2.4 %copy-start.2 = (f32[1536]{0:T(1024)S(1)}, f32[1536]{0:T(1024)}, u32[]{:S(2)}) copy-start(f32[1536]{0:T(1024)} %param.11) | copy-start | bytes 18436
  11.5 2.4 %copy-start.3 = (f32[1536]{0:T(1024)S(1)}, f32[1536]{0:T(1024)}, u32[]{:S(2)}) copy-start(f32[1536]{0:T(1024)} %param.12) | copy-start | bytes 18436
  13.8 2.0 %collective-permute-start.2 = (bf16[96,1536]{1,0:T(8,128)(2,1)S(1)}, bf16[96,1536]{1,0:T(8,128)(2,1)S(1)}, u32[]{:S(2)}, u32[]{:S(2)}) collective-permute-start(bf16[96,1536]{1,0:T(8,128)(2,1)S(1)} %conv_edge.1.mine_ref), channel_id=1, source_target_pairs={{0,1},{1,0},{2,3},{3,2},{4,5},{5,4},{6,7},{7,6},{8,9},{9,8},{10,11... | collective-permute-start | bytes 884744 | tf_op jit(solution)/shard_map/ppermute | solution.py:620
  17.9 7.9 %collective-permute-start.4 = (bf16[288,384]{1,0:T(8,128)(2,1)S(1)}, bf16[288,384]{1,0:T(8,128)(2,1)S(1)}, u32[]{:S(2)}, u32[]{:S(2)}) collective-permute-start(bf16[288,384]{1,0:T(8,128)(2,1)S(1)} %get-tuple-element.43), channel_id=1, source_target_pairs={{4,0},{8,4},{12,8},{14,12},{10,14},{6,10},{2,6},{0,2},{5,1},{9,5},... | collective-permute-start | bytes 663560 | tf_op jit(solution)/shard_map/ppermute | solution.py:638
  18.1 7.7 %collective-permute-start.3 = (bf16[288,384]{1,0:T(8,128)(2,1)S(1)}, bf16[288,384]{1,0:T(8,128)(2,1)S(1)}, u32[]{:S(2)}, u32[]{:S(2)}) collective-permute-start(bf16[288,384]{1,0:T(8,128)(2,1)S(1)} %get-tuple-element.43), channel_id=1, source_target_pairs={{0,4},{4,8},{8,12},{12,14},{14,10},{10,6},{6,2},{2,0},{1,5},{5,9},... | collective-permute-start | bytes 663560 | tf_op jit(solution)/shard_map/ppermute | solution.py:638
  25.8 7.0 %collective-permute-start.5 = (bf16[288,384]{1,0:T(8,128)(2,1)S(1)}, bf16[288,384]{1,0:T(8,128)(2,1)S(1)}, u32[]{:S(2)}, u32[]{:S(2)}) collective-permute-start(bf16[288,384]{1,0:T(8,128)(2,1)S(1)} %collective-permute-done.3.refs_0_), channel_id=1, source_target_pairs={{0,4},{4,8},{8,12},{12,14},{14,10},{10,6},{6,2},{2,0},{1,5},{5,9},... | collective-permute-start | bytes 663560 | tf_op jit(solution)/shard_map/ppermute | solution.py:638
  27.5 6.6 %collective-permute-start.6 = (bf16[288,384]{1,0:T(8,128)(2,1)S(1)}, bf16[288,384]{1,0:T(8,128)(2,1)S(1)}, u32[]{:S(2)}, u32[]{:S(2)}) collective-permute-start(bf16[288,384]{1,0:T(8,128)(2,1)S(1)} %collective-permute-done.4.refs_1_), channel_id=1, source_target_pairs={{4,0},{8,4},{12,8},{14,12},{10,14},{6,10},{2,6},{0,2},{5,1},{9,5},... | collective-permute-start | bytes 663560 | tf_op jit(solution)/shard_map/ppermute | solution.py:638
  27.8 8.4 %collective-permute-start.10 = (bf16[288,384]{1,0:T(8,128)(2,1)S(1)}, bf16[288,384]{1,0:T(8,128)(2,1)S(1)}, u32[]{:S(2)}, u32[]{:S(2)}) collective-permute-start(bf16[288,384]{1,0:T(8,128)(2,1)S(1)} %collective-permute-done.4.refs_1_), channel_id=1, source_target_pairs={{0,1},{1,0},{2,3},{3,2},{4,5},{5,4},{6,7},{7,6},{8,9},{9,8},{10,11... | collective-permute-start | bytes 663560 | tf_op jit(solution)/shard_map/ppermute | solution.py:642
  27.8 8.9 %collective-permute-start.9 = (bf16[288,384]{1,0:T(8,128)(2,1)S(1)}, bf16[288,384]{1,0:T(8,128)(2,1)S(1)}, u32[]{:S(2)}, u32[]{:S(2)}) collective-permute-start(bf16[288,384]{1,0:T(8,128)(2,1)S(1)} %collective-permute-done.3.refs_0_), channel_id=1, source_target_pairs={{0,1},{1,0},{2,3},{3,2},{4,5},{5,4},{6,7},{7,6},{8,9},{9,8},{10,11... | collective-permute-start | bytes 663560 | tf_op jit(solution)/shard_map/ppermute | solution.py:642
  32.8 5.2 %collective-permute-start.11 = (bf16[288,384]{1,0:T(8,128)(2,1)S(1)}, bf16[288,384]{1,0:T(8,128)(2,1)S(1)}, u32[]{:S(2)}, u32[]{:S(2)}) collective-permute-start(bf16[288,384]{1,0:T(8,128)(2,1)S(1)} %collective-permute-done.5.refs_0_), channel_id=1, source_target_pairs={{0,1},{1,0},{2,3},{3,2},{4,5},{5,4},{6,7},{7,6},{8,9},{9,8},{10,11... | collective-permute-start | bytes 663560 | tf_op jit(solution)/shard_map/ppermute | solution.py:642
  34.1 3.9 %collective-permute-start.12 = (bf16[288,384]{1,0:T(8,128)(2,1)S(1)}, bf16[288,384]{1,0:T(8,128)(2,1)S(1)}, u32[]{:S(2)}, u32[]{:S(2)}) collective-permute-start(bf16[288,384]{1,0:T(8,128)(2,1)S(1)} %collective-permute-done.6.refs_1_), channel_id=1, source_target_pairs={{0,1},{1,0},{2,3},{3,2},{4,5},{5,4},{6,7},{7,6},{8,9},{9,8},{10,11... | collective-permute-start | bytes 663560 | tf_op jit(solution)/shard_map/ppermute | solution.py:642
  34.6 7.9 %collective-permute-start.7 = (bf16[288,384]{1,0:T(8,128)(2,1)S(1)}, bf16[288,384]{1,0:T(8,128)(2,1)S(1)}, u32[]{:S(2)}, u32[]{:S(2)}) collective-permute-start(bf16[288,384]{1,0:T(8,128)(2,1)S(1)} %collective-permute-done.5.refs_0_), channel_id=1, source_target_pairs={{0,4},{4,8},{8,12},{12,14},{14,10},{10,6},{6,2},{2,0},{1,5},{5,9},... | collective-permute-start | bytes 663560 | tf_op jit(solution)/shard_map/ppermute | solution.py:638
  36.2 7.6 %collective-permute-start.8 = (bf16[288,384]{1,0:T(8,128)(2,1)S(1)}, bf16[288,384]{1,0:T(8,128)(2,1)S(1)}, u32[]{:S(2)}, u32[]{:S(2)}) collective-permute-start(bf16[288,384]{1,0:T(8,128)(2,1)S(1)} %collective-permute-done.6.refs_1_), channel_id=1, source_target_pairs={{4,0},{8,4},{12,8},{14,12},{10,14},{6,10},{2,6},{0,2},{5,1},{9,5},... | collective-permute-start | bytes 663560 | tf_op jit(solution)/shard_map/ppermute | solution.py:638
  43.8 6.7 %collective-permute-start.15 = (bf16[288,384]{1,0:T(8,128)(2,1)S(1)}, bf16[288,384]{1,0:T(8,128)(2,1)S(1)}, u32[]{:S(2)}, u32[]{:S(2)}) collective-permute-start(bf16[288,384]{1,0:T(8,128)(2,1)S(1)} %collective-permute-done.7.refs_0_), channel_id=1, source_target_pairs={{0,4},{4,8},{8,12},{12,14},{14,10},{10,6},{6,2},{2,0},{1,5},{5,9},... | collective-permute-start | bytes 663560 | tf_op jit(solution)/shard_map/ppermute | solution.py:641
  45.2 5.3 %collective-permute-start.13 = (bf16[288,384]{1,0:T(8,128)(2,1)S(1)}, bf16[288,384]{1,0:T(8,128)(2,1)S(1)}, u32[]{:S(2)}, u32[]{:S(2)}) collective-permute-start(bf16[288,384]{1,0:T(8,128)(2,1)S(1)} %collective-permute-done.7.refs_0_), channel_id=1, source_target_pairs={{0,1},{1,0},{2,3},{3,2},{4,5},{5,4},{6,7},{7,6},{8,9},{9,8},{10,11... | collective-permute-start | bytes 663560 | tf_op jit(solution)/shard_map/ppermute | solution.py:642
  45.2 5.3 %collective-permute-start.14 = (bf16[288,384]{1,0:T(8,128)(2,1)S(1)}, bf16[288,384]{1,0:T(8,128)(2,1)S(1)}, u32[]{:S(2)}, u32[]{:S(2)}) collective-permute-start(bf16[288,384]{1,0:T(8,128)(2,1)S(1)} %collective-permute-done.8.refs_1_), channel_id=1, source_target_pairs={{0,1},{1,0},{2,3},{3,2},{4,5},{5,4},{6,7},{7,6},{8,9},{9,8},{10,11... | collective-permute-start | bytes 663560 | tf_op jit(solution)/shard_map/ppermute | solution.py:642
  50.5 1.5 %collective-permute-start.16 = (bf16[288,384]{1,0:T(8,128)(2,1)S(1)}, bf16[288,384]{1,0:T(8,128)(2,1)S(1)}, u32[]{:S(2)}, u32[]{:S(2)}) collective-permute-start(bf16[288,384]{1,0:T(8,128)(2,1)S(1)} %collective-permute-done.15.refs_0_), channel_id=1, source_target_pairs={{0,1},{1,0},{2,3},{3,2},{4,5},{5,4},{6,7},{7,6},{8,9},{9,8},{10,11... | collective-permute-start | bytes 663560 | tf_op jit(solution)/shard_map/ppermute | solution.py:642
  51.8 1.3 %copy-start = (bf16[384,1536]{1,0:T(8,128)(2,1)S(1)}, bf16[384,1536]{1,0:T(8,128)(2,1)}, u32[]{:S(2)}) copy-start(bf16[384,1536]{1,0:T(8,128)(2,1)} %refs_9_.1) | copy-start | bytes 3538948
  58.5 2.2 %copy-start.1 = (bf16[1,96,1536]{2,1,0:T(8,128)(2,1)S(1)}, bf16[1,96,1536]{2,1,0:T(8,128)(2,1)}, u32[]{:S(2)}) copy-start(bf16[1,96,1536]{2,1,0:T(8,128)(2,1)} %param.17) | copy-start | bytes 884740
  58.5 2.2 %collective-permute-start.17 = (bf16[192,1536]{1,0:T(8,128)(2,1)S(1)}, bf16[192,1536]{1,0:T(8,128)(2,1)S(1)}, u32[]{:S(2)}, u32[]{:S(2)}) collective-permute-start(bf16[192,1536]{1,0:T(8,128)(2,1)S(1)} %get-tuple-element.66.here_ref), channel_id=1, source_target_pairs={{0,1},{1,0},{2,3},{3,2},{4,5},{5,4},{6,7},{7,6},{8,9},{9,8},{10,11... | collective-permute-start | bytes 1769480 | tf_op jit(solution)/shard_map/ppermute | solution.py:655
  63.1 7.3 %collective-permute-start.19 = (bf16[2,1536]{1,0:T(2,128)(2,1)S(1)}, bf16[2,1536]{1,0:T(2,128)(2,1)S(1)}, u32[]{:S(2)}, u32[]{:S(2)}) collective-permute-start(bf16[2,1536]{1,0:T(2,128)(2,1)S(1)} %get-tuple-element.71), channel_id=1, source_target_pairs={{2,4},{6,8},{10,12},{4,2},{8,6},{12,10},{3,5},{7,9},{11,13},{5,3},... | collective-permute-start | bytes 18440 | tf_op jit(solution)/shard_map/ppermute | solution.py:660
  63.8 6.6 %collective-permute-start.18 = (bf16[2,1536]{1,0:T(2,128)(2,1)S(1)}, bf16[2,1536]{1,0:T(2,128)(2,1)S(1)}, u32[]{:S(2)}, u32[]{:S(2)}) collective-permute-start(bf16[2,1536]{1,0:T(2,128)(2,1)S(1)} %get-tuple-element.71), channel_id=1, source_target_pairs={{0,2},{2,0},{4,6},{6,4},{8,10},{10,8},{12,14},{14,12},{1,3},{3,1},... | collective-permute-start | bytes 18440 | tf_op jit(solution)/shard_map/ppermute | solution.py:660

commit v4 on v3

--- a/solution.py
+++ b/solution.py
@@ -267,11 +267,9 @@
     )(wide, mine, theirs, bias, gain, *[far(w) for w in weights], grad)
 
 
-def project(value, place_ref, weights, qkv_ref, slice_ref, proj_ref=None):
-    features, width = weights[0].shape
-    count = slice_ref.shape[1]
-    start = place_ref[0] * count
-    slice_ref[...] = dot(value, pick((features, count), lambda r, c: r == c + start)).astype(BF16)
+def project(value, chosen, weights, qkv_ref, slice_ref, proj_ref=None):
+    width = weights[0].shape[1]
+    slice_ref[...] = dot(value, chosen).astype(BF16)
     for i, w in enumerate(weights):
         proj = dot(value, w[...])
         if proj_ref is not None and i < 2:
@@ -281,9 +279,12 @@
         qkv_ref[:, i * width : (i + 1) * width] = proj.astype(BF16)
 
 
-def own_kernel(place_ref, normed_ref, grad_ref, wq_ref, wk_ref, wv_ref, qkv_ref, slice_ref, proj_ref):
+def own_kernel(place_ref, normed_ref, grad_ref, wq_ref, wk_ref, wv_ref, qkv_ref, slice_ref, proj_ref, chosen_ref):
+    count = slice_ref.shape[1]
+    start = place_ref[0] * count
+    chosen_ref[...] = pick(chosen_ref.shape, lambda r, c: r == c + start)
     qkv_ref[:, 3 * wq_ref.shape[1] :] = grad_ref[...]
-    project(normed_ref[...], place_ref, (wq_ref, wk_ref, wv_ref), qkv_ref, slice_ref, proj_ref)
+    project(normed_ref[...], chosen_ref[...], (wq_ref, wk_ref, wv_ref), qkv_ref, slice_ref, proj_ref)
 
 
 def own_project(place, normed, grad, wq, wk, wv, count):
@@ -295,16 +296,17 @@
             jax.ShapeDtypeStruct((rows, 4 * width), BF16),
             jax.ShapeDtypeStruct((rows, count), BF16),
             jax.ShapeDtypeStruct((rows, 2 * width), F32),
+            jax.ShapeDtypeStruct((features, count), BF16),
         ],
         in_specs=[SMEM] + [spec()] * 5,
-        out_specs=[spec()] * 3,
+        out_specs=[spec()] * 4,
         compiler_params=params(),
         cost_estimate=cost(6 * rows * features * width, 6 * features * width),
         name="own_project",
     )(place, normed, grad, wq, wk, wv)
 
 
-def others_kernel(count, half, place_ref, wide_ref, *refs):
+def others_kernel(count, half, wide_ref, chosen_ref, *refs):
     mine, theirs = refs[:count], refs[count : 2 * count]
     wq_ref, wk_ref, wv_ref, qkv_ref, slice_ref, lhs = refs[2 * count :]
     width = wq_ref.shape[1]
@@ -315,10 +317,10 @@
                 lhs[row, j * width : (j + 1) * width] = ref[j * half : (j + 1) * half, :]
         base = b * 2 * half
         qkv_ref[base : base + 2 * half, 3 * width :] = mine[b][mine[b].shape[0] - 2 * half :, :]
-    project(lhs[...], place_ref, (wq_ref, wk_ref, wv_ref), qkv_ref, slice_ref)
-
-
-def others_project(place, wide, mine, theirs, wq, wk, wv, count, half):
+    project(lhs[...], chosen_ref[...], (wq_ref, wk_ref, wv_ref), qkv_ref, slice_ref)
+
+
+def others_project(wide, chosen, mine, theirs, wq, wk, wv, count, half):
     features, width = wq.shape
     rows = len(mine) * 2 * half
     return pl.pallas_call(
@@ -327,13 +329,13 @@
             jax.ShapeDtypeStruct((rows, 4 * width), BF16),
             jax.ShapeDtypeStruct((rows, count), BF16),
         ],
-        in_specs=[SMEM] * 2 + [spec()] * (2 * len(mine) + 3),
+        in_specs=[SMEM] + [spec()] * (2 * len(mine) + 4),
         out_specs=[spec()] * 2,
         scratch_shapes=[pltpu.VMEM((rows, features), BF16)],
         compiler_params=params(),
         cost_estimate=cost(6 * rows * features * width, 6 * features * width),
         name="others_project",
-    )(place, wide, *mine, *theirs, wq, wk, wv)
+    )(wide, chosen, *mine, *theirs, wq, wk, wv)
 
 
 def attention_kernel(tok, tile, heads, qkv_rows, *refs):
@@ -343,10 +345,12 @@
     qkv_in = refs[:groups]
     proj_ref, wq, wk, wv, wo, both_ref, dv_ref = refs[groups : groups + 7]
     qkv, dv_acc, dk_acc, dq_acc, att, sems = refs[groups + 7 :]
-    loads = []
-    at = 0
+    at, loads = 0, []
     for i, rows in enumerate(qkv_rows):
-        loads.append(pltpu.make_async_copy(qkv_in[i], qkv.at[pl.ds(at, rows)], sems.at[len(loads)]))
+        if total <= 1024:
+            qkv[at : at + rows, :] = qkv_in[i][...]
+        else:
+            loads.append(pltpu.make_async_copy(qkv_in[i], qkv.at[pl.ds(at, rows)], sems.at[i]))
         at += rows
     for c in loads:
         c.start()
@@ -386,7 +390,7 @@
         elif first is None:
             pl.when(start == 0)(own)
 
-    if total <= 2048:
+    if total <= 1024:
         for step in range(total // tile):
             for h in range(heads):
                 block(step * tile, step == 0, h)
@@ -417,14 +421,14 @@
     total = sum(qkv_rows)
     features, width = wq.shape
     heads = width // DH
-    tile = 256 if total <= 2048 else 128
+    tile = total if total <= 1024 else 128
     return pl.pallas_call(
         functools.partial(attention_kernel, tok, tile, heads, qkv_rows),
         out_shape=[
             jax.ShapeDtypeStruct((2 * tok, features), BF16),
             jax.ShapeDtypeStruct((total, width), BF16),
         ],
-        in_specs=[anywhere()] * len(qkvs) + [spec()] * 5,
+        in_specs=[spec() if total <= 1024 else anywhere()] * len(qkvs) + [spec()] * 5,
         out_specs=[spec()] * 2,
         scratch_shapes=[
             pltpu.VMEM((total, 4 * width), BF16),
@@ -434,7 +438,7 @@
             pltpu.VMEM((tok, width), BF16),
             pltpu.SemaphoreType.DMA((len(qkvs),)),
         ],
-        compiler_params=params(24 if total <= 2048 else 56),
+        compiler_params=params(32 if total <= 1024 else 56),
         cost_estimate=cost(6 * total * total * width, 8 * total * width),
         name="attention",
     )(*qkvs, proj, wq, wk, wv, wo)
@@ -641,13 +645,13 @@
             blocks = [lax.ppermute(cw, "seq", ahead)]
         sisters = [lax.ppermute(a, "wide", swap) for a in blocks]
         if k == 1:
-            qkv, piece, proj = own_project(place, normed, att_grad, *weights, count)
+            qkv, piece, proj, chosen = own_project(place, normed, att_grad, *weights, count)
         else:
-            qkv, piece = others_project(place, wide, *ready, *weights, count, core_rows)
+            qkv, piece = others_project(wide, chosen, *ready, *weights, count, core_rows)
         qkvs.append(qkv)
         slices.append(piece)
         ready = (blocks, sisters)
-    qkv, piece = others_project(place, wide, *ready, *weights, count, core_rows)
+    qkv, piece = others_project(wide, chosen, *ready, *weights, count, core_rows)
     qkvs.append(qkv)
     slices.append(piece)
 

time: 72.8 us -> 70.3 us (0.966)
  the two profiles are of different devices: /device:TPU:0 before, /device:TPU:4 now
where the time goes in v4:
time: 70.3 us; the launch traced here: 70 us
  Pallas kernels  28.9 us (41%)
  waiting for transfers between devices  21.5 us (31%)
  starting transfers between devices  18.4 us (26%)
  between operations  0.91 us (1%)
    ppermute x6, waiting for transfers between devices, on_device(): cw, ccw = (lax.ppermute(cw, 'seq', ahead), lax.ppermute(ccw, 'seq', behind))  14.6 us
    ppermute x2, starting transfers between devices, on_device(): lax.ppermute(edge, 'seq', across)  7.28 us
    ppermute x6, starting transfers between devices, on_device(): cw, ccw = (lax.ppermute(cw, 'seq', ahead), lax.ppermute(ccw, 'seq', behind))  6.17 us
    pallas_call x4, Pallas kernels, others_project(): pl.pallas_call(functools.partial(others_kernel, len(mine), half), out_sha...  4.8 us
    ppermute x1, waiting for transfers between devices, on_device(): blocks = [lax.ppermute(cw, 'seq', ahead)]  4.65 us
    pallas_call x1, Pallas kernels, attention(): pl.pallas_call(functools.partial(attention_kernel, tok, tile, heads, qkv_...  4.14 us
    pallas_call x1, Pallas kernels, conv_inner(): pl.pallas_call(functools.partial(conv_kernel, tuple(range(taps))), out_sh...  3.38 us
    pallas_call x1, Pallas kernels, back_mid(): pl.pallas_call(back_mid_kernel, out_shape=[jax.ShapeDtypeStruct((tok, 2 *...  2.4 us
  transfers between devices with their start and end apart: 20, of which 10 were waited for; matrix products, arithmetic and copies ran while one was open for 0% of the time, Pallas kernels for 20%

profile of v4, /device:TPU:4, one launch (start us, length us, event | category | flops | bytes accessed | tf_op | source)
XLA Modules:
  0.0 70.0 jit_solution(18444691524029647981)
XLA Ops:
  0.6 0.9 %edges.1 = (bf16[192,384]{1,0:T(8,128)(2,1)S(1)}, bf16[3,384]{1,0:T(4,128)(2,1)S(1)}) custom-call(bf16[192,384]{1,0:T(8,128)(2,1)} %bitcast.10), custom_call_target="tpu_custom_call" | custom-call | flops 73728 | bytes 147456 | tf_op jit(solution)/shard_map/edges/pallas_call | solution.py:80
  1.6 0.1 collective-permute-start
  1.6 4.9 %collective-permute-start.1 = (bf16[3,384]{1,0:T(4,128)(2,1)S(1)}, bf16[3,384]{1,0:T(4,128)(2,1)S(1)}, u32[]{:S(2)}, u32[]{:S(2)}) collective-permute-start(bf16[3,384]{1,0:T(4,128)(2,1)S(1)} %get-tuple-element.43), channel_id=1, source_target_pairs={{2,4},{6,8},{10,12},{4,2},{8,6},{12,10},{3,5},{7,9},{11,13},{5,3},... | collective-permute-start | bytes 6920 | tf_op jit(solution)/shard_map/ppermute | solution.py:620
  6.6 3.4 %conv_inner.1.inner_ref = f32[96,1536]{1,0:T(8,128)S(1)} custom-call(bf16[192,384]{1,0:T(8,128)(2,1)S(1)} %get-tuple-element.42.fine_ref, bf16[5,384,1536]{2,1,0:T(8,128)(2,1)} %taps_any.5), custom_call_target="tpu_custom_call" | custom-call | flops 566231040 | bytes 5898240 | tf_op jit(solution)/shard_map/conv_inner/pallas_call | solution.py:152
  10.0 0.0 collective-permute-done.first_ref
  10.0 0.0 collective-permute-done.1.second_ref
  10.0 0.0 copy-start.2
  10.0 0.0 copy-start.3
  10.0 2.3 %conv_edge.1.mine_ref = bf16[96,1536]{1,0:T(8,128)(2,1)S(1)} custom-call(s32[1]{0:T(128)} %bitcast.1.place_ref, f32[96,1536]{1,0:T(8,128)S(1)} %conv_inner.1.inner_ref, bf16[3,384]{1,0:T(4,128)(2,1)S(1)} %collective-permute-done.first_ref, bf16[3,384]{1,0:T(4,128)(2,1)S(1)} %collective-permute-done.1.second_ref, bf16[5,384,1536]{2,1,0:T(8,128)(2,1)} %taps_any.5), custom_call_target="tpu_custom_call" | custom-call | flops 56623104 | bytes 3538944 | tf_op jit(solution)/shard_map/conv_edge/pallas_call | solution.py:185
  12.3 0.1 collective-permute-start.2
  12.4 0.0 copy-done.2
  12.4 0.0 copy-done.3
  12.5 1.9 %early.1.refs_3_.grad_ref = bf16[96,384]{1,0:T(8,128)(2,1)S(1)} custom-call(bf16[96,1536]{1,0:T(8,128)(2,1)} %bitcast.7, bf16[384,1536]{1,0:T(8,128)(2,1)} %refs_9_.1), custom_call_target="tpu_custom_call" | custom-call | flops 113246208 | bytes 1179648 | tf_op jit(solution)/shard_map/early/pallas_call | solution.py:117
  14.4 0.0 collective-permute-done.2.theirs_ref
  14.4 2.0 %norm.1 = (bf16[96,1536]{1,0:T(8,128)(2,1)S(1)}, bf16[288,384]{1,0:T(8,128)(2,1)S(1)}, bf16[1536,384]{1,0:T(8,128)(2,1)S(1)}, bf16[1536,384]{1,0:T(8,128)(2,1)S(1)}, bf16[1536,384]{1,0:T(8,128)(2,1)S(1)}) custom-call(s32[1]{0:T(128)} %bitcast.wide_ref, bf16[96,1536]{1,0:T(8,128)(2,1)S(1)} %conv_edge.1.mine_ref, ...), custom_call_target="tpu_custom_call" | custom-call | flops 4423680 | bytes 884736 | tf_op jit(solution)/shard_map/norm/pallas_call | solution.py:254
  16.4 0.1 collective-permute-start.3
  16.5 2.0 %collective-permute-start.4 = (bf16[288,384]{1,0:T(8,128)(2,1)S(1)}, bf16[288,384]{1,0:T(8,128)(2,1)S(1)}, u32[]{:S(2)}, u32[]{:S(2)}) collective-permute-start(bf16[288,384]{1,0:T(8,128)(2,1)S(1)} %get-tuple-element.44), channel_id=1, source_target_pairs={{4,0},{8,4},{12,8},{14,12},{10,14},{6,10},{2,6},{0,2},{5,1},{9,5},... | collective-permute-start | bytes 663560 | tf_op jit(solution)/shard_map/ppermute | solution.py:642
  18.5 0.9 %own_project.1 = (bf16[96,1536]{1,0:T(8,128)(2,1)S(1)}, bf16[96,192]{1,0:T(8,128)(2,1)S(1)}, f32[96,768]{1,0:T(8,128)S(1)}, bf16[1536,192]{1,0:T(8,128)(2,1)S(1)}) custom-call(s32[1]{0:T(128)} %bitcast.1.place_ref, bf16[96,1536]{1,0:T(8,128)(2,1)S(1)} %get-tuple-element.45.normed_ref, bf16[96,384]{1,0:T(8,128)(2,1)S(1)} %early.1.refs_3_.grad_ref, ...), custom_call_target="tpu_custom_call" | custom-call | flops 339738624 | bytes 3538944 | tf_op jit(solution)/shard_map/own_project/pallas_call | solution.py:293
  19.4 4.9 %collective-permute-done.3.refs_0_ = bf16[288,384]{1,0:T(8,128)(2,1)S(1)} collective-permute-done((bf16[288,384]{1,0:T(8,128)(2,1)S(1)}, bf16[288,384]{1,0:T(8,128)(2,1)S(1)}, u32[]{:S(2)}, u32[]{:S(2)}) %collective-permute-start.3) | collective-permute-done | bytes 221216 | tf_op jit(solution)/shard_map/ppermute | solution.py:642
  24.3 0.1 collective-permute-done.4.refs_1_
  24.3 1.3 %collective-permute-start.5 = (bf16[288,384]{1,0:T(8,128)(2,1)S(1)}, bf16[288,384]{1,0:T(8,128)(2,1)S(1)}, u32[]{:S(2)}, u32[]{:S(2)}) collective-permute-start(bf16[288,384]{1,0:T(8,128)(2,1)S(1)} %collective-permute-done.3.refs_0_), channel_id=1, source_target_pairs={{0,4},{4,8},{8,12},{12,14},{14,10},{10,6},{6,2},{2,0},{1,5},{5,9},... | collective-permute-start | bytes 663560 | tf_op jit(solution)/shard_map/ppermute | solution.py:642
  25.6 0.7 %collective-permute-start.6 = (bf16[288,384]{1,0:T(8,128)(2,1)S(1)}, bf16[288,384]{1,0:T(8,128)(2,1)S(1)}, u32[]{:S(2)}, u32[]{:S(2)}) collective-permute-start(bf16[288,384]{1,0:T(8,128)(2,1)S(1)} %collective-permute-done.4.refs_1_), channel_id=1, source_target_pairs={{4,0},{8,4},{12,8},{14,12},{10,14},{6,10},{2,6},{0,2},{5,1},{9,5},... | collective-permute-start | bytes 663560 | tf_op jit(solution)/shard_map/ppermute | solution.py:642
  26.4 0.0 collective-permute-start.9
  26.4 0.5 collective-permute-start.10
  26.9 4.5 %collective-permute-done.5.refs_0_ = bf16[288,384]{1,0:T(8,128)(2,1)S(1)} collective-permute-done((bf16[288,384]{1,0:T(8,128)(2,1)S(1)}, bf16[288,384]{1,0:T(8,128)(2,1)S(1)}, u32[]{:S(2)}, u32[]{:S(2)}) %collective-permute-start.5) | collective-permute-done | bytes 221216 | tf_op jit(solution)/shard_map/ppermute | solution.py:642
  31.4 0.0 collective-permute-start.11
  31.4 0.7 collective-permute-done.6.refs_1_
  32.1 0.0 collective-permute-start.12
  32.1 0.5 local_terms.1
  32.6 1.6 %collective-permute-start.7 = (bf16[288,384]{1,0:T(8,128)(2,1)S(1)}, bf16[288,384]{1,0:T(8,128)(2,1)S(1)}, u32[]{:S(2)}, u32[]{:S(2)}) collective-permute-start(bf16[288,384]{1,0:T(8,128)(2,1)S(1)} %collective-permute-done.5.refs_0_), channel_id=1, source_target_pairs={{0,4},{4,8},{8,12},{12,14},{14,10},{10,6},{6,2},{2,0},{1,5},{5,9},... | collective-permute-start | bytes 663560 | tf_op jit(solution)/shard_map/ppermute | solution.py:642
  34.2 0.0 collective-permute-done.9.refs_2_
  34.2 0.5 collective-permute-start.8
  34.7 0.0 collective-permute-done.10.refs_3_
  34.7 1.3 %others_project.4 = (bf16[192,1536]{1,0:T(8,128)(2,1)S(1)}, bf16[192,192]{1,0:T(8,128)(2,1)S(1)}) custom-call(s32[1]{0:T(128)} %bitcast.wide_ref, bf16[1536,192]{1,0:T(8,128)(2,1)S(1)} %get-tuple-element.59.chosen_ref, bf16[288,384]{1,0:T(8,128)(2,1)S(1)} %collective-permute-done.3.refs_0_, bf16[288,384]{1,0:T(8,128)(2,1)S(1)} %collective-permute-done.4.refs_1_, ...), custom_call_target="tpu_custom_call" | custom-call | flops 679477248 | bytes 3538944 | tf_op jit(solution)/shard_map/others_project/pallas_call | solution.py:326
  36.0 0.0 collective-permute-done.11.refs_2_
  36.0 0.0 collective-permute-done.12.refs_3_
  36.0 1.3 %others_project.5 = (bf16[192,1536]{1,0:T(8,128)(2,1)S(1)}, bf16[192,192]{1,0:T(8,128)(2,1)S(1)}) custom-call(s32[1]{0:T(128)} %bitcast.wide_ref, bf16[1536,192]{1,0:T(8,128)(2,1)S(1)} %get-tuple-element.59.chosen_ref, bf16[288,384]{1,0:T(8,128)(2,1)S(1)} %collective-permute-done.5.refs_0_, bf16[288,384]{1,0:T(8,128)(2,1)S(1)} %collective-permute-done.6.refs_1_, ...), custom_call_target="tpu_custom_call" | custom-call | flops 679477248 | bytes 3538944 | tf_op jit(solution)/shard_map/others_project/pallas_call | solution.py:326
  37.3 3.2 %collective-permute-done.7.refs_0_ = bf16[288,384]{1,0:T(8,128)(2,1)S(1)} collective-permute-done((bf16[288,384]{1,0:T(8,128)(2,1)S(1)}, bf16[288,384]{1,0:T(8,128)(2,1)S(1)}, u32[]{:S(2)}, u32[]{:S(2)}) %collective-permute-start.7) | collective-permute-done | bytes 221216 | tf_op jit(solution)/shard_map/ppermute | solution.py:642
  40.5 1.3 %collective-permute-done.8.refs_1_ = bf16[288,384]{1,0:T(8,128)(2,1)S(1)} collective-permute-done((bf16[288,384]{1,0:T(8,128)(2,1)S(1)}, bf16[288,384]{1,0:T(8,128)(2,1)S(1)}, u32[]{:S(2)}, u32[]{:S(2)}) %collective-permute-start.8) | collective-permute-done | bytes 221216 | tf_op jit(solution)/shard_map/ppermute | solution.py:642
  41.8 1.6 %collective-permute-start.15 = (bf16[288,384]{1,0:T(8,128)(2,1)S(1)}, bf16[288,384]{1,0:T(8,128)(2,1)S(1)}, u32[]{:S(2)}, u32[]{:S(2)}) collective-permute-start(bf16[288,384]{1,0:T(8,128)(2,1)S(1)} %collective-permute-done.7.refs_0_), channel_id=1, source_target_pairs={{0,4},{4,8},{8,12},{12,14},{14,10},{10,6},{6,2},{2,0},{1,5},{5,9},... | collective-permute-start | bytes 663560 | tf_op jit(solution)/shard_map/ppermute | solution.py:645
  43.3 0.0 collective-permute-start.13
  43.4 0.5 collective-permute-start.14
  43.9 4.7 %collective-permute-done.15.refs_0_ = bf16[288,384]{1,0:T(8,128)(2,1)S(1)} collective-permute-done((bf16[288,384]{1,0:T(8,128)(2,1)S(1)}, bf16[288,384]{1,0:T(8,128)(2,1)S(1)}, u32[]{:S(2)}, u32[]{:S(2)}) %collective-permute-start.15) | collective-permute-done | bytes 221216 | tf_op jit(solution)/shard_map/ppermute | solution.py:645
  48.5 0.0 collective-permute-start.16
  48.5 0.0 collective-permute-done.13.refs_2_
  48.5 0.0 collective-permute-done.14.refs_3_
  48.5 1.3 %others_project.6 = (bf16[192,1536]{1,0:T(8,128)(2,1)S(1)}, bf16[192,192]{1,0:T(8,128)(2,1)S(1)}) custom-call(s32[1]{0:T(128)} %bitcast.wide_ref, bf16[1536,192]{1,0:T(8,128)(2,1)S(1)} %get-tuple-element.59.chosen_ref, bf16[288,384]{1,0:T(8,128)(2,1)S(1)} %collective-permute-done.7.refs_0_, bf16[288,384]{1,0:T(8,128)(2,1)S(1)} %collective-permute-done.8.refs_1_, ...), custom_call_target="tpu_custom_call" | custom-call | flops 679477248 | bytes 3538944 | tf_op jit(solution)/shard_map/others_project/pallas_call | solution.py:326
  49.8 0.0 copy-start
  49.9 0.1 collective-permute-done.16.refs_1_
  50.0 0.9 %others_project.7 = (bf16[96,1536]{1,0:T(8,128)(2,1)S(1)}, bf16[96,192]{1,0:T(8,128)(2,1)S(1)}) custom-call(s32[1]{0:T(128)} %bitcast.wide_ref, bf16[1536,192]{1,0:T(8,128)(2,1)S(1)} %get-tuple-element.59.chosen_ref, bf16[288,384]{1,0:T(8,128)(2,1)S(1)} %collective-permute-done.15.refs_0_, bf16[288,384]{1,0:T(8,128)(2,1)S(1)} %collective-permute-done.16.refs_1_, ...), custom_call_target="tpu_custom_call" | custom-call | flops 339738624 | bytes 3538944 | tf_op jit(solution)/shard_map/others_project/pallas_call | solution.py:326
  50.9 0.2 copy-done
  51.1 4.1 %attention.1 = (bf16[192,1536]{1,0:T(8,128)(2,1)S(1)}, bf16[768,384]{1,0:T(8,128)(2,1)S(1)}) custom-call(bf16[96,1536]{1,0:T(8,128)(2,1)S(1)} %get-tuple-element.56.refs_0_, bf16[192,1536]{1,0:T(8,128)(2,1)S(1)} %get-tuple-element.62.refs_1_, bf16[192,1536]{1,0:T(8,128)(2,1)S(1)} %get-tuple-element.63.refs_2_, ...), custom_call_target="tpu_custom_call" | custom-call | flops 1358954496 | bytes 2359296 | tf_op jit(solution)/shard_map/attention/pallas_call | solution.py:425
  55.3 0.0 copy-start.1
  55.3 0.6 collective-permute-start.17
  55.8 1.1 %value_gradient.1 = f32[192,384]{1,0:T(8,128)} custom-call(bf16[768,384]{1,0:T(8,128)(2,1)S(1)} %get-tuple-element.75.dv_ref, bf16[96,192]{1,0:T(8,128)(2,1)S(1)} %get-tuple-element.76.refs_0_, bf16[192,192]{1,0:T(8,128)(2,1)S(1)} %get-tuple-element.77.refs_1_, bf16[192,192]{1,0:T(8,128)(2,1)S(1)} %get-tuple-element.78.refs_2_, ...), custom_call_target="tpu_custom_call" | custom-call | flops 113246208 | bytes 589824 | tf_op jit(solution)/shard_map/value_gradient/pallas_call | solution.py:579
  57.0 0.5 collective-permute-done.17.there_ref
  57.5 0.0 copy-done.1
  57.5 2.4 %finish.1 = (bf16[96,1536]{1,0:T(8,128)(2,1)}, bf16[96,1536]{1,0:T(8,128)(2,1)S(1)}, bf16[2,1536]{1,0:T(2,128)(2,1)S(1)}, bf16[2,384,1536]{2,1,0:T(8,128)(2,1)S(1)}) custom-call(bf16[96,1536]{1,0:T(8,128)(2,1)S(1)} %get-tuple-element.54.hidden_ref, f32[96,1536]{1,0:T(8,128)S(1)} %get-tuple-element.55.slope_ref, f32[1,1536]{1,0:T(1,128)S(1)} %reshape.21.gain_ref, ...), custom_call_target="tpu_custom_call" | custom-call | flops 5898240 | bytes 1769472 | tf_op jit(solution)/shard_map/finish/pallas_call | solution.py:498
  59.9 1.7 %collective-permute-start.18 = (bf16[2,1536]{1,0:T(2,128)(2,1)S(1)}, bf16[2,1536]{1,0:T(2,128)(2,1)S(1)}, u32[]{:S(2)}, u32[]{:S(2)}) collective-permute-start(bf16[2,1536]{1,0:T(2,128)(2,1)S(1)} %get-tuple-element.73), channel_id=1, source_target_pairs={{0,2},{2,0},{4,6},{6,4},{8,10},{10,8},{12,14},{14,12},{1,3},{3,1},... | collective-permute-start | bytes 18440 | tf_op jit(solution)/shard_map/ppermute | solution.py:664
  61.5 2.4 %collective-permute-start.19 = (bf16[2,1536]{1,0:T(2,128)(2,1)S(1)}, bf16[2,1536]{1,0:T(2,128)(2,1)S(1)}, u32[]{:S(2)}, u32[]{:S(2)}) collective-permute-start(bf16[2,1536]{1,0:T(2,128)(2,1)S(1)} %get-tuple-element.73), channel_id=1, source_target_pairs={{2,4},{6,8},{10,12},{4,2},{8,6},{12,10},{3,5},{7,9},{11,13},{5,3},... | collective-permute-start | bytes 18440 | tf_op jit(solution)/shard_map/ppermute | solution.py:664
  63.9 2.4 %back_mid.1 = (f32[96,768]{1,0:T(8,128)S(1)}, bf16[3,384,1536]{2,1,0:T(8,128)(2,1)S(1)}) custom-call(bf16[96,1536]{1,0:T(8,128)(2,1)S(1)} %get-tuple-element.70.pre_ref, bf16[2,384,1536]{2,1,0:T(8,128)(2,1)S(1)} %get-tuple-element.71.weight_ref, bf16[5,384,1536]{2,1,0:T(8,128)(2,1)} %taps_any.5), custom_call_target="tpu_custom_call" | custom-call | flops 226492416 | bytes 5898240 | tf_op jit(solution)/shard_map/back_mid/pallas_call | solution.py:525
  66.3 0.0 collective-permute-done.18.first_ref
  66.3 1.6 %collective-permute-done.19.second_ref = bf16[2,1536]{1,0:T(2,128)(2,1)S(1)} collective-permute-done((bf16[2,1536]{1,0:T(2,128)(2,1)S(1)}, bf16[2,1536]{1,0:T(2,128)(2,1)S(1)}, u32[]{:S(2)}, u32[]{:S(2)}) %collective-permute-start.19) | collective-permute-done | bytes 6176 | tf_op jit(solution)/shard_map/ppermute | solution.py:664
  67.9 2.0 %back_rest.1 = bf16[192,384]{1,0:T(8,128)(2,1)} custom-call(s32[1]{0:T(128)} %bitcast.1.place_ref, bf16[96,1536]{1,0:T(8,128)(2,1)S(1)} %get-tuple-element.70.pre_ref, f32[96,768]{1,0:T(8,128)S(1)} %get-tuple-element.72.mid_ref, bf16[2,1536]{1,0:T(2,128)(2,1)S(1)} %collective-permute-done.18.first_ref, ...), custom_call_target="tpu_custom_call" | custom-call | flops 339738624 | bytes 3538944 | tf_op jit(solution)/shard_map/back_rest/pallas_call | solution.py:556
  (2 shorter events, 0.0 us)
Async XLA Ops:
  1.6 8.4 %collective-permute-start = (bf16[3,384]{1,0:T(4,128)(2,1)S(1)}, bf16[3,384]{1,0:T(4,128)(2,1)S(1)}, u32[]{:S(2)}, u32[]{:S(2)}) collective-permute-start(bf16[3,384]{1,0:T(4,128)(2,1)S(1)} %get-tuple-element.43), channel_id=1, source_target_pairs={{0,2},{2,0},{4,6},{6,4},{8,10},{10,8},{12,14},{14,12},{1,3},{3,1},... | collective-permute-start | bytes 6920 | tf_op jit(solution)/shard_map/ppermute | solution.py:620
  1.6 8.3 %collective-permute-start.1 = (bf16[3,384]{1,0:T(4,128)(2,1)S(1)}, bf16[3,384]{1,0:T(4,128)(2,1)S(1)}, u32[]{:S(2)}, u32[]{:S(2)}) collective-permute-start(bf16[3,384]{1,0:T(4,128)(2,1)S(1)} %get-tuple-element.43), channel_id=1, source_target_pairs={{2,4},{6,8},{10,12},{4,2},{8,6},{12,10},{3,5},{7,9},{11,13},{5,3},... | collective-permute-start | bytes 6920 | tf_op jit(solution)/shard_map/ppermute | solution.py:620
  10.0 2.4 %copy-start.2 = (f32[1536]{0:T(1024)S(1)}, f32[1536]{0:T(1024)}, u32[]{:S(2)}) copy-start(f32[1536]{0:T(1024)} %param.11) | copy-start | bytes 18436
  10.0 2.4 %copy-start.3 = (f32[1536]{0:T(1024)S(1)}, f32[1536]{0:T(1024)}, u32[]{:S(2)}) copy-start(f32[1536]{0:T(1024)} %param.12) | copy-start | bytes 18436
  12.3 2.0 %collective-permute-start.2 = (bf16[96,1536]{1,0:T(8,128)(2,1)S(1)}, bf16[96,1536]{1,0:T(8,128)(2,1)S(1)}, u32[]{:S(2)}, u32[]{:S(2)}) collective-permute-start(bf16[96,1536]{1,0:T(8,128)(2,1)S(1)} %conv_edge.1.mine_ref), channel_id=1, source_target_pairs={{0,1},{1,0},{2,3},{3,2},{4,5},{5,4},{6,7},{7,6},{8,9},{9,8},{10,11... | collective-permute-start | bytes 884744 | tf_op jit(solution)/shard_map/ppermute | solution.py:624
  16.4 7.9 %collective-permute-start.3 = (bf16[288,384]{1,0:T(8,128)(2,1)S(1)}, bf16[288,384]{1,0:T(8,128)(2,1)S(1)}, u32[]{:S(2)}, u32[]{:S(2)}) collective-permute-start(bf16[288,384]{1,0:T(8,128)(2,1)S(1)} %get-tuple-element.44), channel_id=1, source_target_pairs={{0,4},{4,8},{8,12},{12,14},{14,10},{10,6},{6,2},{2,0},{1,5},{5,9},... | collective-permute-start | bytes 663560 | tf_op jit(solution)/shard_map/ppermute | solution.py:642
  16.5 7.9 %collective-permute-start.4 = (bf16[288,384]{1,0:T(8,128)(2,1)S(1)}, bf16[288,384]{1,0:T(8,128)(2,1)S(1)}, u32[]{:S(2)}, u32[]{:S(2)}) collective-permute-start(bf16[288,384]{1,0:T(8,128)(2,1)S(1)} %get-tuple-element.44), channel_id=1, source_target_pairs={{4,0},{8,4},{12,8},{14,12},{10,14},{6,10},{2,6},{0,2},{5,1},{9,5},... | collective-permute-start | bytes 663560 | tf_op jit(solution)/shard_map/ppermute | solution.py:642
  24.3 7.0 %collective-permute-start.5 = (bf16[288,384]{1,0:T(8,128)(2,1)S(1)}, bf16[288,384]{1,0:T(8,128)(2,1)S(1)}, u32[]{:S(2)}, u32[]{:S(2)}) collective-permute-start(bf16[288,384]{1,0:T(8,128)(2,1)S(1)} %collective-permute-done.3.refs_0_), channel_id=1, source_target_pairs={{0,4},{4,8},{8,12},{12,14},{14,10},{10,6},{6,2},{2,0},{1,5},{5,9},... | collective-permute-start | bytes 663560 | tf_op jit(solution)/shard_map/ppermute | solution.py:642
  25.6 6.4 %collective-permute-start.6 = (bf16[288,384]{1,0:T(8,128)(2,1)S(1)}, bf16[288,384]{1,0:T(8,128)(2,1)S(1)}, u32[]{:S(2)}, u32[]{:S(2)}) collective-permute-start(bf16[288,384]{1,0:T(8,128)(2,1)S(1)} %collective-permute-done.4.refs_1_), channel_id=1, source_target_pairs={{4,0},{8,4},{12,8},{14,12},{10,14},{6,10},{2,6},{0,2},{5,1},{9,5},... | collective-permute-start | bytes 663560 | tf_op jit(solution)/shard_map/ppermute | solution.py:642
  26.4 7.8 %collective-permute-start.9 = (bf16[288,384]{1,0:T(8,128)(2,1)S(1)}, bf16[288,384]{1,0:T(8,128)(2,1)S(1)}, u32[]{:S(2)}, u32[]{:S(2)}) collective-permute-start(bf16[288,384]{1,0:T(8,128)(2,1)S(1)} %collective-permute-done.3.refs_0_), channel_id=1, source_target_pairs={{0,1},{1,0},{2,3},{3,2},{4,5},{5,4},{6,7},{7,6},{8,9},{9,8},{10,11... | collective-permute-start | bytes 663560 | tf_op jit(solution)/shard_map/ppermute | solution.py:646
  26.4 8.3 %collective-permute-start.10 = (bf16[288,384]{1,0:T(8,128)(2,1)S(1)}, bf16[288,384]{1,0:T(8,128)(2,1)S(1)}, u32[]{:S(2)}, u32[]{:S(2)}) collective-permute-start(bf16[288,384]{1,0:T(8,128)(2,1)S(1)} %collective-permute-done.4.refs_1_), channel_id=1, source_target_pairs={{0,1},{1,0},{2,3},{3,2},{4,5},{5,4},{6,7},{7,6},{8,9},{9,8},{10,11... | collective-permute-start | bytes 663560 | tf_op jit(solution)/shard_map/ppermute | solution.py:646
  31.4 4.6 %collective-permute-start.11 = (bf16[288,384]{1,0:T(8,128)(2,1)S(1)}, bf16[288,384]{1,0:T(8,128)(2,1)S(1)}, u32[]{:S(2)}, u32[]{:S(2)}) collective-permute-start(bf16[288,384]{1,0:T(8,128)(2,1)S(1)} %collective-permute-done.5.refs_0_), channel_id=1, source_target_pairs={{0,1},{1,0},{2,3},{3,2},{4,5},{5,4},{6,7},{7,6},{8,9},{9,8},{10,11... | collective-permute-start | bytes 663560 | tf_op jit(solution)/shard_map/ppermute | solution.py:646
  32.1 3.9 %collective-permute-start.12 = (bf16[288,384]{1,0:T(8,128)(2,1)S(1)}, bf16[288,384]{1,0:T(8,128)(2,1)S(1)}, u32[]{:S(2)}, u32[]{:S(2)}) collective-permute-start(bf16[288,384]{1,0:T(8,128)(2,1)S(1)} %collective-permute-done.6.refs_1_), channel_id=1, source_target_pairs={{0,1},{1,0},{2,3},{3,2},{4,5},{5,4},{6,7},{7,6},{8,9},{9,8},{10,11... | collective-permute-start | bytes 663560 | tf_op jit(solution)/shard_map/ppermute | solution.py:646
  32.6 7.9 %collective-permute-start.7 = (bf16[288,384]{1,0:T(8,128)(2,1)S(1)}, bf16[288,384]{1,0:T(8,128)(2,1)S(1)}, u32[]{:S(2)}, u32[]{:S(2)}) collective-permute-start(bf16[288,384]{1,0:T(8,128)(2,1)S(1)} %collective-permute-done.5.refs_0_), channel_id=1, source_target_pairs={{0,4},{4,8},{8,12},{12,14},{14,10},{10,6},{6,2},{2,0},{1,5},{5,9},... | collective-permute-start | bytes 663560 | tf_op jit(solution)/shard_map/ppermute | solution.py:642
  34.2 7.6 %collective-permute-start.8 = (bf16[288,384]{1,0:T(8,128)(2,1)S(1)}, bf16[288,384]{1,0:T(8,128)(2,1)S(1)}, u32[]{:S(2)}, u32[]{:S(2)}) collective-permute-start(bf16[288,384]{1,0:T(8,128)(2,1)S(1)} %collective-permute-done.6.refs_1_), channel_id=1, source_target_pairs={{4,0},{8,4},{12,8},{14,12},{10,14},{6,10},{2,6},{0,2},{5,1},{9,5},... | collective-permute-start | bytes 663560 | tf_op jit(solution)/shard_map/ppermute | solution.py:642
  41.8 6.7 %collective-permute-start.15 = (bf16[288,384]{1,0:T(8,128)(2,1)S(1)}, bf16[288,384]{1,0:T(8,128)(2,1)S(1)}, u32[]{:S(2)}, u32[]{:S(2)}) collective-permute-start(bf16[288,384]{1,0:T(8,128)(2,1)S(1)} %collective-permute-done.7.refs_0_), channel_id=1, source_target_pairs={{0,4},{4,8},{8,12},{12,14},{14,10},{10,6},{6,2},{2,0},{1,5},{5,9},... | collective-permute-start | bytes 663560 | tf_op jit(solution)/shard_map/ppermute | solution.py:645
  43.3 5.2 %collective-permute-start.13 = (bf16[288,384]{1,0:T(8,128)(2,1)S(1)}, bf16[288,384]{1,0:T(8,128)(2,1)S(1)}, u32[]{:S(2)}, u32[]{:S(2)}) collective-permute-start(bf16[288,384]{1,0:T(8,128)(2,1)S(1)} %collective-permute-done.7.refs_0_), channel_id=1, source_target_pairs={{0,1},{1,0},{2,3},{3,2},{4,5},{5,4},{6,7},{7,6},{8,9},{9,8},{10,11... | collective-permute-start | bytes 663560 | tf_op jit(solution)/shard_map/ppermute | solution.py:646
  43.4 5.2 %collective-permute-start.14 = (bf16[288,384]{1,0:T(8,128)(2,1)S(1)}, bf16[288,384]{1,0:T(8,128)(2,1)S(1)}, u32[]{:S(2)}, u32[]{:S(2)}) collective-permute-start(bf16[288,384]{1,0:T(8,128)(2,1)S(1)} %collective-permute-done.8.refs_1_), channel_id=1, source_target_pairs={{0,1},{1,0},{2,3},{3,2},{4,5},{5,4},{6,7},{7,6},{8,9},{9,8},{10,11... | collective-permute-start | bytes 663560 | tf_op jit(solution)/shard_map/ppermute | solution.py:646
  48.5 1.5 %collective-permute-start.16 = (bf16[288,384]{1,0:T(8,128)(2,1)S(1)}, bf16[288,384]{1,0:T(8,128)(2,1)S(1)}, u32[]{:S(2)}, u32[]{:S(2)}) collective-permute-start(bf16[288,384]{1,0:T(8,128)(2,1)S(1)} %collective-permute-done.15.refs_0_), channel_id=1, source_target_pairs={{0,1},{1,0},{2,3},{3,2},{4,5},{5,4},{6,7},{7,6},{8,9},{9,8},{10,11... | collective-permute-start | bytes 663560 | tf_op jit(solution)/shard_map/ppermute | solution.py:646
  49.8 1.3 %copy-start = (bf16[384,1536]{1,0:T(8,128)(2,1)S(1)}, bf16[384,1536]{1,0:T(8,128)(2,1)}, u32[]{:S(2)}) copy-start(bf16[384,1536]{1,0:T(8,128)(2,1)} %refs_9_.1) | copy-start | bytes 3538948
  55.3 2.2 %copy-start.1 = (bf16[1,96,1536]{2,1,0:T(8,128)(2,1)S(1)}, bf16[1,96,1536]{2,1,0:T(8,128)(2,1)}, u32[]{:S(2)}) copy-start(bf16[1,96,1536]{2,1,0:T(8,128)(2,1)} %param.17) | copy-start | bytes 884740
  55.3 2.2 %collective-permute-start.17 = (bf16[192,1536]{1,0:T(8,128)(2,1)S(1)}, bf16[192,1536]{1,0:T(8,128)(2,1)S(1)}, u32[]{:S(2)}, u32[]{:S(2)}) collective-permute-start(bf16[192,1536]{1,0:T(8,128)(2,1)S(1)} %get-tuple-element.68.here_ref), channel_id=1, source_target_pairs={{0,1},{1,0},{2,3},{3,2},{4,5},{5,4},{6,7},{7,6},{8,9},{9,8},{10,11... | collective-permute-start | bytes 1769480 | tf_op jit(solution)/shard_map/ppermute | solution.py:659
  59.9 6.4 %collective-permute-start.18 = (bf16[2,1536]{1,0:T(2,128)(2,1)S(1)}, bf16[2,1536]{1,0:T(2,128)(2,1)S(1)}, u32[]{:S(2)}, u32[]{:S(2)}) collective-permute-start(bf16[2,1536]{1,0:T(2,128)(2,1)S(1)} %get-tuple-element.73), channel_id=1, source_target_pairs={{0,2},{2,0},{4,6},{6,4},{8,10},{10,8},{12,14},{14,12},{1,3},{3,1},... | collective-permute-start | bytes 18440 | tf_op jit(solution)/shard_map/ppermute | solution.py:664
  61.5 6.4 %collective-permute-start.19 = (bf16[2,1536]{1,0:T(2,128)(2,1)S(1)}, bf16[2,1536]{1,0:T(2,128)(2,1)S(1)}, u32[]{:S(2)}, u32[]{:S(2)}) collective-permute-start(bf16[2,1536]{1,0:T(2,128)(2,1)S(1)} %get-tuple-element.73), channel_id=1, source_target_pairs={{2,4},{6,8},{10,12},{4,2},{8,6},{12,10},{3,5},{7,9},{11,13},{5,3},... | collective-permute-start | bytes 18440 | tf_op jit(solution)/shard_map/ppermute | solution.py:664

commit v5 on v4

--- a/solution.py
+++ b/solution.py
@@ -67,27 +67,34 @@
     return jnp.where(test(row, col), 1.0, 0.0).astype(BF16)
 
 
-def edges_kernel(fine_any, fine_ref, edge_ref, sem):
-    copy = pltpu.make_async_copy(fine_any, fine_ref, sem)
-    copy.start()
-    copy.wait()
-    rows = fine_ref.shape[0]
-    edge_ref[0:2, :] = fine_ref[rows - 2 :, :]
-    edge_ref[2:3, :] = fine_ref[0:1, :]
+def edges_kernel(fine_any, edge_ref, top, low, sems):
+    rows = fine_any.shape[0]
+    copies = [
+        pltpu.make_async_copy(fine_any.at[pl.ds(0, CHUNK)], top, sems.at[0]),
+        pltpu.make_async_copy(fine_any.at[pl.ds(rows - CHUNK, CHUNK)], low, sems.at[1]),
+    ]
+    for c in copies:
+        c.start()
+    for c in copies:
+        c.wait()
+    edge_ref[0:2, :] = low[CHUNK - 2 :, :]
+    edge_ref[2:3, :] = top[0:1, :]
 
 
 def edges(fine):
+    channels = fine.shape[1]
     return pl.pallas_call(
         edges_kernel,
-        out_shape=[
-            jax.ShapeDtypeStruct(fine.shape, BF16),
-            jax.ShapeDtypeStruct((3, fine.shape[1]), BF16),
+        out_shape=jax.ShapeDtypeStruct((3, channels), BF16),
+        in_specs=[in_hbm()],
+        out_specs=spec(),
+        scratch_shapes=[
+            pltpu.VMEM((CHUNK, channels), BF16),
+            pltpu.VMEM((CHUNK, channels), BF16),
+            pltpu.SemaphoreType.DMA((2,)),
         ],
-        in_specs=[in_hbm()],
-        out_specs=[spec()] * 2,
-        scratch_shapes=[pltpu.SemaphoreType.DMA],
-        compiler_params=params(),
-        cost_estimate=cost(fine.size, 2 * fine.size),
+        compiler_params=params(),
+        cost_estimate=cost(channels, 64 * channels),
         name="edges",
     )(far(fine))
 
@@ -130,13 +137,16 @@
     )(far(cot), far(wo))
 
 
-def conv_kernel(order, fine_ref, taps_any, out_ref, taps, sems):
-    fine_rows, channels = fine_ref.shape
+def conv_kernel(order, fine_any, taps_any, out_ref, fine, taps, sems):
+    fine_rows, channels = fine.shape
+    fine_copy = pltpu.make_async_copy(fine_any, fine, sems.at[len(order)])
+    fine_copy.start()
     tok = fine_rows // 2
     copies = {k: pltpu.make_async_copy(taps_any.at[k], taps.at[k], sems.at[k]) for k in order}
     for k in order:
         copies[k].start()
-    block = fine_ref[...]
+    fine_copy.wait()
+    block = fine[...]
     total = None
     for k in order:
         rows = dot(pick((tok, fine_rows), lambda r, c, k=k: c == 2 * r + k - 2), block).astype(BF16)
@@ -152,13 +162,17 @@
     return pl.pallas_call(
         functools.partial(conv_kernel, tuple(range(taps))),
         out_shape=jax.ShapeDtypeStruct((tok, features), F32),
-        in_specs=[spec(), in_hbm()],
+        in_specs=[in_hbm()] * 2,
         out_specs=spec(),
-        scratch_shapes=[pltpu.VMEM(weight.shape, BF16), pltpu.SemaphoreType.DMA((taps,))],
+        scratch_shapes=[
+            pltpu.VMEM(fine.shape, BF16),
+            pltpu.VMEM(weight.shape, BF16),
+            pltpu.SemaphoreType.DMA((taps + 1,)),
+        ],
         compiler_params=params(12),
         cost_estimate=cost(2 * tok * weight.size, 2 * weight.size),
         name="conv_inner",
-    )(fine, far(weight))
+    )(far(fine), far(weight))
 
 
 def conv_edge_kernel(place_ref, inner_ref, first_ref, second_ref, taps_any, out_ref, taps, sems):
@@ -373,7 +387,10 @@
         delta = jnp.sum(expo * back, 0, keepdims=True) * inv
         prob_b = (expo * inv).astype(BF16)
         score_own = (expo[:tok] * inv * (back[:tok] - delta) * scale).astype(BF16)
-        if first:
+        if tile == total:
+            dv_ref[:, cols] = dot(prob_b, up).astype(BF16)
+            dk_acc[:, cols] = dot(score_own, query)
+        elif first:
             dv_acc[:, cols] = dot(prob_b, up)
             dk_acc[:, cols] = dot(score_own, query)
         else:
@@ -403,7 +420,8 @@
             def _(step):
                 block(pl.multiple_of(step * tile, tile), None, h)
 
-    dv_ref[...] = dv_acc[...].astype(BF16)
+    if tile != total:
+        dv_ref[...] = dv_acc[...].astype(BF16)
     both_ref[:tok, :] = dot(att[...], wo[...]).astype(BF16)
     backs = []
     for acc, lo in ((dq_acc, 0), (dk_acc, width)):
@@ -616,10 +634,10 @@
     count, core_rows = features // n, tok // 2
     weights = (query_weight, key_weight, value_weight)
 
-    fine_here, edge = edges(fine)
+    edge = edges(fine)
     edge_near, edge_across = lax.ppermute(edge, "seq", near), lax.ppermute(edge, "seq", across)
     att_grad = early(cot, out_weight)
-    inner = conv_inner(fine_here, conv_weight)
+    inner = conv_inner(fine, conv_weight)
     mine = conv_edge(place, inner, edge_near, edge_across, conv_weight)
     theirs = lax.ppermute(mine, "wide", swap)
     normed, message, *weights = norm(wide, mine, theirs, bias, gain, weights, att_grad)

time: 70.3 us -> 70.1 us (level)
  no operation moved by 1% of the time
where the time goes in v5:
time: 70.1 us; the launch traced here: 69.7 us
  Pallas kernels  28.7 us (41%)
  waiting for transfers between devices  21.3 us (30%)
  starting transfers between devices  18.5 us (26%)
  between operations  0.91 us (1%)
    ppermute x6, waiting for transfers between devices, on_device(): cw, ccw = (lax.ppermute(cw, 'seq', ahead), lax.ppermute(ccw, 'seq', behind))  14.5 us
    ppermute x2, starting transfers between devices, on_device(): lax.ppermute(edge, 'seq', across)  7.39 us
    ppermute x6, starting transfers between devices, on_device(): cw, ccw = (lax.ppermute(cw, 'seq', ahead), lax.ppermute(ccw, 'seq', behind))  6.17 us
    pallas_call x4, Pallas kernels, others_project(): pl.pallas_call(functools.partial(others_kernel, len(mine), half), out_sha...  4.79 us
    ppermute x1, waiting for transfers between devices, on_device(): blocks = [lax.ppermute(cw, 'seq', ahead)]  4.66 us
    pallas_call x1, Pallas kernels, attention(): pl.pallas_call(functools.partial(attention_kernel, tok, tile, heads, qkv_...  4.06 us
    pallas_call x1, Pallas kernels, conv_inner(): pl.pallas_call(functools.partial(conv_kernel, tuple(range(taps))), out_sh...  3.47 us
    pallas_call x1, Pallas kernels, back_mid(): pl.pallas_call(back_mid_kernel, out_shape=[jax.ShapeDtypeStruct((tok, 2 *...  2.39 us
  transfers between devices with their start and end apart: 20, of which 10 were waited for; matrix products, arithmetic and copies ran while one was open for 0% of the time, Pallas kernels for 20%

profile of v5, /device:TPU:4, one launch (start us, length us, event | category | flops | bytes accessed | tf_op | source)
XLA Modules:
  0.0 69.7 jit_solution(12932754896803219933)
XLA Ops:
  0.6 0.8 %edges.1 = bf16[3,384]{1,0:T(4,128)(2,1)S(1)} custom-call(bf16[192,384]{1,0:T(8,128)(2,1)} %bitcast.9), custom_call_target="tpu_custom_call" | custom-call | flops 384 | bytes 24576 | tf_op jit(solution)/shard_map/edges/pallas_call | solution.py:86
  1.4 0.1 collective-permute-start
  1.5 4.9 %collective-permute-start.1 = (bf16[3,384]{1,0:T(4,128)(2,1)S(1)}, bf16[3,384]{1,0:T(4,128)(2,1)S(1)}, u32[]{:S(2)}, u32[]{:S(2)}) collective-permute-start(bf16[3,384]{1,0:T(4,128)(2,1)S(1)} %edges.1), channel_id=1, source_target_pairs={{2,4},{6,8},{10,12},{4,2},{8,6},{12,10},{3,5},{7,9},{11,13},{5,3},... | collective-permute-start | bytes 6920 | tf_op jit(solution)/shard_map/ppermute | solution.py:638
  6.4 3.5 %conv_inner.1.inner_ref = f32[96,1536]{1,0:T(8,128)S(1)} custom-call(bf16[192,384]{1,0:T(8,128)(2,1)} %bitcast.10, bf16[5,384,1536]{2,1,0:T(8,128)(2,1)} %taps_any.5), custom_call_target="tpu_custom_call" | custom-call | flops 566231040 | bytes 5898240 | tf_op jit(solution)/shard_map/conv_inner/pallas_call | solution.py:162
  9.9 0.0 collective-permute-done.first_ref
  9.9 0.0 collective-permute-done.1.second_ref
  9.9 0.0 copy-start.2
  9.9 0.0 copy-start.3
  9.9 2.3 %conv_edge.1.mine_ref = bf16[96,1536]{1,0:T(8,128)(2,1)S(1)} custom-call(s32[1]{0:T(128)} %bitcast.1.place_ref, f32[96,1536]{1,0:T(8,128)S(1)} %conv_inner.1.inner_ref, bf16[3,384]{1,0:T(4,128)(2,1)S(1)} %collective-permute-done.first_ref, bf16[3,384]{1,0:T(4,128)(2,1)S(1)} %collective-permute-done.1.second_ref, bf16[5,384,1536]{2,1,0:T(8,128)(2,1)} %taps_any.5), custom_call_target="tpu_custom_call" | custom-call | flops 56623104 | bytes 3538944 | tf_op jit(solution)/shard_map/conv_edge/pallas_call | solution.py:199
  12.2 0.1 collective-permute-start.2
  12.3 0.0 copy-done.2
  12.4 0.0 copy-done.3
  12.4 1.9 %early.1.refs_3_.grad_ref = bf16[96,384]{1,0:T(8,128)(2,1)S(1)} custom-call(bf16[96,1536]{1,0:T(8,128)(2,1)} %bitcast.7, bf16[384,1536]{1,0:T(8,128)(2,1)} %refs_9_.1), custom_call_target="tpu_custom_call" | custom-call | flops 113246208 | bytes 1179648 | tf_op jit(solution)/shard_map/early/pallas_call | solution.py:124
  14.3 0.0 collective-permute-done.2.theirs_ref
  14.3 2.0 %norm.1 = (bf16[96,1536]{1,0:T(8,128)(2,1)S(1)}, bf16[288,384]{1,0:T(8,128)(2,1)S(1)}, bf16[1536,384]{1,0:T(8,128)(2,1)S(1)}, bf16[1536,384]{1,0:T(8,128)(2,1)S(1)}, bf16[1536,384]{1,0:T(8,128)(2,1)S(1)}) custom-call(s32[1]{0:T(128)} %bitcast.wide_ref, bf16[96,1536]{1,0:T(8,128)(2,1)S(1)} %conv_edge.1.mine_ref, ...), custom_call_target="tpu_custom_call" | custom-call | flops 4423680 | bytes 884736 | tf_op jit(solution)/shard_map/norm/pallas_call | solution.py:268
  16.3 0.1 collective-permute-start.3
  16.4 2.0 %collective-permute-start.4 = (bf16[288,384]{1,0:T(8,128)(2,1)S(1)}, bf16[288,384]{1,0:T(8,128)(2,1)S(1)}, u32[]{:S(2)}, u32[]{:S(2)}) collective-permute-start(bf16[288,384]{1,0:T(8,128)(2,1)S(1)} %get-tuple-element.40), channel_id=1, source_target_pairs={{4,0},{8,4},{12,8},{14,12},{10,14},{6,10},{2,6},{0,2},{5,1},{9,5},... | collective-permute-start | bytes 663560 | tf_op jit(solution)/shard_map/ppermute | solution.py:660
  18.4 0.9 %own_project.1 = (bf16[96,1536]{1,0:T(8,128)(2,1)S(1)}, bf16[96,192]{1,0:T(8,128)(2,1)S(1)}, f32[96,768]{1,0:T(8,128)S(1)}, bf16[1536,192]{1,0:T(8,128)(2,1)S(1)}) custom-call(s32[1]{0:T(128)} %bitcast.1.place_ref, bf16[96,1536]{1,0:T(8,128)(2,1)S(1)} %get-tuple-element.41.normed_ref, bf16[96,384]{1,0:T(8,128)(2,1)S(1)} %early.1.refs_3_.grad_ref, ...), custom_call_target="tpu_custom_call" | custom-call | flops 339738624 | bytes 3538944 | tf_op jit(solution)/shard_map/own_project/pallas_call | solution.py:307
  19.3 4.9 %collective-permute-done.3.refs_0_ = bf16[288,384]{1,0:T(8,128)(2,1)S(1)} collective-permute-done((bf16[288,384]{1,0:T(8,128)(2,1)S(1)}, bf16[288,384]{1,0:T(8,128)(2,1)S(1)}, u32[]{:S(2)}, u32[]{:S(2)}) %collective-permute-start.3) | collective-permute-done | bytes 221216 | tf_op jit(solution)/shard_map/ppermute | solution.py:660
  24.2 0.1 collective-permute-done.4.refs_1_
  24.3 1.2 %collective-permute-start.5 = (bf16[288,384]{1,0:T(8,128)(2,1)S(1)}, bf16[288,384]{1,0:T(8,128)(2,1)S(1)}, u32[]{:S(2)}, u32[]{:S(2)}) collective-permute-start(bf16[288,384]{1,0:T(8,128)(2,1)S(1)} %collective-permute-done.3.refs_0_), channel_id=1, source_target_pairs={{0,4},{4,8},{8,12},{12,14},{14,10},{10,6},{6,2},{2,0},{1,5},{5,9},... | collective-permute-start | bytes 663560 | tf_op jit(solution)/shard_map/ppermute | solution.py:660
  25.4 0.8 %collective-permute-start.6 = (bf16[288,384]{1,0:T(8,128)(2,1)S(1)}, bf16[288,384]{1,0:T(8,128)(2,1)S(1)}, u32[]{:S(2)}, u32[]{:S(2)}) collective-permute-start(bf16[288,384]{1,0:T(8,128)(2,1)S(1)} %collective-permute-done.4.refs_1_), channel_id=1, source_target_pairs={{4,0},{8,4},{12,8},{14,12},{10,14},{6,10},{2,6},{0,2},{5,1},{9,5},... | collective-permute-start | bytes 663560 | tf_op jit(solution)/shard_map/ppermute | solution.py:660
  26.3 0.0 collective-permute-start.9
  26.3 0.5 collective-permute-start.10
  26.8 4.5 %collective-permute-done.5.refs_0_ = bf16[288,384]{1,0:T(8,128)(2,1)S(1)} collective-permute-done((bf16[288,384]{1,0:T(8,128)(2,1)S(1)}, bf16[288,384]{1,0:T(8,128)(2,1)S(1)}, u32[]{:S(2)}, u32[]{:S(2)}) %collective-permute-start.5) | collective-permute-done | bytes 221216 | tf_op jit(solution)/shard_map/ppermute | solution.py:660
  31.3 0.0 collective-permute-start.11
  31.3 0.6 collective-permute-done.6.refs_1_
  31.9 0.0 collective-permute-start.12
  31.9 0.5 local_terms.1
  32.4 1.6 %collective-permute-start.7 = (bf16[288,384]{1,0:T(8,128)(2,1)S(1)}, bf16[288,384]{1,0:T(8,128)(2,1)S(1)}, u32[]{:S(2)}, u32[]{:S(2)}) collective-permute-start(bf16[288,384]{1,0:T(8,128)(2,1)S(1)} %collective-permute-done.5.refs_0_), channel_id=1, source_target_pairs={{0,4},{4,8},{8,12},{12,14},{14,10},{10,6},{6,2},{2,0},{1,5},{5,9},... | collective-permute-start | bytes 663560 | tf_op jit(solution)/shard_map/ppermute | solution.py:660
  34.0 0.0 collective-permute-done.9.refs_2_
  34.0 0.4 collective-permute-start.8
  34.5 0.0 collective-permute-done.10.refs_3_
  34.5 1.3 %others_project.4 = (bf16[192,1536]{1,0:T(8,128)(2,1)S(1)}, bf16[192,192]{1,0:T(8,128)(2,1)S(1)}) custom-call(s32[1]{0:T(128)} %bitcast.wide_ref, bf16[1536,192]{1,0:T(8,128)(2,1)S(1)} %get-tuple-element.55.chosen_ref, bf16[288,384]{1,0:T(8,128)(2,1)S(1)} %collective-permute-done.3.refs_0_, bf16[288,384]{1,0:T(8,128)(2,1)S(1)} %collective-permute-done.4.refs_1_, ...), custom_call_target="tpu_custom_call" | custom-call | flops 679477248 | bytes 3538944 | tf_op jit(solution)/shard_map/others_project/pallas_call | solution.py:340
  35.8 0.0 collective-permute-done.11.refs_2_
  35.8 0.0 collective-permute-done.12.refs_3_
  35.8 1.3 %others_project.5 = (bf16[192,1536]{1,0:T(8,128)(2,1)S(1)}, bf16[192,192]{1,0:T(8,128)(2,1)S(1)}) custom-call(s32[1]{0:T(128)} %bitcast.wide_ref, bf16[1536,192]{1,0:T(8,128)(2,1)S(1)} %get-tuple-element.55.chosen_ref, bf16[288,384]{1,0:T(8,128)(2,1)S(1)} %collective-permute-done.5.refs_0_, bf16[288,384]{1,0:T(8,128)(2,1)S(1)} %collective-permute-done.6.refs_1_, ...), custom_call_target="tpu_custom_call" | custom-call | flops 679477248 | bytes 3538944 | tf_op jit(solution)/shard_map/others_project/pallas_call | solution.py:340
  37.1 3.1 %collective-permute-done.7.refs_0_ = bf16[288,384]{1,0:T(8,128)(2,1)S(1)} collective-permute-done((bf16[288,384]{1,0:T(8,128)(2,1)S(1)}, bf16[288,384]{1,0:T(8,128)(2,1)S(1)}, u32[]{:S(2)}, u32[]{:S(2)}) %collective-permute-start.7) | collective-permute-done | bytes 221216 | tf_op jit(solution)/shard_map/ppermute | solution.py:660
  40.3 1.3 %collective-permute-done.8.refs_1_ = bf16[288,384]{1,0:T(8,128)(2,1)S(1)} collective-permute-done((bf16[288,384]{1,0:T(8,128)(2,1)S(1)}, bf16[288,384]{1,0:T(8,128)(2,1)S(1)}, u32[]{:S(2)}, u32[]{:S(2)}) %collective-permute-start.8) | collective-permute-done | bytes 221216 | tf_op jit(solution)/shard_map/ppermute | solution.py:660
  41.6 1.6 %collective-permute-start.15 = (bf16[288,384]{1,0:T(8,128)(2,1)S(1)}, bf16[288,384]{1,0:T(8,128)(2,1)S(1)}, u32[]{:S(2)}, u32[]{:S(2)}) collective-permute-start(bf16[288,384]{1,0:T(8,128)(2,1)S(1)} %collective-permute-done.7.refs_0_), channel_id=1, source_target_pairs={{0,4},{4,8},{8,12},{12,14},{14,10},{10,6},{6,2},{2,0},{1,5},{5,9},... | collective-permute-start | bytes 663560 | tf_op jit(solution)/shard_map/ppermute | solution.py:663
  43.2 0.0 collective-permute-start.13
  43.2 0.5 collective-permute-start.14
  43.7 4.7 %collective-permute-done.15.refs_0_ = bf16[288,384]{1,0:T(8,128)(2,1)S(1)} collective-permute-done((bf16[288,384]{1,0:T(8,128)(2,1)S(1)}, bf16[288,384]{1,0:T(8,128)(2,1)S(1)}, u32[]{:S(2)}, u32[]{:S(2)}) %collective-permute-start.15) | collective-permute-done | bytes 221216 | tf_op jit(solution)/shard_map/ppermute | solution.py:663
  48.3 0.0 collective-permute-start.16
  48.3 0.0 collective-permute-done.13.refs_2_
  48.3 0.0 collective-permute-done.14.refs_3_
  48.4 1.3 %others_project.6 = (bf16[192,1536]{1,0:T(8,128)(2,1)S(1)}, bf16[192,192]{1,0:T(8,128)(2,1)S(1)}) custom-call(s32[1]{0:T(128)} %bitcast.wide_ref, bf16[1536,192]{1,0:T(8,128)(2,1)S(1)} %get-tuple-element.55.chosen_ref, bf16[288,384]{1,0:T(8,128)(2,1)S(1)} %collective-permute-done.7.refs_0_, bf16[288,384]{1,0:T(8,128)(2,1)S(1)} %collective-permute-done.8.refs_1_, ...), custom_call_target="tpu_custom_call" | custom-call | flops 679477248 | bytes 3538944 | tf_op jit(solution)/shard_map/others_project/pallas_call | solution.py:340
  49.7 0.0 copy-start
  49.7 0.1 collective-permute-done.16.refs_1_
  49.8 0.9 %others_project.7 = (bf16[96,1536]{1,0:T(8,128)(2,1)S(1)}, bf16[96,192]{1,0:T(8,128)(2,1)S(1)}) custom-call(s32[1]{0:T(128)} %bitcast.wide_ref, bf16[1536,192]{1,0:T(8,128)(2,1)S(1)} %get-tuple-element.55.chosen_ref, bf16[288,384]{1,0:T(8,128)(2,1)S(1)} %collective-permute-done.15.refs_0_, bf16[288,384]{1,0:T(8,128)(2,1)S(1)} %collective-permute-done.16.refs_1_, ...), custom_call_target="tpu_custom_call" | custom-call | flops 339738624 | bytes 3538944 | tf_op jit(solution)/shard_map/others_project/pallas_call | solution.py:340
  50.7 0.2 copy-done
  50.9 4.1 %attention.1 = (bf16[192,1536]{1,0:T(8,128)(2,1)S(1)}, bf16[768,384]{1,0:T(8,128)(2,1)S(1)}) custom-call(bf16[96,1536]{1,0:T(8,128)(2,1)S(1)} %get-tuple-element.52.refs_0_, bf16[192,1536]{1,0:T(8,128)(2,1)S(1)} %get-tuple-element.58.refs_1_, bf16[192,1536]{1,0:T(8,128)(2,1)S(1)} %get-tuple-element.59.refs_2_, ...), custom_call_target="tpu_custom_call" | custom-call | flops 1358954496 | bytes 2359296 | tf_op jit(solution)/shard_map/attention/pallas_call | solution.py:443
  55.0 0.0 copy-start.1
  55.0 0.6 collective-permute-start.17
  55.6 1.1 %value_gradient.1 = f32[192,384]{1,0:T(8,128)} custom-call(bf16[768,384]{1,0:T(8,128)(2,1)S(1)} %get-tuple-element.71.dv_ref, bf16[96,192]{1,0:T(8,128)(2,1)S(1)} %get-tuple-element.72.refs_0_, bf16[192,192]{1,0:T(8,128)(2,1)S(1)} %get-tuple-element.73.refs_1_, bf16[192,192]{1,0:T(8,128)(2,1)S(1)} %get-tuple-element.74.refs_2_, ...), custom_call_target="tpu_custom_call" | custom-call | flops 113246208 | bytes 589824 | tf_op jit(solution)/shard_map/value_gradient/pallas_call | solution.py:597
  56.7 0.5 collective-permute-done.17.there_ref
  57.2 0.0 copy-done.1
  57.2 2.4 %finish.1 = (bf16[96,1536]{1,0:T(8,128)(2,1)}, bf16[96,1536]{1,0:T(8,128)(2,1)S(1)}, bf16[2,1536]{1,0:T(2,128)(2,1)S(1)}, bf16[2,384,1536]{2,1,0:T(8,128)(2,1)S(1)}) custom-call(bf16[96,1536]{1,0:T(8,128)(2,1)S(1)} %get-tuple-element.50.hidden_ref, f32[96,1536]{1,0:T(8,128)S(1)} %get-tuple-element.51.slope_ref, f32[1,1536]{1,0:T(1,128)S(1)} %reshape.21.gain_ref, ...), custom_call_target="tpu_custom_call" | custom-call | flops 5898240 | bytes 1769472 | tf_op jit(solution)/shard_map/finish/pallas_call | solution.py:516
  59.6 1.6 %collective-permute-start.18 = (bf16[2,1536]{1,0:T(2,128)(2,1)S(1)}, bf16[2,1536]{1,0:T(2,128)(2,1)S(1)}, u32[]{:S(2)}, u32[]{:S(2)}) collective-permute-start(bf16[2,1536]{1,0:T(2,128)(2,1)S(1)} %get-tuple-element.69), channel_id=1, source_target_pairs={{0,2},{2,0},{4,6},{6,4},{8,10},{10,8},{12,14},{14,12},{1,3},{3,1},... | collective-permute-start | bytes 18440 | tf_op jit(solution)/shard_map/ppermute | solution.py:682
  61.3 2.5 %collective-permute-start.19 = (bf16[2,1536]{1,0:T(2,128)(2,1)S(1)}, bf16[2,1536]{1,0:T(2,128)(2,1)S(1)}, u32[]{:S(2)}, u32[]{:S(2)}) collective-permute-start(bf16[2,1536]{1,0:T(2,128)(2,1)S(1)} %get-tuple-element.69), channel_id=1, source_target_pairs={{2,4},{6,8},{10,12},{4,2},{8,6},{12,10},{3,5},{7,9},{11,13},{5,3},... | collective-permute-start | bytes 18440 | tf_op jit(solution)/shard_map/ppermute | solution.py:682
  63.7 2.4 %back_mid.1 = (f32[96,768]{1,0:T(8,128)S(1)}, bf16[3,384,1536]{2,1,0:T(8,128)(2,1)S(1)}) custom-call(bf16[96,1536]{1,0:T(8,128)(2,1)S(1)} %get-tuple-element.66.pre_ref, bf16[2,384,1536]{2,1,0:T(8,128)(2,1)S(1)} %get-tuple-element.67.weight_ref, bf16[5,384,1536]{2,1,0:T(8,128)(2,1)} %taps_any.5), custom_call_target="tpu_custom_call" | custom-call | flops 226492416 | bytes 5898240 | tf_op jit(solution)/shard_map/back_mid/pallas_call | solution.py:543
  66.1 0.0 collective-permute-done.18.first_ref
  66.2 1.5 %collective-permute-done.19.second_ref = bf16[2,1536]{1,0:T(2,128)(2,1)S(1)} collective-permute-done((bf16[2,1536]{1,0:T(2,128)(2,1)S(1)}, bf16[2,1536]{1,0:T(2,128)(2,1)S(1)}, u32[]{:S(2)}, u32[]{:S(2)}) %collective-permute-start.19) | collective-permute-done | bytes 6176 | tf_op jit(solution)/shard_map/ppermute | solution.py:682
  67.7 2.0 %back_rest.1 = bf16[192,384]{1,0:T(8,128)(2,1)} custom-call(s32[1]{0:T(128)} %bitcast.1.place_ref, bf16[96,1536]{1,0:T(8,128)(2,1)S(1)} %get-tuple-element.66.pre_ref, f32[96,768]{1,0:T(8,128)S(1)} %get-tuple-element.68.mid_ref, bf16[2,1536]{1,0:T(2,128)(2,1)S(1)} %collective-permute-done.18.first_ref, ...), custom_call_target="tpu_custom_call" | custom-call | flops 339738624 | bytes 3538944 | tf_op jit(solution)/shard_map/back_rest/pallas_call | solution.py:574
  (2 shorter events, 0.0 us)
Async XLA Ops:
  1.4 8.5 %collective-permute-start = (bf16[3,384]{1,0:T(4,128)(2,1)S(1)}, bf16[3,384]{1,0:T(4,128)(2,1)S(1)}, u32[]{:S(2)}, u32[]{:S(2)}) collective-permute-start(bf16[3,384]{1,0:T(4,128)(2,1)S(1)} %edges.1), channel_id=1, source_target_pairs={{0,2},{2,0},{4,6},{6,4},{8,10},{10,8},{12,14},{14,12},{1,3},{3,1},... | collective-permute-start | bytes 6920 | tf_op jit(solution)/shard_map/ppermute | solution.py:638
  1.5 8.4 %collective-permute-start.1 = (bf16[3,384]{1,0:T(4,128)(2,1)S(1)}, bf16[3,384]{1,0:T(4,128)(2,1)S(1)}, u32[]{:S(2)}, u32[]{:S(2)}) collective-permute-start(bf16[3,384]{1,0:T(4,128)(2,1)S(1)} %edges.1), channel_id=1, source_target_pairs={{2,4},{6,8},{10,12},{4,2},{8,6},{12,10},{3,5},{7,9},{11,13},{5,3},... | collective-permute-start | bytes 6920 | tf_op jit(solution)/shard_map/ppermute | solution.py:638
  9.9 2.4 %copy-start.2 = (f32[1536]{0:T(1024)S(1)}, f32[1536]{0:T(1024)}, u32[]{:S(2)}) copy-start(f32[1536]{0:T(1024)} %param.11) | copy-start | bytes 18436
  9.9 2.4 %copy-start.3 = (f32[1536]{0:T(1024)S(1)}, f32[1536]{0:T(1024)}, u32[]{:S(2)}) copy-start(f32[1536]{0:T(1024)} %param.12) | copy-start | bytes 18436
  12.2 2.0 %collective-permute-start.2 = (bf16[96,1536]{1,0:T(8,128)(2,1)S(1)}, bf16[96,1536]{1,0:T(8,128)(2,1)S(1)}, u32[]{:S(2)}, u32[]{:S(2)}) collective-permute-start(bf16[96,1536]{1,0:T(8,128)(2,1)S(1)} %conv_edge.1.mine_ref), channel_id=1, source_target_pairs={{0,1},{1,0},{2,3},{3,2},{4,5},{5,4},{6,7},{7,6},{8,9},{9,8},{10,11... | collective-permute-start | bytes 884744 | tf_op jit(solution)/shard_map/ppermute | solution.py:642
  16.3 7.9 %collective-permute-start.3 = (bf16[288,384]{1,0:T(8,128)(2,1)S(1)}, bf16[288,384]{1,0:T(8,128)(2,1)S(1)}, u32[]{:S(2)}, u32[]{:S(2)}) collective-permute-start(bf16[288,384]{1,0:T(8,128)(2,1)S(1)} %get-tuple-element.40), channel_id=1, source_target_pairs={{0,4},{4,8},{8,12},{12,14},{14,10},{10,6},{6,2},{2,0},{1,5},{5,9},... | collective-permute-start | bytes 663560 | tf_op jit(solution)/shard_map/ppermute | solution.py:660
  16.4 7.9 %collective-permute-start.4 = (bf16[288,384]{1,0:T(8,128)(2,1)S(1)}, bf16[288,384]{1,0:T(8,128)(2,1)S(1)}, u32[]{:S(2)}, u32[]{:S(2)}) collective-permute-start(bf16[288,384]{1,0:T(8,128)(2,1)S(1)} %get-tuple-element.40), channel_id=1, source_target_pairs={{4,0},{8,4},{12,8},{14,12},{10,14},{6,10},{2,6},{0,2},{5,1},{9,5},... | collective-permute-start | bytes 663560 | tf_op jit(solution)/shard_map/ppermute | solution.py:660
  24.3 7.0 %collective-permute-start.5 = (bf16[288,384]{1,0:T(8,128)(2,1)S(1)}, bf16[288,384]{1,0:T(8,128)(2,1)S(1)}, u32[]{:S(2)}, u32[]{:S(2)}) collective-permute-start(bf16[288,384]{1,0:T(8,128)(2,1)S(1)} %collective-permute-done.3.refs_0_), channel_id=1, source_target_pairs={{0,4},{4,8},{8,12},{12,14},{14,10},{10,6},{6,2},{2,0},{1,5},{5,9},... | collective-permute-start | bytes 663560 | tf_op jit(solution)/shard_map/ppermute | solution.py:660
  25.4 6.4 %collective-permute-start.6 = (bf16[288,384]{1,0:T(8,128)(2,1)S(1)}, bf16[288,384]{1,0:T(8,128)(2,1)S(1)}, u32[]{:S(2)}, u32[]{:S(2)}) collective-permute-start(bf16[288,384]{1,0:T(8,128)(2,1)S(1)} %collective-permute-done.4.refs_1_), channel_id=1, source_target_pairs={{4,0},{8,4},{12,8},{14,12},{10,14},{6,10},{2,6},{0,2},{5,1},{9,5},... | collective-permute-start | bytes 663560 | tf_op jit(solution)/shard_map/ppermute | solution.py:660
  26.3 7.8 %collective-permute-start.9 = (bf16[288,384]{1,0:T(8,128)(2,1)S(1)}, bf16[288,384]{1,0:T(8,128)(2,1)S(1)}, u32[]{:S(2)}, u32[]{:S(2)}) collective-permute-start(bf16[288,384]{1,0:T(8,128)(2,1)S(1)} %collective-permute-done.3.refs_0_), channel_id=1, source_target_pairs={{0,1},{1,0},{2,3},{3,2},{4,5},{5,4},{6,7},{7,6},{8,9},{9,8},{10,11... | collective-permute-start | bytes 663560 | tf_op jit(solution)/shard_map/ppermute | solution.py:664
  26.3 8.2 %collective-permute-start.10 = (bf16[288,384]{1,0:T(8,128)(2,1)S(1)}, bf16[288,384]{1,0:T(8,128)(2,1)S(1)}, u32[]{:S(2)}, u32[]{:S(2)}) collective-permute-start(bf16[288,384]{1,0:T(8,128)(2,1)S(1)} %collective-permute-done.4.refs_1_), channel_id=1, source_target_pairs={{0,1},{1,0},{2,3},{3,2},{4,5},{5,4},{6,7},{7,6},{8,9},{9,8},{10,11... | collective-permute-start | bytes 663560 | tf_op jit(solution)/shard_map/ppermute | solution.py:664
  31.3 4.5 %collective-permute-start.11 = (bf16[288,384]{1,0:T(8,128)(2,1)S(1)}, bf16[288,384]{1,0:T(8,128)(2,1)S(1)}, u32[]{:S(2)}, u32[]{:S(2)}) collective-permute-start(bf16[288,384]{1,0:T(8,128)(2,1)S(1)} %collective-permute-done.5.refs_0_), channel_id=1, source_target_pairs={{0,1},{1,0},{2,3},{3,2},{4,5},{5,4},{6,7},{7,6},{8,9},{9,8},{10,11... | collective-permute-start | bytes 663560 | tf_op jit(solution)/shard_map/ppermute | solution.py:664
  31.9 3.9 %collective-permute-start.12 = (bf16[288,384]{1,0:T(8,128)(2,1)S(1)}, bf16[288,384]{1,0:T(8,128)(2,1)S(1)}, u32[]{:S(2)}, u32[]{:S(2)}) collective-permute-start(bf16[288,384]{1,0:T(8,128)(2,1)S(1)} %collective-permute-done.6.refs_1_), channel_id=1, source_target_pairs={{0,1},{1,0},{2,3},{3,2},{4,5},{5,4},{6,7},{7,6},{8,9},{9,8},{10,11... | collective-permute-start | bytes 663560 | tf_op jit(solution)/shard_map/ppermute | solution.py:664
  32.4 7.9 %collective-permute-start.7 = (bf16[288,384]{1,0:T(8,128)(2,1)S(1)}, bf16[288,384]{1,0:T(8,128)(2,1)S(1)}, u32[]{:S(2)}, u32[]{:S(2)}) collective-permute-start(bf16[288,384]{1,0:T(8,128)(2,1)S(1)} %collective-permute-done.5.refs_0_), channel_id=1, source_target_pairs={{0,4},{4,8},{8,12},{12,14},{14,10},{10,6},{6,2},{2,0},{1,5},{5,9},... | collective-permute-start | bytes 663560 | tf_op jit(solution)/shard_map/ppermute | solution.py:660
  34.0 7.6 %collective-permute-start.8 = (bf16[288,384]{1,0:T(8,128)(2,1)S(1)}, bf16[288,384]{1,0:T(8,128)(2,1)S(1)}, u32[]{:S(2)}, u32[]{:S(2)}) collective-permute-start(bf16[288,384]{1,0:T(8,128)(2,1)S(1)} %collective-permute-done.6.refs_1_), channel_id=1, source_target_pairs={{4,0},{8,4},{12,8},{14,12},{10,14},{6,10},{2,6},{0,2},{5,1},{9,5},... | collective-permute-start | bytes 663560 | tf_op jit(solution)/shard_map/ppermute | solution.py:660
  41.6 6.7 %collective-permute-start.15 = (bf16[288,384]{1,0:T(8,128)(2,1)S(1)}, bf16[288,384]{1,0:T(8,128)(2,1)S(1)}, u32[]{:S(2)}, u32[]{:S(2)}) collective-permute-start(bf16[288,384]{1,0:T(8,128)(2,1)S(1)} %collective-permute-done.7.refs_0_), channel_id=1, source_target_pairs={{0,4},{4,8},{8,12},{12,14},{14,10},{10,6},{6,2},{2,0},{1,5},{5,9},... | collective-permute-start | bytes 663560 | tf_op jit(solution)/shard_map/ppermute | solution.py:663
  43.2 5.2 %collective-permute-start.13 = (bf16[288,384]{1,0:T(8,128)(2,1)S(1)}, bf16[288,384]{1,0:T(8,128)(2,1)S(1)}, u32[]{:S(2)}, u32[]{:S(2)}) collective-permute-start(bf16[288,384]{1,0:T(8,128)(2,1)S(1)} %collective-permute-done.7.refs_0_), channel_id=1, source_target_pairs={{0,1},{1,0},{2,3},{3,2},{4,5},{5,4},{6,7},{7,6},{8,9},{9,8},{10,11... | collective-permute-start | bytes 663560 | tf_op jit(solution)/shard_map/ppermute | solution.py:664
  43.2 5.2 %collective-permute-start.14 = (bf16[288,384]{1,0:T(8,128)(2,1)S(1)}, bf16[288,384]{1,0:T(8,128)(2,1)S(1)}, u32[]{:S(2)}, u32[]{:S(2)}) collective-permute-start(bf16[288,384]{1,0:T(8,128)(2,1)S(1)} %collective-permute-done.8.refs_1_), channel_id=1, source_target_pairs={{0,1},{1,0},{2,3},{3,2},{4,5},{5,4},{6,7},{7,6},{8,9},{9,8},{10,11... | collective-permute-start | bytes 663560 | tf_op jit(solution)/shard_map/ppermute | solution.py:664
  48.3 1.5 %collective-permute-start.16 = (bf16[288,384]{1,0:T(8,128)(2,1)S(1)}, bf16[288,384]{1,0:T(8,128)(2,1)S(1)}, u32[]{:S(2)}, u32[]{:S(2)}) collective-permute-start(bf16[288,384]{1,0:T(8,128)(2,1)S(1)} %collective-permute-done.15.refs_0_), channel_id=1, source_target_pairs={{0,1},{1,0},{2,3},{3,2},{4,5},{5,4},{6,7},{7,6},{8,9},{9,8},{10,11... | collective-permute-start | bytes 663560 | tf_op jit(solution)/shard_map/ppermute | solution.py:664
  49.7 1.3 %copy-start = (bf16[384,1536]{1,0:T(8,128)(2,1)S(1)}, bf16[384,1536]{1,0:T(8,128)(2,1)}, u32[]{:S(2)}) copy-start(bf16[384,1536]{1,0:T(8,128)(2,1)} %refs_9_.1) | copy-start | bytes 3538948
  55.0 2.2 %copy-start.1 = (bf16[1,96,1536]{2,1,0:T(8,128)(2,1)S(1)}, bf16[1,96,1536]{2,1,0:T(8,128)(2,1)}, u32[]{:S(2)}) copy-start(bf16[1,96,1536]{2,1,0:T(8,128)(2,1)} %param.17) | copy-start | bytes 884740
  55.0 2.2 %collective-permute-start.17 = (bf16[192,1536]{1,0:T(8,128)(2,1)S(1)}, bf16[192,1536]{1,0:T(8,128)(2,1)S(1)}, u32[]{:S(2)}, u32[]{:S(2)}) collective-permute-start(bf16[192,1536]{1,0:T(8,128)(2,1)S(1)} %get-tuple-element.64.here_ref), channel_id=1, source_target_pairs={{0,1},{1,0},{2,3},{3,2},{4,5},{5,4},{6,7},{7,6},{8,9},{9,8},{10,11... | collective-permute-start | bytes 1769480 | tf_op jit(solution)/shard_map/ppermute | solution.py:677
  59.6 6.5 %collective-permute-start.18 = (bf16[2,1536]{1,0:T(2,128)(2,1)S(1)}, bf16[2,1536]{1,0:T(2,128)(2,1)S(1)}, u32[]{:S(2)}, u32[]{:S(2)}) collective-permute-start(bf16[2,1536]{1,0:T(2,128)(2,1)S(1)} %get-tuple-element.69), channel_id=1, source_target_pairs={{0,2},{2,0},{4,6},{6,4},{8,10},{10,8},{12,14},{14,12},{1,3},{3,1},... | collective-permute-start | bytes 18440 | tf_op jit(solution)/shard_map/ppermute | solution.py:682
  61.3 6.4 %collective-permute-start.19 = (bf16[2,1536]{1,0:T(2,128)(2,1)S(1)}, bf16[2,1536]{1,0:T(2,128)(2,1)S(1)}, u32[]{:S(2)}, u32[]{:S(2)}) collective-permute-start(bf16[2,1536]{1,0:T(2,128)(2,1)S(1)} %get-tuple-element.69), channel_id=1, source_target_pairs={{2,4},{6,8},{10,12},{4,2},{8,6},{12,10},{3,5},{7,9},{11,13},{5,3},... | collective-permute-start | bytes 18440 | tf_op jit(solution)/shard_map/ppermute | solution.py:682

commit v6 on v5

--- a/solution.py
+++ b/solution.py
@@ -386,7 +386,8 @@
         inv = 1.0 / jnp.sum(expo, 0, keepdims=True)
         delta = jnp.sum(expo * back, 0, keepdims=True) * inv
         prob_b = (expo * inv).astype(BF16)
-        score_own = (expo[:tok] * inv * (back[:tok] - delta) * scale).astype(BF16)
+        scaled = inv * scale
+        score_own = (expo[:tok] * scaled * (back[:tok] - delta)).astype(BF16)
         if tile == total:
             dv_ref[:, cols] = dot(prob_b, up).astype(BF16)
             dk_acc[:, cols] = dot(score_own, query)
@@ -399,7 +400,7 @@
 
         def own():
             att[:, cols] = dot_lt(prob_b[:, :lanes], val)[:tok].astype(BF16)
-            score = expo[:, :lanes] * inv[:, :lanes] * (back[:, :lanes] - delta[:, :lanes]) * scale
+            score = expo[:, :lanes] * scaled[:, :lanes] * (back[:, :lanes] - delta[:, :lanes])
             dq_acc[:, cols] = dot_lt(score.astype(BF16), key)[:tok]
 
         if first:

time: 70.1 us -> 70.1 us (level)
  no operation moved by 1% of the time
where the time goes in v6:
time: 70.1 us; the launch traced here: 69.7 us
  Pallas kernels  28.7 us (41%)
  waiting for transfers between devices  21.3 us (30%)
  starting transfers between devices  18.5 us (26%)
  between operations  0.91 us (1%)
    ppermute x6, waiting for transfers between devices, on_device(): cw, ccw = (lax.ppermute(cw, 'seq', ahead), lax.ppermute(ccw, 'seq', behind))  14.5 us
    ppermute x2, starting transfers between devices, on_device(): lax.ppermute(edge, 'seq', across)  7.39 us
    ppermute x6, starting transfers between devices, on_device(): cw, ccw = (lax.ppermute(cw, 'seq', ahead), lax.ppermute(ccw, 'seq', behind))  6.17 us
    pallas_call x4, Pallas kernels, others_project(): pl.pallas_call(functools.partial(others_kernel, len(mine), half), out_sha...  4.79 us
    ppermute x1, waiting for transfers between devices, on_device(): blocks = [lax.ppermute(cw, 'seq', ahead)]  4.66 us
    pallas_call x1, Pallas kernels, attention(): pl.pallas_call(functools.partial(attention_kernel, tok, tile, heads, qkv_...  4.08 us
    pallas_call x1, Pallas kernels, conv_inner(): pl.pallas_call(functools.partial(conv_kernel, tuple(range(taps))), out_sh...  3.47 us
    pallas_call x1, Pallas kernels, back_mid(): pl.pallas_call(back_mid_kernel, out_shape=[jax.ShapeDtypeStruct((tok, 2 *...  2.4 us
  transfers between devices with their start and end apart: 20, of which 10 were waited for; matrix products, arithmetic and copies ran while one was open for 0% of the time, Pallas kernels for 20%

profile of v6, /device:TPU:4, one launch (start us, length us, event | category | flops | bytes accessed | tf_op | source)
XLA Modules:
  0.0 69.7 jit_solution(6387251662359172865)
XLA Ops:
  0.6 0.8 %edges.1 = bf16[3,384]{1,0:T(4,128)(2,1)S(1)} custom-call(bf16[192,384]{1,0:T(8,128)(2,1)} %bitcast.9), custom_call_target="tpu_custom_call" | custom-call | flops 384 | bytes 24576 | tf_op jit(solution)/shard_map/edges/pallas_call | solution.py:86
  1.4 0.1 collective-permute-start
  1.5 4.9 %collective-permute-start.1 = (bf16[3,384]{1,0:T(4,128)(2,1)S(1)}, bf16[3,384]{1,0:T(4,128)(2,1)S(1)}, u32[]{:S(2)}, u32[]{:S(2)}) collective-permute-start(bf16[3,384]{1,0:T(4,128)(2,1)S(1)} %edges.1), channel_id=1, source_target_pairs={{2,4},{6,8},{10,12},{4,2},{8,6},{12,10},{3,5},{7,9},{11,13},{5,3},... | collective-permute-start | bytes 6920 | tf_op jit(solution)/shard_map/ppermute | solution.py:639
  6.4 3.5 %conv_inner.1.inner_ref = f32[96,1536]{1,0:T(8,128)S(1)} custom-call(bf16[192,384]{1,0:T(8,128)(2,1)} %bitcast.10, bf16[5,384,1536]{2,1,0:T(8,128)(2,1)} %taps_any.5), custom_call_target="tpu_custom_call" | custom-call | flops 566231040 | bytes 5898240 | tf_op jit(solution)/shard_map/conv_inner/pallas_call | solution.py:162
  9.9 0.0 collective-permute-done.first_ref
  9.9 0.0 collective-permute-done.1.second_ref
  9.9 0.0 copy-start.2
  9.9 0.0 copy-start.3
  9.9 2.3 %conv_edge.1.mine_ref = bf16[96,1536]{1,0:T(8,128)(2,1)S(1)} custom-call(s32[1]{0:T(128)} %bitcast.1.place_ref, f32[96,1536]{1,0:T(8,128)S(1)} %conv_inner.1.inner_ref, bf16[3,384]{1,0:T(4,128)(2,1)S(1)} %collective-permute-done.first_ref, bf16[3,384]{1,0:T(4,128)(2,1)S(1)} %collective-permute-done.1.second_ref, bf16[5,384,1536]{2,1,0:T(8,128)(2,1)} %taps_any.5), custom_call_target="tpu_custom_call" | custom-call | flops 56623104 | bytes 3538944 | tf_op jit(solution)/shard_map/conv_edge/pallas_call | solution.py:199
  12.2 0.1 collective-permute-start.2
  12.3 0.0 copy-done.2
  12.4 0.0 copy-done.3
  12.4 1.9 %early.1.refs_3_.grad_ref = bf16[96,384]{1,0:T(8,128)(2,1)S(1)} custom-call(bf16[96,1536]{1,0:T(8,128)(2,1)} %bitcast.7, bf16[384,1536]{1,0:T(8,128)(2,1)} %refs_9_.1), custom_call_target="tpu_custom_call" | custom-call | flops 113246208 | bytes 1179648 | tf_op jit(solution)/shard_map/early/pallas_call | solution.py:124
  14.3 0.0 collective-permute-done.2.theirs_ref
  14.3 2.0 %norm.1 = (bf16[96,1536]{1,0:T(8,128)(2,1)S(1)}, bf16[288,384]{1,0:T(8,128)(2,1)S(1)}, bf16[1536,384]{1,0:T(8,128)(2,1)S(1)}, bf16[1536,384]{1,0:T(8,128)(2,1)S(1)}, bf16[1536,384]{1,0:T(8,128)(2,1)S(1)}) custom-call(s32[1]{0:T(128)} %bitcast.wide_ref, bf16[96,1536]{1,0:T(8,128)(2,1)S(1)} %conv_edge.1.mine_ref, ...), custom_call_target="tpu_custom_call" | custom-call | flops 4423680 | bytes 884736 | tf_op jit(solution)/shard_map/norm/pallas_call | solution.py:268
  16.3 0.1 collective-permute-start.3
  16.4 2.0 %collective-permute-start.4 = (bf16[288,384]{1,0:T(8,128)(2,1)S(1)}, bf16[288,384]{1,0:T(8,128)(2,1)S(1)}, u32[]{:S(2)}, u32[]{:S(2)}) collective-permute-start(bf16[288,384]{1,0:T(8,128)(2,1)S(1)} %get-tuple-element.40), channel_id=1, source_target_pairs={{4,0},{8,4},{12,8},{14,12},{10,14},{6,10},{2,6},{0,2},{5,1},{9,5},... | collective-permute-start | bytes 663560 | tf_op jit(solution)/shard_map/ppermute | solution.py:661
  18.4 0.9 %own_project.1 = (bf16[96,1536]{1,0:T(8,128)(2,1)S(1)}, bf16[96,192]{1,0:T(8,128)(2,1)S(1)}, f32[96,768]{1,0:T(8,128)S(1)}, bf16[1536,192]{1,0:T(8,128)(2,1)S(1)}) custom-call(s32[1]{0:T(128)} %bitcast.1.place_ref, bf16[96,1536]{1,0:T(8,128)(2,1)S(1)} %get-tuple-element.41.normed_ref, bf16[96,384]{1,0:T(8,128)(2,1)S(1)} %early.1.refs_3_.grad_ref, ...), custom_call_target="tpu_custom_call" | custom-call | flops 339738624 | bytes 3538944 | tf_op jit(solution)/shard_map/own_project/pallas_call | solution.py:307
  19.3 4.9 %collective-permute-done.3.refs_0_ = bf16[288,384]{1,0:T(8,128)(2,1)S(1)} collective-permute-done((bf16[288,384]{1,0:T(8,128)(2,1)S(1)}, bf16[288,384]{1,0:T(8,128)(2,1)S(1)}, u32[]{:S(2)}, u32[]{:S(2)}) %collective-permute-start.3) | collective-permute-done | bytes 221216 | tf_op jit(solution)/shard_map/ppermute | solution.py:661
  24.2 0.1 collective-permute-done.4.refs_1_
  24.3 1.2 %collective-permute-start.5 = (bf16[288,384]{1,0:T(8,128)(2,1)S(1)}, bf16[288,384]{1,0:T(8,128)(2,1)S(1)}, u32[]{:S(2)}, u32[]{:S(2)}) collective-permute-start(bf16[288,384]{1,0:T(8,128)(2,1)S(1)} %collective-permute-done.3.refs_0_), channel_id=1, source_target_pairs={{0,4},{4,8},{8,12},{12,14},{14,10},{10,6},{6,2},{2,0},{1,5},{5,9},... | collective-permute-start | bytes 663560 | tf_op jit(solution)/shard_map/ppermute | solution.py:661
  25.4 0.8 %collective-permute-start.6 = (bf16[288,384]{1,0:T(8,128)(2,1)S(1)}, bf16[288,384]{1,0:T(8,128)(2,1)S(1)}, u32[]{:S(2)}, u32[]{:S(2)}) collective-permute-start(bf16[288,384]{1,0:T(8,128)(2,1)S(1)} %collective-permute-done.4.refs_1_), channel_id=1, source_target_pairs={{4,0},{8,4},{12,8},{14,12},{10,14},{6,10},{2,6},{0,2},{5,1},{9,5},... | collective-permute-start | bytes 663560 | tf_op jit(solution)/shard_map/ppermute | solution.py:661
  26.3 0.0 collective-permute-start.9
  26.3 0.5 collective-permute-start.10
  26.8 4.5 %collective-permute-done.5.refs_0_ = bf16[288,384]{1,0:T(8,128)(2,1)S(1)} collective-permute-done((bf16[288,384]{1,0:T(8,128)(2,1)S(1)}, bf16[288,384]{1,0:T(8,128)(2,1)S(1)}, u32[]{:S(2)}, u32[]{:S(2)}) %collective-permute-start.5) | collective-permute-done | bytes 221216 | tf_op jit(solution)/shard_map/ppermute | solution.py:661
  31.3 0.0 collective-permute-start.11
  31.3 0.6 collective-permute-done.6.refs_1_
  31.9 0.0 collective-permute-start.12
  31.9 0.5 local_terms.1
  32.4 1.6 %collective-permute-start.7 = (bf16[288,384]{1,0:T(8,128)(2,1)S(1)}, bf16[288,384]{1,0:T(8,128)(2,1)S(1)}, u32[]{:S(2)}, u32[]{:S(2)}) collective-permute-start(bf16[288,384]{1,0:T(8,128)(2,1)S(1)} %collective-permute-done.5.refs_0_), channel_id=1, source_target_pairs={{0,4},{4,8},{8,12},{12,14},{14,10},{10,6},{6,2},{2,0},{1,5},{5,9},... | collective-permute-start | bytes 663560 | tf_op jit(solution)/shard_map/ppermute | solution.py:661
  34.0 0.0 collective-permute-done.9.refs_2_
  34.0 0.4 collective-permute-start.8
  34.5 0.0 collective-permute-done.10.refs_3_
  34.5 1.3 %others_project.4 = (bf16[192,1536]{1,0:T(8,128)(2,1)S(1)}, bf16[192,192]{1,0:T(8,128)(2,1)S(1)}) custom-call(s32[1]{0:T(128)} %bitcast.wide_ref, bf16[1536,192]{1,0:T(8,128)(2,1)S(1)} %get-tuple-element.55.chosen_ref, bf16[288,384]{1,0:T(8,128)(2,1)S(1)} %collective-permute-done.3.refs_0_, bf16[288,384]{1,0:T(8,128)(2,1)S(1)} %collective-permute-done.4.refs_1_, ...), custom_call_target="tpu_custom_call" | custom-call | flops 679477248 | bytes 3538944 | tf_op jit(solution)/shard_map/others_project/pallas_call | solution.py:340
  35.8 0.0 collective-permute-done.11.refs_2_
  35.8 0.0 collective-permute-done.12.refs_3_
  35.8 1.3 %others_project.5 = (bf16[192,1536]{1,0:T(8,128)(2,1)S(1)}, bf16[192,192]{1,0:T(8,128)(2,1)S(1)}) custom-call(s32[1]{0:T(128)} %bitcast.wide_ref, bf16[1536,192]{1,0:T(8,128)(2,1)S(1)} %get-tuple-element.55.chosen_ref, bf16[288,384]{1,0:T(8,128)(2,1)S(1)} %collective-permute-done.5.refs_0_, bf16[288,384]{1,0:T(8,128)(2,1)S(1)} %collective-permute-done.6.refs_1_, ...), custom_call_target="tpu_custom_call" | custom-call | flops 679477248 | bytes 3538944 | tf_op jit(solution)/shard_map/others_project/pallas_call | solution.py:340
  37.1 3.1 %collective-permute-done.7.refs_0_ = bf16[288,384]{1,0:T(8,128)(2,1)S(1)} collective-permute-done((bf16[288,384]{1,0:T(8,128)(2,1)S(1)}, bf16[288,384]{1,0:T(8,128)(2,1)S(1)}, u32[]{:S(2)}, u32[]{:S(2)}) %collective-permute-start.7) | collective-permute-done | bytes 221216 | tf_op jit(solution)/shard_map/ppermute | solution.py:661
  40.3 1.3 %collective-permute-done.8.refs_1_ = bf16[288,384]{1,0:T(8,128)(2,1)S(1)} collective-permute-done((bf16[288,384]{1,0:T(8,128)(2,1)S(1)}, bf16[288,384]{1,0:T(8,128)(2,1)S(1)}, u32[]{:S(2)}, u32[]{:S(2)}) %collective-permute-start.8) | collective-permute-done | bytes 221216 | tf_op jit(solution)/shard_map/ppermute | solution.py:661
  41.6 1.6 %collective-permute-start.15 = (bf16[288,384]{1,0:T(8,128)(2,1)S(1)}, bf16[288,384]{1,0:T(8,128)(2,1)S(1)}, u32[]{:S(2)}, u32[]{:S(2)}) collective-permute-start(bf16[288,384]{1,0:T(8,128)(2,1)S(1)} %collective-permute-done.7.refs_0_), channel_id=1, source_target_pairs={{0,4},{4,8},{8,12},{12,14},{14,10},{10,6},{6,2},{2,0},{1,5},{5,9},... | collective-permute-start | bytes 663560 | tf_op jit(solution)/shard_map/ppermute | solution.py:664
  43.2 0.0 collective-permute-start.13
  43.2 0.5 collective-permute-start.14
  43.7 4.7 %collective-permute-done.15.refs_0_ = bf16[288,384]{1,0:T(8,128)(2,1)S(1)} collective-permute-done((bf16[288,384]{1,0:T(8,128)(2,1)S(1)}, bf16[288,384]{1,0:T(8,128)(2,1)S(1)}, u32[]{:S(2)}, u32[]{:S(2)}) %collective-permute-start.15) | collective-permute-done | bytes 221216 | tf_op jit(solution)/shard_map/ppermute | solution.py:664
  48.3 0.0 collective-permute-start.16
  48.3 0.0 collective-permute-done.13.refs_2_
  48.3 0.0 collective-permute-done.14.refs_3_
  48.4 1.3 %others_project.6 = (bf16[192,1536]{1,0:T(8,128)(2,1)S(1)}, bf16[192,192]{1,0:T(8,128)(2,1)S(1)}) custom-call(s32[1]{0:T(128)} %bitcast.wide_ref, bf16[1536,192]{1,0:T(8,128)(2,1)S(1)} %get-tuple-element.55.chosen_ref, bf16[288,384]{1,0:T(8,128)(2,1)S(1)} %collective-permute-done.7.refs_0_, bf16[288,384]{1,0:T(8,128)(2,1)S(1)} %collective-permute-done.8.refs_1_, ...), custom_call_target="tpu_custom_call" | custom-call | flops 679477248 | bytes 3538944 | tf_op jit(solution)/shard_map/others_project/pallas_call | solution.py:340
  49.7 0.0 copy-start
  49.7 0.1 collective-permute-done.16.refs_1_
  49.8 0.9 %others_project.7 = (bf16[96,1536]{1,0:T(8,128)(2,1)S(1)}, bf16[96,192]{1,0:T(8,128)(2,1)S(1)}) custom-call(s32[1]{0:T(128)} %bitcast.wide_ref, bf16[1536,192]{1,0:T(8,128)(2,1)S(1)} %get-tuple-element.55.chosen_ref, bf16[288,384]{1,0:T(8,128)(2,1)S(1)} %collective-permute-done.15.refs_0_, bf16[288,384]{1,0:T(8,128)(2,1)S(1)} %collective-permute-done.16.refs_1_, ...), custom_call_target="tpu_custom_call" | custom-call | flops 339738624 | bytes 3538944 | tf_op jit(solution)/shard_map/others_project/pallas_call | solution.py:340
  50.7 0.2 copy-done
  50.9 4.1 %attention.1 = (bf16[192,1536]{1,0:T(8,128)(2,1)S(1)}, bf16[768,384]{1,0:T(8,128)(2,1)S(1)}) custom-call(bf16[96,1536]{1,0:T(8,128)(2,1)S(1)} %get-tuple-element.52.refs_0_, bf16[192,1536]{1,0:T(8,128)(2,1)S(1)} %get-tuple-element.58.refs_1_, bf16[192,1536]{1,0:T(8,128)(2,1)S(1)} %get-tuple-element.59.refs_2_, ...), custom_call_target="tpu_custom_call" | custom-call | flops 1358954496 | bytes 2359296 | tf_op jit(solution)/shard_map/attention/pallas_call | solution.py:444
  55.0 0.0 copy-start.1
  55.0 0.6 collective-permute-start.17
  55.6 1.2 %value_gradient.1 = f32[192,384]{1,0:T(8,128)} custom-call(bf16[768,384]{1,0:T(8,128)(2,1)S(1)} %get-tuple-element.71.dv_ref, bf16[96,192]{1,0:T(8,128)(2,1)S(1)} %get-tuple-element.72.refs_0_, bf16[192,192]{1,0:T(8,128)(2,1)S(1)} %get-tuple-element.73.refs_1_, bf16[192,192]{1,0:T(8,128)(2,1)S(1)} %get-tuple-element.74.refs_2_, ...), custom_call_target="tpu_custom_call" | custom-call | flops 113246208 | bytes 589824 | tf_op jit(solution)/shard_map/value_gradient/pallas_call | solution.py:598
  56.8 0.5 collective-permute-done.17.there_ref
  57.2 0.0 copy-done.1
  57.2 2.4 %finish.1 = (bf16[96,1536]{1,0:T(8,128)(2,1)}, bf16[96,1536]{1,0:T(8,128)(2,1)S(1)}, bf16[2,1536]{1,0:T(2,128)(2,1)S(1)}, bf16[2,384,1536]{2,1,0:T(8,128)(2,1)S(1)}) custom-call(bf16[96,1536]{1,0:T(8,128)(2,1)S(1)} %get-tuple-element.50.hidden_ref, f32[96,1536]{1,0:T(8,128)S(1)} %get-tuple-element.51.slope_ref, f32[1,1536]{1,0:T(1,128)S(1)} %reshape.21.gain_ref, ...), custom_call_target="tpu_custom_call" | custom-call | flops 5898240 | bytes 1769472 | tf_op jit(solution)/shard_map/finish/pallas_call | solution.py:517
  59.6 1.6 %collective-permute-start.18 = (bf16[2,1536]{1,0:T(2,128)(2,1)S(1)}, bf16[2,1536]{1,0:T(2,128)(2,1)S(1)}, u32[]{:S(2)}, u32[]{:S(2)}) collective-permute-start(bf16[2,1536]{1,0:T(2,128)(2,1)S(1)} %get-tuple-element.69), channel_id=1, source_target_pairs={{0,2},{2,0},{4,6},{6,4},{8,10},{10,8},{12,14},{14,12},{1,3},{3,1},... | collective-permute-start | bytes 18440 | tf_op jit(solution)/shard_map/ppermute | solution.py:683
  61.3 2.5 %collective-permute-start.19 = (bf16[2,1536]{1,0:T(2,128)(2,1)S(1)}, bf16[2,1536]{1,0:T(2,128)(2,1)S(1)}, u32[]{:S(2)}, u32[]{:S(2)}) collective-permute-start(bf16[2,1536]{1,0:T(2,128)(2,1)S(1)} %get-tuple-element.69), channel_id=1, source_target_pairs={{2,4},{6,8},{10,12},{4,2},{8,6},{12,10},{3,5},{7,9},{11,13},{5,3},... | collective-permute-start | bytes 18440 | tf_op jit(solution)/shard_map/ppermute | solution.py:683
  63.8 2.4 %back_mid.1 = (f32[96,768]{1,0:T(8,128)S(1)}, bf16[3,384,1536]{2,1,0:T(8,128)(2,1)S(1)}) custom-call(bf16[96,1536]{1,0:T(8,128)(2,1)S(1)} %get-tuple-element.66.pre_ref, bf16[2,384,1536]{2,1,0:T(8,128)(2,1)S(1)} %get-tuple-element.67.weight_ref, bf16[5,384,1536]{2,1,0:T(8,128)(2,1)} %taps_any.5), custom_call_target="tpu_custom_call" | custom-call | flops 226492416 | bytes 5898240 | tf_op jit(solution)/shard_map/back_mid/pallas_call | solution.py:544
  66.2 0.0 collective-permute-done.18.first_ref
  66.2 1.5 %collective-permute-done.19.second_ref = bf16[2,1536]{1,0:T(2,128)(2,1)S(1)} collective-permute-done((bf16[2,1536]{1,0:T(2,128)(2,1)S(1)}, bf16[2,1536]{1,0:T(2,128)(2,1)S(1)}, u32[]{:S(2)}, u32[]{:S(2)}) %collective-permute-start.19) | collective-permute-done | bytes 6176 | tf_op jit(solution)/shard_map/ppermute | solution.py:683
  67.7 2.0 %back_rest.1 = bf16[192,384]{1,0:T(8,128)(2,1)} custom-call(s32[1]{0:T(128)} %bitcast.1.place_ref, bf16[96,1536]{1,0:T(8,128)(2,1)S(1)} %get-tuple-element.66.pre_ref, f32[96,768]{1,0:T(8,128)S(1)} %get-tuple-element.68.mid_ref, bf16[2,1536]{1,0:T(2,128)(2,1)S(1)} %collective-permute-done.18.first_ref, ...), custom_call_target="tpu_custom_call" | custom-call | flops 339738624 | bytes 3538944 | tf_op jit(solution)/shard_map/back_rest/pallas_call | solution.py:575
  (2 shorter events, 0.0 us)
Async XLA Ops:
  1.4 8.5 %collective-permute-start = (bf16[3,384]{1,0:T(4,128)(2,1)S(1)}, bf16[3,384]{1,0:T(4,128)(2,1)S(1)}, u32[]{:S(2)}, u32[]{:S(2)}) collective-permute-start(bf16[3,384]{1,0:T(4,128)(2,1)S(1)} %edges.1), channel_id=1, source_target_pairs={{0,2},{2,0},{4,6},{6,4},{8,10},{10,8},{12,14},{14,12},{1,3},{3,1},... | collective-permute-start | bytes 6920 | tf_op jit(solution)/shard_map/ppermute | solution.py:639
  1.5 8.4 %collective-permute-start.1 = (bf16[3,384]{1,0:T(4,128)(2,1)S(1)}, bf16[3,384]{1,0:T(4,128)(2,1)S(1)}, u32[]{:S(2)}, u32[]{:S(2)}) collective-permute-start(bf16[3,384]{1,0:T(4,128)(2,1)S(1)} %edges.1), channel_id=1, source_target_pairs={{2,4},{6,8},{10,12},{4,2},{8,6},{12,10},{3,5},{7,9},{11,13},{5,3},... | collective-permute-start | bytes 6920 | tf_op jit(solution)/shard_map/ppermute | solution.py:639
  9.9 2.4 %copy-start.2 = (f32[1536]{0:T(1024)S(1)}, f32[1536]{0:T(1024)}, u32[]{:S(2)}) copy-start(f32[1536]{0:T(1024)} %param.11) | copy-start | bytes 18436
  9.9 2.4 %copy-start.3 = (f32[1536]{0:T(1024)S(1)}, f32[1536]{0:T(1024)}, u32[]{:S(2)}) copy-start(f32[1536]{0:T(1024)} %param.12) | copy-start | bytes 18436
  12.2 2.0 %collective-permute-start.2 = (bf16[96,1536]{1,0:T(8,128)(2,1)S(1)}, bf16[96,1536]{1,0:T(8,128)(2,1)S(1)}, u32[]{:S(2)}, u32[]{:S(2)}) collective-permute-start(bf16[96,1536]{1,0:T(8,128)(2,1)S(1)} %conv_edge.1.mine_ref), channel_id=1, source_target_pairs={{0,1},{1,0},{2,3},{3,2},{4,5},{5,4},{6,7},{7,6},{8,9},{9,8},{10,11... | collective-permute-start | bytes 884744 | tf_op jit(solution)/shard_map/ppermute | solution.py:643
  16.3 7.9 %collective-permute-start.3 = (bf16[288,384]{1,0:T(8,128)(2,1)S(1)}, bf16[288,384]{1,0:T(8,128)(2,1)S(1)}, u32[]{:S(2)}, u32[]{:S(2)}) collective-permute-start(bf16[288,384]{1,0:T(8,128)(2,1)S(1)} %get-tuple-element.40), channel_id=1, source_target_pairs={{0,4},{4,8},{8,12},{12,14},{14,10},{10,6},{6,2},{2,0},{1,5},{5,9},... | collective-permute-start | bytes 663560 | tf_op jit(solution)/shard_map/ppermute | solution.py:661
  16.4 7.9 %collective-permute-start.4 = (bf16[288,384]{1,0:T(8,128)(2,1)S(1)}, bf16[288,384]{1,0:T(8,128)(2,1)S(1)}, u32[]{:S(2)}, u32[]{:S(2)}) collective-permute-start(bf16[288,384]{1,0:T(8,128)(2,1)S(1)} %get-tuple-element.40), channel_id=1, source_target_pairs={{4,0},{8,4},{12,8},{14,12},{10,14},{6,10},{2,6},{0,2},{5,1},{9,5},... | collective-permute-start | bytes 663560 | tf_op jit(solution)/shard_map/ppermute | solution.py:661
  24.3 7.0 %collective-permute-start.5 = (bf16[288,384]{1,0:T(8,128)(2,1)S(1)}, bf16[288,384]{1,0:T(8,128)(2,1)S(1)}, u32[]{:S(2)}, u32[]{:S(2)}) collective-permute-start(bf16[288,384]{1,0:T(8,128)(2,1)S(1)} %collective-permute-done.3.refs_0_), channel_id=1, source_target_pairs={{0,4},{4,8},{8,12},{12,14},{14,10},{10,6},{6,2},{2,0},{1,5},{5,9},... | collective-permute-start | bytes 663560 | tf_op jit(solution)/shard_map/ppermute | solution.py:661
  25.4 6.4 %collective-permute-start.6 = (bf16[288,384]{1,0:T(8,128)(2,1)S(1)}, bf16[288,384]{1,0:T(8,128)(2,1)S(1)}, u32[]{:S(2)}, u32[]{:S(2)}) collective-permute-start(bf16[288,384]{1,0:T(8,128)(2,1)S(1)} %collective-permute-done.4.refs_1_), channel_id=1, source_target_pairs={{4,0},{8,4},{12,8},{14,12},{10,14},{6,10},{2,6},{0,2},{5,1},{9,5},... | collective-permute-start | bytes 663560 | tf_op jit(solution)/shard_map/ppermute | solution.py:661
  26.3 7.8 %collective-permute-start.9 = (bf16[288,384]{1,0:T(8,128)(2,1)S(1)}, bf16[288,384]{1,0:T(8,128)(2,1)S(1)}, u32[]{:S(2)}, u32[]{:S(2)}) collective-permute-start(bf16[288,384]{1,0:T(8,128)(2,1)S(1)} %collective-permute-done.3.refs_0_), channel_id=1, source_target_pairs={{0,1},{1,0},{2,3},{3,2},{4,5},{5,4},{6,7},{7,6},{8,9},{9,8},{10,11... | collective-permute-start | bytes 663560 | tf_op jit(solution)/shard_map/ppermute | solution.py:665
  26.3 8.2 %collective-permute-start.10 = (bf16[288,384]{1,0:T(8,128)(2,1)S(1)}, bf16[288,384]{1,0:T(8,128)(2,1)S(1)}, u32[]{:S(2)}, u32[]{:S(2)}) collective-permute-start(bf16[288,384]{1,0:T(8,128)(2,1)S(1)} %collective-permute-done.4.refs_1_), channel_id=1, source_target_pairs={{0,1},{1,0},{2,3},{3,2},{4,5},{5,4},{6,7},{7,6},{8,9},{9,8},{10,11... | collective-permute-start | bytes 663560 | tf_op jit(solution)/shard_map/ppermute | solution.py:665
  31.3 4.5 %collective-permute-start.11 = (bf16[288,384]{1,0:T(8,128)(2,1)S(1)}, bf16[288,384]{1,0:T(8,128)(2,1)S(1)}, u32[]{:S(2)}, u32[]{:S(2)}) collective-permute-start(bf16[288,384]{1,0:T(8,128)(2,1)S(1)} %collective-permute-done.5.refs_0_), channel_id=1, source_target_pairs={{0,1},{1,0},{2,3},{3,2},{4,5},{5,4},{6,7},{7,6},{8,9},{9,8},{10,11... | collective-permute-start | bytes 663560 | tf_op jit(solution)/shard_map/ppermute | solution.py:665
  31.9 3.9 %collective-permute-start.12 = (bf16[288,384]{1,0:T(8,128)(2,1)S(1)}, bf16[288,384]{1,0:T(8,128)(2,1)S(1)}, u32[]{:S(2)}, u32[]{:S(2)}) collective-permute-start(bf16[288,384]{1,0:T(8,128)(2,1)S(1)} %collective-permute-done.6.refs_1_), channel_id=1, source_target_pairs={{0,1},{1,0},{2,3},{3,2},{4,5},{5,4},{6,7},{7,6},{8,9},{9,8},{10,11... | collective-permute-start | bytes 663560 | tf_op jit(solution)/shard_map/ppermute | solution.py:665
  32.4 7.9 %collective-permute-start.7 = (bf16[288,384]{1,0:T(8,128)(2,1)S(1)}, bf16[288,384]{1,0:T(8,128)(2,1)S(1)}, u32[]{:S(2)}, u32[]{:S(2)}) collective-permute-start(bf16[288,384]{1,0:T(8,128)(2,1)S(1)} %collective-permute-done.5.refs_0_), channel_id=1, source_target_pairs={{0,4},{4,8},{8,12},{12,14},{14,10},{10,6},{6,2},{2,0},{1,5},{5,9},... | collective-permute-start | bytes 663560 | tf_op jit(solution)/shard_map/ppermute | solution.py:661
  34.0 7.6 %collective-permute-start.8 = (bf16[288,384]{1,0:T(8,128)(2,1)S(1)}, bf16[288,384]{1,0:T(8,128)(2,1)S(1)}, u32[]{:S(2)}, u32[]{:S(2)}) collective-permute-start(bf16[288,384]{1,0:T(8,128)(2,1)S(1)} %collective-permute-done.6.refs_1_), channel_id=1, source_target_pairs={{4,0},{8,4},{12,8},{14,12},{10,14},{6,10},{2,6},{0,2},{5,1},{9,5},... | collective-permute-start | bytes 663560 | tf_op jit(solution)/shard_map/ppermute | solution.py:661
  41.6 6.7 %collective-permute-start.15 = (bf16[288,384]{1,0:T(8,128)(2,1)S(1)}, bf16[288,384]{1,0:T(8,128)(2,1)S(1)}, u32[]{:S(2)}, u32[]{:S(2)}) collective-permute-start(bf16[288,384]{1,0:T(8,128)(2,1)S(1)} %collective-permute-done.7.refs_0_), channel_id=1, source_target_pairs={{0,4},{4,8},{8,12},{12,14},{14,10},{10,6},{6,2},{2,0},{1,5},{5,9},... | collective-permute-start | bytes 663560 | tf_op jit(solution)/shard_map/ppermute | solution.py:664
  43.2 5.2 %collective-permute-start.13 = (bf16[288,384]{1,0:T(8,128)(2,1)S(1)}, bf16[288,384]{1,0:T(8,128)(2,1)S(1)}, u32[]{:S(2)}, u32[]{:S(2)}) collective-permute-start(bf16[288,384]{1,0:T(8,128)(2,1)S(1)} %collective-permute-done.7.refs_0_), channel_id=1, source_target_pairs={{0,1},{1,0},{2,3},{3,2},{4,5},{5,4},{6,7},{7,6},{8,9},{9,8},{10,11... | collective-permute-start | bytes 663560 | tf_op jit(solution)/shard_map/ppermute | solution.py:665
  43.2 5.2 %collective-permute-start.14 = (bf16[288,384]{1,0:T(8,128)(2,1)S(1)}, bf16[288,384]{1,0:T(8,128)(2,1)S(1)}, u32[]{:S(2)}, u32[]{:S(2)}) collective-permute-start(bf16[288,384]{1,0:T(8,128)(2,1)S(1)} %collective-permute-done.8.refs_1_), channel_id=1, source_target_pairs={{0,1},{1,0},{2,3},{3,2},{4,5},{5,4},{6,7},{7,6},{8,9},{9,8},{10,11... | collective-permute-start | bytes 663560 | tf_op jit(solution)/shard_map/ppermute | solution.py:665
  48.3 1.5 %collective-permute-start.16 = (bf16[288,384]{1,0:T(8,128)(2,1)S(1)}, bf16[288,384]{1,0:T(8,128)(2,1)S(1)}, u32[]{:S(2)}, u32[]{:S(2)}) collective-permute-start(bf16[288,384]{1,0:T(8,128)(2,1)S(1)} %collective-permute-done.15.refs_0_), channel_id=1, source_target_pairs={{0,1},{1,0},{2,3},{3,2},{4,5},{5,4},{6,7},{7,6},{8,9},{9,8},{10,11... | collective-permute-start | bytes 663560 | tf_op jit(solution)/shard_map/ppermute | solution.py:665
  49.7 1.3 %copy-start = (bf16[384,1536]{1,0:T(8,128)(2,1)S(1)}, bf16[384,1536]{1,0:T(8,128)(2,1)}, u32[]{:S(2)}) copy-start(bf16[384,1536]{1,0:T(8,128)(2,1)} %refs_9_.1) | copy-start | bytes 3538948
  55.0 2.2 %copy-start.1 = (bf16[1,96,1536]{2,1,0:T(8,128)(2,1)S(1)}, bf16[1,96,1536]{2,1,0:T(8,128)(2,1)}, u32[]{:S(2)}) copy-start(bf16[1,96,1536]{2,1,0:T(8,128)(2,1)} %param.17) | copy-start | bytes 884740
  55.0 2.2 %collective-permute-start.17 = (bf16[192,1536]{1,0:T(8,128)(2,1)S(1)}, bf16[192,1536]{1,0:T(8,128)(2,1)S(1)}, u32[]{:S(2)}, u32[]{:S(2)}) collective-permute-start(bf16[192,1536]{1,0:T(8,128)(2,1)S(1)} %get-tuple-element.64.here_ref), channel_id=1, source_target_pairs={{0,1},{1,0},{2,3},{3,2},{4,5},{5,4},{6,7},{7,6},{8,9},{9,8},{10,11... | collective-permute-start | bytes 1769480 | tf_op jit(solution)/shard_map/ppermute | solution.py:678
  59.6 6.5 %collective-permute-start.18 = (bf16[2,1536]{1,0:T(2,128)(2,1)S(1)}, bf16[2,1536]{1,0:T(2,128)(2,1)S(1)}, u32[]{:S(2)}, u32[]{:S(2)}) collective-permute-start(bf16[2,1536]{1,0:T(2,128)(2,1)S(1)} %get-tuple-element.69), channel_id=1, source_target_pairs={{0,2},{2,0},{4,6},{6,4},{8,10},{10,8},{12,14},{14,12},{1,3},{3,1},... | collective-permute-start | bytes 18440 | tf_op jit(solution)/shard_map/ppermute | solution.py:683
  61.3 6.4 %collective-permute-start.19 = (bf16[2,1536]{1,0:T(2,128)(2,1)S(1)}, bf16[2,1536]{1,0:T(2,128)(2,1)S(1)}, u32[]{:S(2)}, u32[]{:S(2)}) collective-permute-start(bf16[2,1536]{1,0:T(2,128)(2,1)S(1)} %get-tuple-element.69), channel_id=1, source_target_pairs={{2,4},{6,8},{10,12},{4,2},{8,6},{12,10},{3,5},{7,9},{11,13},{5,3},... | collective-permute-start | bytes 18440 | tf_op jit(solution)/shard_map/ppermute | solution.py:683
